TPU v7x, 512 devices: a whole 4x4x16 slice. The times are simulated.
512 devices in a mesh: rows: 128 (over z, y, core), freq: 4 (over x).
Axes of the slice: x: 4, y: 4, z: 16, core: 2. Of those that a mesh axis runs over, the one named last changes fastest.
Arguments:
- correlation: bfloat16 [2, 128, 4, 512, 1024], P(None, 'rows', None, None, 'freq'), may hold values from -1500 to 1500
- band_tiles: int32 [128, 4], P('rows'), may hold values from 0 to 130, as said below
Outputs:
- coherence: bfloat16 [2, 128, 3, 1024, 512], P(None, 'rows', None, 'freq')
Inputs may be any that keep to these rules, and one draw needn't show every extreme that they name: band_tiles[a, :] lists in increasing order the 4 live tiles with index at or after a; a tile is live for every row or for none; tiles 0 and 127 and all tiles from 128 on are live.
All inputs are finite; a program needn't handle non-finite values.
Results may differ from a plain program's by a relative error of at most 0.001.
Values may be sent and summed in bfloat16 or wider, within the bound.
No kernel may reach another device: no remote copies, remote signals or barrier semaphores. Data moves between devices by JAX's collectives and lax.ppermute only.
A program may use at most 64 MiB of HBM per device.

v0:
```python
import jax
import jax.numpy as jnp
from jax import lax
from jax.sharding import PartitionSpec as P

NE = 3


EPSILON = 1e-06


def from_behind(block, axis, distance):
    devices = range(lax.axis_size(axis))
    route = [(i - distance, i) for i in devices if i - distance in devices]
    return lax.ppermute(block, axis, route)


def swapped_2(value, axis, apart):
    return lax.ppermute(value, axis, [(i, i ^ 1 << apart) for i in range(lax.axis_size(axis))])


def extend(correlation, band_tiles, row_count, reach_rows):
    hop_count = (reach_rows + row_count - 1) // row_count
    tile_pieces = [correlation]
    source_pieces = [band_tiles]
    carried = (correlation, band_tiles)
    for distance in range(1, hop_count + 1):
        need_rows = min(row_count, reach_rows - (distance - 1) * row_count)
        carried = from_behind((carried[0], carried[1]), "rows", -1)
        tile_pieces.append(carried[0])
        source_pieces.append(carried[1])
    return (jnp.concatenate(tile_pieces, axis=1), jnp.concatenate(source_pieces, axis=0))


def row_energy(tile_block):
    return jnp.sum(jnp.square(tile_block.astype(jnp.float32)), axis=(0, 2, 4))


def signed_left(left_tiles):
    swapped = jnp.stack([left_tiles[1], -left_tiles[0]])
    return jnp.stack([left_tiles, swapped])


def aligned_rows(ext_tiles, ext_sources, band_tiles, offset, row_count):
    near_sources = ext_sources[offset : offset + row_count]
    matches = (band_tiles[:, :, None] == near_sources[:, None, :]).astype(jnp.bfloat16)
    near_tiles = ext_tiles[:, offset : offset + row_count]
    return jnp.einsum(
        "tdk,rtkqc->rtdqc", matches, near_tiles, preferred_element_type=jnp.float32
    ).astype(jnp.bfloat16)


def products(left_signed, ext_tiles, ext_sources, band_tiles, row_count):
    blocks = []
    for offset in range(NE):
        aligned = aligned_rows(ext_tiles, ext_sources, band_tiles, offset, row_count)
        blocks.append(
            jnp.einsum(
                "srtdpc,rtdqc->stpq", left_signed, aligned, preferred_element_type=jnp.float32
            )
        )
    return jnp.stack(blocks, axis=2)


def shards(correlation, band_tiles):
    row_count = correlation.shape[1]
    tile_size = correlation.shape[3]
    half_rows = tile_size // 2
    my_half = lax.axis_index("freq") % 2
    ext_tiles, ext_sources = extend(correlation, band_tiles, row_count, NE - 1)
    energy_part = row_energy(ext_tiles)
    partial_value = products(
        signed_left(correlation), ext_tiles, ext_sources, band_tiles, row_count
    )
    kept = lax.dynamic_slice_in_dim(partial_value, my_half * half_rows, half_rows, 3)
    given = lax.dynamic_slice_in_dim(partial_value, (1 - my_half) * half_rows, half_rows, 3)
    received, other_energy = swapped_2((given, energy_part), "freq", 0)
    summed = kept + received
    energy = energy_part + other_energy
    own_energy = lax.dynamic_slice_in_dim(energy[:row_count], my_half * half_rows, half_rows, 1)
    scaled = []
    for offset in range(NE):
        far_energy = energy[offset : offset + row_count]
        denominator = own_energy[:, :, None] * far_energy[:, None, :] + EPSILON
        scaled.append(summed[:, :, offset] * lax.rsqrt(denominator)[None])
    return jnp.stack(scaled, axis=2).astype(jnp.bfloat16)


def solution(mesh):
    return jax.shard_map(
        shards,
        mesh=mesh,
        in_specs=(P(None, "rows", None, None, "freq"), P("rows", None)),
        out_specs=P(None, "rows", None, "freq", None),
        check_vma=False,
    )
```

profile of v0, /device:TPU:25, one launch (start us, length us, event | category | flops | bytes accessed | tf_op | source)
XLA Modules:
  0.0 145.9 jit_solution(4045840484997379424)
XLA Ops:
  0.0 0.0 copy-start.1
  0.0 0.0 copy-start.7
  0.0 3.4 %copy.8 = bf16[2,1,4,512,256]{4,2,3,0,1:T(4,128)(2,1)S(1)} copy(bf16[2,1,4,512,256]{4,3,2,1,0:T(8,128)(2,1)} %param.2) | data formatting | bytes 4194304 | tf_op args[0]
  3.4 0.0 copy-start.3
  3.4 2.6 %collective-permute-start.1 = (bf16[2,1,4,512,256]{4,2,3,0,1:T(4,128)(2,1)S(1)}, bf16[2,1,4,512,256]{4,2,3,0,1:T(4,128)(2,1)S(1)}, u32[]{:S(2)}, u32[]{:S(2)}) collective-permute-start(bf16[2,1,4,512,256]{4,2,3,0,1:T(4,128)(2,1)S(1)} %copy.8), channel_id=1, source_target_pairs={{4,0},{8,4},{12,8},{16,12},{20,16},{24,20},{28,24},{32,28},{36,32}... | collective-permute-start | bytes 6291464 | tf_op jit(solution)/shard_map/ppermute | solution.py:15
  6.0 0.0 copy-done.7
  6.0 2.1 %collective-permute-start = (s32[1,4]{1,0:T(1,128)S(1)}, s32[1,4]{1,0:T(1,128)S(1)}, u32[]{:S(2)}, u32[]{:S(2)}) collective-permute-start(s32[1,4]{1,0:T(1,128)S(1)} %copy-done.7), channel_id=1, source_target_pairs={{4,0},{8,4},{12,8},{16,12},{20,16},{24,20},{28,24},{32,28},{36,32}... | collective-permute-start | bytes 56 | tf_op jit(solution)/shard_map/ppermute | solution.py:15
  8.1 0.0 copy-done.1
  8.1 0.1 copy.43
  8.2 0.0 copy-done.3
  8.3 0.0 copy-start.5
  8.3 24.6 %collective-permute-done.1 = bf16[2,1,4,512,256]{4,2,3,0,1:T(4,128)(2,1)S(1)} collective-permute-done((bf16[2,1,4,512,256]{4,2,3,0,1:T(4,128)(2,1)S(1)}, bf16[2,1,4,512,256]{4,2,3,0,1:T(4,128)(2,1)S(1)}, u32[]{:S(2)}, u32[]{:S(2)}) %collective-permute-start.1) | collective-permute-done | bytes 2097184 | tf_op jit(solution)/shard_map/ppermute | solution.py:15
  32.9 1.9 %collective-permute-start.3 = (bf16[2,1,4,512,256]{4,2,3,0,1:T(4,128)(2,1)S(1)}, bf16[2,1,4,512,256]{4,2,3,0,1:T(4,128)(2,1)}, u32[]{:S(2)}, u32[]{:S(2)}) collective-permute-start(bf16[2,1,4,512,256]{4,2,3,0,1:T(4,128)(2,1)S(1)} %collective-permute-done.1), channel_id=1, source_target_pairs={{4,0},{8,4},{12,8},{16,12},{20,16},{24,20},{28,24},{32,28},{36,32}... | collective-permute-start | bytes 6291464 | tf_op jit(solution)/shard_map/ppermute | solution.py:15
  34.8 0.0 copy-done.5
  34.8 1.1 fusion.48
  35.9 0.0 copy-start.2
  35.9 1.6 %maximum_bitcast_fusion.1 = bf16[1,2,1,4,512,256]{5,4,1,3,0,2:T(8,128)(2,1)S(1)} fusion(bf16[1,1,4,512,256]{4,3,0,2,1:T(8,128)(2,1)} %get-tuple-element.11, bf16[1,1,4,512,256]{4,3,0,2,1:T(8,128)(2,1)S(1)} %get-tuple-element.10), kind=kLoop, calls=%fused_computation.4 | loop fusion | flops 1048576 | bytes 4194304 | tf_op jit(solution)/shard_map/stack | solution.py:41
  37.5 0.3 copy-done.2
  37.8 0.0 copy-start.6
  37.8 1.8 %convert_bitcast_fusion.2 = bf16[2,4,512,256]{3,1,2,0:T(4,128)(2,1)S(1)} fusion(bf16[2,4,512,256]{3,2,1,0:T(8,128)(2,1)S(1)} %bitcast.118, s32[4]{0:T(128)S(1)} %bitcast.126), kind=kOutput, calls=%fused_computation.22 | convolution fusion | flops 9437200 | bytes 4194320 | tf_op jit(solution)/shard_map/tdk,rtkqc->rtdqc/dot_general | solution.py:48
  39.6 0.0 copy-done.6
  39.6 2.4 %fusion.21 = f32[2,1,1,512,512]{3,4,0,2,1:T(8,128)S(1)} fusion(bf16[2,4,512,256]{3,1,2,0:T(4,128)(2,1)S(1)} %convert_bitcast_fusion.2, bf16[1,2,1,4,512,256]{5,4,1,3,0,2:T(8,128)(2,1)S(1)} %maximum_bitcast_fusion.1, bf16[1,2,1,4,512,256]{5,4,1,3,0,2:T(8,128)(2,1)S(1)} %bitcast.119), kind=kOutput, calls=%fused_computation.23 | convolution fusion | flops 2155872256 | bytes 8388608 | tf_op jit(solution)/shard_map/srtdpc,rtdqc->stpq/dot_general | solution.py:58
  41.9 0.0 collective-permute-done
  42.0 2.1 %collective-permute-start.2 = (s32[1,4]{1,0:T(1,128)S(1)}, s32[1,4]{1,0:T(1,128)S(1)}, u32[]{:S(2)}, u32[]{:S(2)}) collective-permute-start(s32[1,4]{1,0:T(1,128)S(1)} %collective-permute-done), channel_id=1, source_target_pairs={{4,0},{8,4},{12,8},{16,12},{20,16},{24,20},{28,24},{32,28},{36,32}... | collective-permute-start | bytes 56 | tf_op jit(solution)/shard_map/ppermute | solution.py:15
  44.1 1.3 convert_bitcast_fusion.1
  45.4 2.4 %fusion.24 = f32[2,1,1,512,512]{3,4,0,2,1:T(8,128)S(1)} fusion(bf16[2,4,512,256]{3,1,2,0:T(4,128)(2,1)S(1)} %convert_bitcast_fusion.1, bf16[1,2,1,4,512,256]{5,4,1,3,0,2:T(8,128)(2,1)S(1)} %maximum_bitcast_fusion.1, bf16[1,2,1,4,512,256]{5,4,1,3,0,2:T(8,128)(2,1)S(1)} %bitcast.120), kind=kOutput, calls=%fused_computation.24 | convolution fusion | flops 2155872256 | bytes 8388608 | tf_op jit(solution)/shard_map/srtdpc,rtdqc->stpq/dot_general | solution.py:58
  47.7 14.7 %collective-permute-done.2 = s32[1,4]{1,0:T(1,128)S(1)} collective-permute-done((s32[1,4]{1,0:T(1,128)S(1)}, s32[1,4]{1,0:T(1,128)S(1)}, u32[]{:S(2)}, u32[]{:S(2)}) %collective-permute-start.2) | collective-permute-done | bytes 48 | tf_op jit(solution)/shard_map/ppermute | solution.py:15
  62.4 0.0 collective-permute-done.3
  62.4 2.9 %convert_bitcast_fusion = bf16[2,4,512,256]{3,1,2,0:T(4,128)(2,1)S(1)} fusion(bf16[2,1,4,512,256]{4,2,3,0,1:T(4,128)(2,1)} %collective-permute-done.3, s32[4]{0:T(128)S(1)} %bitcast.130, s32[4]{0:T(128)S(1)} %bitcast.128), kind=kOutput, calls=%fused_computation.20 | convolution fusion | flops 9437200 | bytes 4194336 | tf_op jit(solution)/shard_map/tdk,rtkqc->rtdqc/dot_general | solution.py:48
  65.3 2.4 %fusion.27 = f32[2,1,1,512,512]{3,4,0,2,1:T(8,128)S(1)} fusion(bf16[2,4,512,256]{3,1,2,0:T(4,128)(2,1)S(1)} %convert_bitcast_fusion, bf16[1,2,1,4,512,256]{5,4,1,3,0,2:T(8,128)(2,1)S(1)} %maximum_bitcast_fusion.1, bf16[1,2,1,4,512,256]{5,4,1,3,0,2:T(8,128)(2,1)S(1)} %bitcast.121), kind=kOutput, calls=%fused_computation.25 | convolution fusion | flops 2155872256 | bytes 8388608 | tf_op jit(solution)/shard_map/srtdpc,rtdqc->stpq/dot_general | solution.py:58
  67.7 1.4 pad_maximum_fusion
  69.1 0.0 copy-start
  69.1 0.0 copy-start.4
  69.1 2.0 %constant_dynamic-slice_fusion.1 = f32[2,1,3,256,512]{3,4,0,2,1:T(8,128)} fusion(f32[2,1,3,512,512]{3,4,0,2,1:T(8,128)S(1)} %pad_maximum_fusion, s32[]{:T(128)S(6)} %select_n.16), kind=kLoop, calls=%fused_computation.50 | loop fusion | bytes 6291460 | tf_op jit(solution)/shard_map/dynamic_slice | solution.py:76
  71.1 1.7 %copy-done = f32[2,1,3,512,512]{3,4,0,2,1:T(8,128)} copy-done((f32[2,1,3,512,512]{3,4,0,2,1:T(8,128)}, f32[2,1,3,512,512]{3,4,0,2,1:T(8,128)S(1)}, u32[]{:S(2)}) %copy-start) | copy-done | bytes 6291480
  72.9 3.1 %collective-permute-start.4 = (f32[2,1,3,256,512]{3,4,0,2,1:T(8,128)}, f32[2,1,3,256,512]{3,4,0,2,1:T(8,128)}, u32[]{:S(2)}, u32[]{:S(2)}) collective-permute-start(f32[2,1,3,256,512]{3,4,0,2,1:T(8,128)} %constant_dynamic-slice_fusion.1), channel_id=1, source_target_pairs={{0,1},{1,0},{2,3},{3,2},{4,5},{5,4},{6,7},{7,6},{8,9},{9,8},{10,11... | collective-permute-start | bytes 9437192 | tf_op jit(solution)/shard_map/ppermute | solution.py:19
  76.0 0.0 copy-done.4
  76.0 24.2 %multiply_reduce_fusion = f32[3,512]{1,0:T(4,128)S(1)} fusion(bf16[2,1,4,512,256]{4,2,3,0,1:T(4,128)(2,1)} %collective-permute-done.3, bf16[2,1,4,512,256]{4,2,3,0,1:T(4,128)(2,1)S(1)} %collective-permute-done.1, bf16[2,1,4,512,256]{4,2,3,0,1:T(4,128)(2,1)S(1)} %copy-done.4), kind=kLoop, calls=%fused_computation | loop fusion | flops 15727104 | bytes 6297600 | tf_op jit(solution)/shard_map/reduce_sum | solution.py:36
  100.1 2.2 %collective-permute-start.5 = (f32[3,512]{1,0:T(4,128)S(1)}, f32[3,512]{1,0:T(4,128)S(1)}, u32[]{:S(2)}, u32[]{:S(2)}) collective-permute-start(f32[3,512]{1,0:T(4,128)S(1)} %multiply_reduce_fusion), channel_id=1, source_target_pairs={{0,1},{1,0},{2,3},{3,2},{4,5},{5,4},{6,7},{7,6},{8,9},{9,8},{10,11... | collective-permute-start | bytes 18440 | tf_op jit(solution)/shard_map/ppermute | solution.py:19
  102.3 37.8 %collective-permute-done.5 = f32[3,512]{1,0:T(4,128)S(1)} collective-permute-done((f32[3,512]{1,0:T(4,128)S(1)}, f32[3,512]{1,0:T(4,128)S(1)}, u32[]{:S(2)}, u32[]{:S(2)}) %collective-permute-start.5) | collective-permute-done | bytes 6176 | tf_op jit(solution)/shard_map/ppermute | solution.py:19
  140.1 0.3 add_rsqrt_fusion.2
  140.4 0.0 collective-permute-done.4
  140.4 3.3 %dynamic-slice_add_fusion = f32[2,1,3,256,512]{3,4,0,2,1:T(8,128)S(1)} fusion(f32[2,1,3,256,512]{3,4,0,2,1:T(8,128)} %collective-permute-done.4, f32[2,1,3,512,512]{3,4,0,2,1:T(8,128)} %copy-done, s32[]{:T(128)S(6)} %select_n.15), kind=kLoop, calls=%fused_computation.3 | loop fusion | flops 786432 | bytes 9437188 | tf_op jit(solution)/shard_map/add | solution.py:78
  143.7 0.4 fusion.32
  144.1 0.2 pad_maximum_fusion.1
  144.3 1.6 %copy.12 = bf16[2,1,3,256,512]{4,3,2,1,0:T(8,128)(2,1)} copy(bf16[2,1,3,256,512]{3,4,0,2,1:T(8,128)(2,1)S(1)} %pad_maximum_fusion.1) | data formatting | bytes 3145728 | tf_op jit(solution)/shard_map/stack | solution.py:86
  (3 shorter events, 0.0 us)
Async XLA Ops:
  0.0 8.1 %copy-start.1 = (bf16[2,1,4,512,256]{4,3,2,1,0:T(8,128)(2,1)S(1)}, bf16[2,1,4,512,256]{4,3,2,1,0:T(8,128)(2,1)}, u32[]{:S(2)}) copy-start(bf16[2,1,4,512,256]{4,3,2,1,0:T(8,128)(2,1)} %param.2) | copy-start | bytes 6291460
  0.0 6.0 %copy-start.7 = (s32[1,4]{1,0:T(1,128)S(1)}, s32[1,4]{1,0:T(1,128)}, u32[]{:S(2)}) copy-start(s32[1,4]{1,0:T(1,128)} %param.3) | copy-start | bytes 52
  3.4 4.9 %copy-start.3 = (bf16[2,1,4,512,256]{4,2,3,0,1:T(4,128)(2,1)}, bf16[2,1,4,512,256]{4,2,3,0,1:T(4,128)(2,1)S(1)}, u32[]{:S(2)}) copy-start(bf16[2,1,4,512,256]{4,2,3,0,1:T(4,128)(2,1)S(1)} %copy.8) | copy-start | bytes 6291460
  3.4 29.5 %collective-permute-start.1 = (bf16[2,1,4,512,256]{4,2,3,0,1:T(4,128)(2,1)S(1)}, bf16[2,1,4,512,256]{4,2,3,0,1:T(4,128)(2,1)S(1)}, u32[]{:S(2)}, u32[]{:S(2)}) collective-permute-start(bf16[2,1,4,512,256]{4,2,3,0,1:T(4,128)(2,1)S(1)} %copy.8), channel_id=1, source_target_pairs={{4,0},{8,4},{12,8},{16,12},{20,16},{24,20},{28,24},{32,28},{36,32}... | collective-permute-start | bytes 6291464 | tf_op jit(solution)/shard_map/ppermute | solution.py:15
  6.0 36.0 %collective-permute-start = (s32[1,4]{1,0:T(1,128)S(1)}, s32[1,4]{1,0:T(1,128)S(1)}, u32[]{:S(2)}, u32[]{:S(2)}) collective-permute-start(s32[1,4]{1,0:T(1,128)S(1)} %copy-done.7), channel_id=1, source_target_pairs={{4,0},{8,4},{12,8},{16,12},{20,16},{24,20},{28,24},{32,28},{36,32}... | collective-permute-start | bytes 56 | tf_op jit(solution)/shard_map/ppermute | solution.py:15
  8.3 26.5 %copy-start.5 = (bf16[2,1,4,512,256]{4,3,0,2,1:T(8,128)(2,1)}, bf16[2,1,4,512,256]{4,3,0,2,1:T(8,128)(2,1)S(1)}, u32[]{:S(2)}) copy-start(bf16[2,1,4,512,256]{4,3,0,2,1:T(8,128)(2,1)S(1)} %copy.43) | copy-start | bytes 6291460
  32.9 29.6 %collective-permute-start.3 = (bf16[2,1,4,512,256]{4,2,3,0,1:T(4,128)(2,1)S(1)}, bf16[2,1,4,512,256]{4,2,3,0,1:T(4,128)(2,1)}, u32[]{:S(2)}, u32[]{:S(2)}) collective-permute-start(bf16[2,1,4,512,256]{4,2,3,0,1:T(4,128)(2,1)S(1)} %collective-permute-done.1), channel_id=1, source_target_pairs={{4,0},{8,4},{12,8},{16,12},{20,16},{24,20},{28,24},{32,28},{36,32}... | collective-permute-start | bytes 6291464 | tf_op jit(solution)/shard_map/ppermute | solution.py:15
  35.9 1.9 %copy-start.2 = (bf16[2,1,4,512,256]{4,3,2,1,0:T(8,128)(2,1)S(1)}, bf16[2,1,4,512,256]{4,3,2,1,0:T(8,128)(2,1)}, u32[]{:S(2)}) copy-start(bf16[2,1,4,512,256]{4,3,2,1,0:T(8,128)(2,1)} %param.2) | copy-start | bytes 6291460
  37.8 1.8 %copy-start.6 = (bf16[2,1,4,512,256]{4,3,0,2,1:T(8,128)(2,1)S(1)}, bf16[2,1,4,512,256]{4,3,0,2,1:T(8,128)(2,1)}, u32[]{:S(2)}) copy-start(bf16[2,1,4,512,256]{4,3,0,2,1:T(8,128)(2,1)} %copy-done.5) | copy-start | bytes 6291460
  42.0 20.5 %collective-permute-start.2 = (s32[1,4]{1,0:T(1,128)S(1)}, s32[1,4]{1,0:T(1,128)S(1)}, u32[]{:S(2)}, u32[]{:S(2)}) collective-permute-start(s32[1,4]{1,0:T(1,128)S(1)} %collective-permute-done), channel_id=1, source_target_pairs={{4,0},{8,4},{12,8},{16,12},{20,16},{24,20},{28,24},{32,28},{36,32}... | collective-permute-start | bytes 56 | tf_op jit(solution)/shard_map/ppermute | solution.py:15
  69.1 3.8 %copy-start = (f32[2,1,3,512,512]{3,4,0,2,1:T(8,128)}, f32[2,1,3,512,512]{3,4,0,2,1:T(8,128)S(1)}, u32[]{:S(2)}) copy-start(f32[2,1,3,512,512]{3,4,0,2,1:T(8,128)S(1)} %pad_maximum_fusion) | copy-start | bytes 18874372
  69.1 6.9 %copy-start.4 = (bf16[2,1,4,512,256]{4,2,3,0,1:T(4,128)(2,1)S(1)}, bf16[2,1,4,512,256]{4,2,3,0,1:T(4,128)(2,1)}, u32[]{:S(2)}) copy-start(bf16[2,1,4,512,256]{4,2,3,0,1:T(4,128)(2,1)} %copy-done.3) | copy-start | bytes 6291460
  72.9 67.6 %collective-permute-start.4 = (f32[2,1,3,256,512]{3,4,0,2,1:T(8,128)}, f32[2,1,3,256,512]{3,4,0,2,1:T(8,128)}, u32[]{:S(2)}, u32[]{:S(2)}) collective-permute-start(f32[2,1,3,256,512]{3,4,0,2,1:T(8,128)} %constant_dynamic-slice_fusion.1), channel_id=1, source_target_pairs={{0,1},{1,0},{2,3},{3,2},{4,5},{5,4},{6,7},{7,6},{8,9},{9,8},{10,11... | collective-permute-start | bytes 9437192 | tf_op jit(solution)/shard_map/ppermute | solution.py:19
  100.1 40.0 %collective-permute-start.5 = (f32[3,512]{1,0:T(4,128)S(1)}, f32[3,512]{1,0:T(4,128)S(1)}, u32[]{:S(2)}, u32[]{:S(2)}) collective-permute-start(f32[3,512]{1,0:T(4,128)S(1)} %multiply_reduce_fusion), channel_id=1, source_target_pairs={{0,1},{1,0},{2,3},{3,2},{4,5},{5,4},{6,7},{7,6},{8,9},{9,8},{10,11... | collective-permute-start | bytes 18440 | tf_op jit(solution)/shard_map/ppermute | solution.py:19
where the time goes:
time: 147 us; the launch traced here: 146 us
  waiting for transfers between devices  77.1 us (52%)
  other arithmetic  32.3 us (22%)
  starting transfers between devices  13.9 us (9%)
  matrix products  13 us (9%)
  local copies, waits for them, and re-layouts  9.25 us (6%)
    ppermute x4, waiting for transfers between devices, from_behind(): return lax.ppermute(block, axis, route)  39.3 us
    ppermute x2, waiting for transfers between devices, swapped_2(): lax.ppermute(value, axis, [(i, i ^ 1 << apart) for i in range(lax.axis_si...  37.8 us
    reduce_sum x1, other arithmetic, row_energy(): return jnp.sum(jnp.square(tile_block.astype(jnp.float32)), axis=(0, 2, 4))  24.2 us
    ppermute x4, starting transfers between devices, from_behind(): return lax.ppermute(block, axis, route)  8.69 us
    dot_general x3, matrix products, products(): jnp.einsum('srtdpc,rtdqc->stpq', left_signed, aligned, preferred_element_...  7.09 us
    dot_general x3, matrix products, aligned_rows(): jnp.einsum('tdk,rtkqc->rtdqc', matches, near_tiles, preferred_element_typ...  5.95 us
    unnamed x18, local copies, waits for them, and re-layouts  5.61 us
    ppermute x2, starting transfers between devices, swapped_2(): lax.ppermute(value, axis, [(i, i ^ 1 << apart) for i in range(lax.axis_si...  5.26 us
  transfers between devices with their start and end apart: 6, of which 3 were waited for; matrix products, arithmetic and copies ran while one was open for 24% of the time, Pallas kernels for 0%

commit v1 on v0

v1 whole, which is shorter than its diff:
```python
import jax
import jax.numpy as jnp
from jax import lax
from jax.experimental import pallas as pl
from jax.experimental.pallas import tpu as pltpu
from jax.sharding import PartitionSpec as P

TS = 512
HALF = 256
BAND = 4
CHUNKS = 2
CR = HALF // CHUNKS
EPSILON = 1e-06
CODE = 2.0**7.5
VMEM = pl.BlockSpec(memory_space=pltpu.VMEM)
ANY = pl.BlockSpec(memory_space=pl.ANY)
SMEM = pl.BlockSpec(memory_space=pltpu.SMEM)
PARAMS = pltpu.CompilerParams(vmem_limit_bytes=40 * 1024 * 1024)


def encode(x):
    u = x * CODE
    y = u * u
    y = y * y
    y = y * y
    y = y * y
    return jnp.where(u < 0, -y, y).astype(jnp.bfloat16)


def decode(y):
    y = y.astype(jnp.float32)
    r = lax.rsqrt(lax.rsqrt(lax.rsqrt(lax.rsqrt(jnp.abs(y))))) * (1.0 / CODE)
    return jnp.where(y < 0, -r, r)


def column(row):
    width = row.shape[1]
    return jnp.transpose(jnp.broadcast_to(row, (128, width)))


def complex_product(left, right_re, right_im):
    dims = (((1,), (1,)), ((), ()))
    with_re = lax.dot_general(left, right_re, dims, preferred_element_type=jnp.float32)
    with_im = lax.dot_general(left, right_im, dims, preferred_element_type=jnp.float32)
    rows = left.shape[0] // 2
    return with_re[:rows] + with_im[rows:], with_re[rows:] - with_im[:rows]


def pack_kernel(own_ref, band_ref, chunk0_ref, chunk1_ref, msg_ref):
    chunks = (chunk0_ref, chunk1_ref)
    msg_ref[...] = jnp.zeros_like(msg_ref)
    for d in range(BAND):
        msg_ref[1 + d : 2 + d, :] = jnp.full((1, TS), band_ref[0, d].astype(jnp.float32))
    for half in range(2):
        for j in range(CHUNKS):
            start = half * HALF + j * CR
            total = jnp.zeros((CR, HALF), jnp.float32)
            for part in range(2):
                for d in range(BAND):
                    block = own_ref[part, d, start : start + CR, :]
                    chunks[j][part, d, half] = block
                    wide = block.astype(jnp.float32)
                    total += wide * wide
            folded = jnp.transpose(total[:, :128] + total[:, 128:])
            msg_ref[0:1, start : start + CR] = jnp.sum(folded, axis=0, keepdims=True)


def self_kernel(pos_ref, own_ref, msg_ref, kept_ref, given_ref, col_ref):
    mine = pos_ref[1]
    row = msg_ref[0:1, :]
    col_ref[...] = column(row)
    right_re = jnp.concatenate([own_ref[0, d] for d in range(BAND)], axis=1)
    right_im = jnp.concatenate([own_ref[1, d] for d in range(BAND)], axis=1)
    for keep in (False, True):
        start = pl.multiple_of((mine if keep else 1 - mine) * HALF, HALF)
        left = jnp.concatenate(
            [
                jnp.concatenate(
                    [own_ref[part, d, pl.ds(start, HALF), :] for d in range(BAND)], axis=1
                )
                for part in range(2)
            ],
            axis=0,
        )
        real, imag = complex_product(left, right_re, right_im)
        scale = lax.rsqrt(col_ref[pl.ds(start, HALF), 0:1] * row + EPSILON)
        if keep:
            kept_ref[0] = real * scale
            kept_ref[1] = imag * scale
        else:
            given_ref[0] = encode(real * scale)
            given_ref[1] = encode(imag * scale)


def pair_kernel(
    j, pos_ref, own_s, near_s, far_s, own_ref, near_ref, far_ref, own_m, near_m, far_m,
    kept_ref, given_ref, col_ref,
):
    core = pos_ref[0]
    mine = pos_ref[1]

    def shift(left_s, right_s):
        first = right_s[1, 0]
        return sum((left_s[1 + d, 0] < first).astype(jnp.int32) for d in range(BAND))

    def aligned(load, part, s):
        blocks = []
        for d in range(BAND):
            block = load(part, jnp.maximum(d - s, 0))
            if d < 2:
                block = jnp.where(d >= s, block, jnp.zeros_like(block))
            blocks.append(block)
        return jnp.concatenate(blocks, axis=1)

    def chunk_of_rows(ref):
        def load(part, k):
            return jnp.concatenate(
                [ref[part, k, h * HALF + j * CR : h * HALF + j * CR + CR, :] for h in range(2)],
                axis=0,
            )
        return load

    def chunk_of_lanes(ref):
        return jnp.concatenate(
            [ref[0:1, h * HALF + j * CR : h * HALF + j * CR + CR] for h in range(2)], axis=1
        )

    def emit(unit, keep, real, imag, scale, split):
        for part, value in enumerate((real, imag)):
            value = value * scale
            for tile in range(2):
                piece = split(value, tile)
                if keep:
                    kept_ref[unit, part, tile] = piece
                else:
                    given_ref[unit, part, tile] = encode(piece)

    @pl.when(core == 0)
    def _():
        col_ref[...] = column(own_m[0:1, :])
        units = (
            (near_s, chunk_of_rows(near_ref), near_m),
            (far_s, lambda part, k: far_ref[part, k].reshape(2 * CR, HALF), far_m),
        )
        for unit, (right_s, load, right_m) in enumerate(units):
            s = shift(own_s, right_s)
            right_re = aligned(load, 0, s)
            right_im = aligned(load, 1, s)
            row = chunk_of_lanes(right_m)
            for keep in (False, True):
                start = pl.multiple_of((mine if keep else 1 - mine) * HALF, HALF)
                left = jnp.concatenate(
                    [
                        jnp.concatenate(
                            [own_ref[part, d, pl.ds(start, HALF), :] for d in range(BAND)], axis=1
                        )
                        for part in range(2)
                    ],
                    axis=0,
                )
                real, imag = complex_product(left, right_re, right_im)
                scale = lax.rsqrt(col_ref[pl.ds(start, HALF), 0:1] * row + EPSILON)
                emit(unit, keep, real, imag, scale, lambda v, t: v[t * CR : t * CR + CR])

    @pl.when(core == 1)
    def _():
        col_ref[...] = column(far_m[0:1, :])
        units = ((near_s, near_ref, near_m), (own_s, own_ref, own_m))
        for unit, (right_s, right_ref, right_m) in enumerate(units):
            s = shift(far_s, right_s)
            load = lambda part, k: right_ref[part, k]
            right_re = aligned(load, 0, s)
            right_im = aligned(load, 1, s)
            row = right_m[0:1, :]
            for keep in (False, True):
                half = mine if keep else 1 - mine
                left = jnp.concatenate(
                    [
                        jnp.concatenate([far_ref[part, d, half] for d in range(BAND)], axis=1)
                        for part in range(2)
                    ],
                    axis=0,
                )
                real, imag = complex_product(left, right_re, right_im)
                start = pl.multiple_of(half * HALF + j * CR, CR)
                scale = lax.rsqrt(col_ref[pl.ds(start, CR), 0:1] * row + EPSILON)
                emit(unit, keep, real, imag, scale, lambda v, t: v[:, t * HALF : t * HALF + HALF])


def self_finish_kernel(kept_ref, got_ref, out_ref, token_ref, fin_ref, sem):
    token_ref[...] = jnp.zeros_like(token_ref)
    for part in range(2):
        fin_ref[part] = (kept_ref[part] + decode(got_ref[part])).astype(jnp.bfloat16)
    copies = [
        pltpu.make_async_copy(fin_ref.at[part], out_ref.at[part, 0, 0], sem.at[part])
        for part in range(2)
    ]
    for copy in copies:
        copy.start()
    for copy in copies:
        copy.wait()


def pair_finish_kernel(kept_ref, got_ref, fin_ref):
    for unit in range(2):
        for part in range(2):
            for tile in range(2):
                value = kept_ref[unit, part, tile] + decode(got_ref[unit, part, tile])
                fin_ref[unit, part, tile] = value.astype(jnp.bfloat16)


def place_kernel(j, pos_ref, out_in_ref, fin_ref, back_ref, out_ref, sem):
    del out_in_ref
    rows = pl.ds(j * CR, CR)
    pieces = [(unit, part, tile) for unit in range(2) for part in range(2) for tile in range(2)]

    def run(copies):
        for copy in copies:
            copy.start()
        for copy in copies:
            copy.wait()

    @pl.when(pos_ref[0] == 0)
    def _():
        run(
            [
                pltpu.make_async_copy(
                    fin_ref.at[unit, part, tile, :, pl.ds(h * CR, CR)],
                    out_ref.at[
                        part, 0, 1 + unit, pl.ds(tile * CR, CR), pl.ds(h * HALF + j * CR, CR)
                    ],
                    sem.at[2 * i + h],
                )
                for i, (unit, part, tile) in enumerate(pieces)
                for h in range(2)
            ]
        )

    @pl.when(pos_ref[0] == 1)
    def _():
        run(
            [
                pltpu.make_async_copy(
                    back_ref.at[unit, part, tile],
                    out_ref.at[part, 0, 1 + unit, rows, pl.ds(tile * HALF, HALF)],
                    sem.at[i],
                )
                for i, (unit, part, tile) in enumerate(pieces)
            ]
        )


def call(kernel, outs, specs, scratch=(), flops=0, after=None, out_specs=None, aliases=None):
    shapes = [jax.ShapeDtypeStruct(shape, dtype) for shape, dtype in outs]
    body = kernel if after is None else lambda _, *refs: kernel(*refs)
    run = pl.pallas_call(
        body,
        out_shape=shapes if len(shapes) > 1 else shapes[0],
        in_specs=specs if after is None else [ANY, *specs],
        out_specs=out_specs or ([VMEM] * len(shapes) if len(shapes) > 1 else VMEM),
        scratch_shapes=list(scratch),
        compiler_params=PARAMS,
        input_output_aliases=aliases or {},
        cost_estimate=pl.CostEstimate(flops=flops, bytes_accessed=2**21, transcendentals=0),
    )
    return run if after is None else lambda *args: run(after, *args)


def shards(correlation, band_tiles):
    bf16, f32 = jnp.bfloat16, jnp.float32
    count = lax.axis_size("rows")
    core = lax.axis_index("rows") % 2
    mine = lax.axis_index("freq") % 2
    pos = jnp.stack([core, mine]).astype(jnp.int32)
    own = correlation.reshape(2, BAND, TS, HALF)
    swap = [(i, i ^ 1) for i in range(lax.axis_size("freq"))]
    pair = [(i, i ^ 1) for i in range(count)]
    far_route = [(i + 2, i) for i in range(0, count - 2, 2)] + [(i - 2, i) for i in range(3, count, 2)]
    back_route = [(i, i - 2) for i in range(3, count, 2)]

    chunk_shape = (2, BAND, 2, CR, HALF)
    chunk0, chunk1, my_energy = call(
        pack_kernel,
        [(chunk_shape, bf16), (chunk_shape, bf16), ((8, TS), f32)],
        [VMEM, SMEM],
    )(own, band_tiles)
    far = [lax.ppermute(chunk, "rows", far_route) for chunk in (chunk0, chunk1)]
    near = lax.ppermute(own, "rows", pair)
    message = my_energy + lax.ppermute(my_energy, "freq", swap)
    near_message = lax.ppermute(message, "rows", pair)
    far_message = lax.ppermute(message, "rows", far_route)
    kept_self, given_self = call(
        self_kernel,
        [((2, HALF, TS), f32), ((2, HALF, TS), bf16)],
        [SMEM, VMEM, VMEM],
        [pltpu.VMEM((TS, 128), f32)],
    )(pos, own, message)
    got_self = lax.ppermute(given_self, "freq", swap)

    unit_shape = (2, 2, 2, CR, HALF)
    after = kept_self
    out, products = None, []
    for j in range(CHUNKS):
        kept, given = call(
            lambda *refs, j=j: pair_kernel(j, *refs),
            [(unit_shape, f32), (unit_shape, bf16)],
            [SMEM] * 4 + [VMEM] * 6,
            [pltpu.VMEM((TS, 128), f32)],
            flops=2**28,
            after=after,
        )(pos, message, near_message, far_message, own, near, far[j], message, near_message, far_message)
        got = lax.ppermute(given, "freq", swap)
        if j == 0:
            out, after = call(
                self_finish_kernel,
                [((2, 1, 3, HALF, TS), bf16), ((8, 128), f32)],
                [VMEM, VMEM],
                [pltpu.VMEM((2, HALF, TS), bf16), pltpu.SemaphoreType.DMA((2,))],
                after=kept,
                out_specs=[ANY, VMEM],
            )(kept_self, got_self)
        products.append((kept, got))
    for j, (kept, got) in enumerate(products):
        fin = call(pair_finish_kernel, [(unit_shape, bf16)], [VMEM, VMEM], after=after)(kept, got)
        after = fin
        back = lax.ppermute(fin, "rows", back_route)
        out = call(
            lambda *refs, j=j: place_kernel(j, *refs),
            [((2, 1, 3, HALF, TS), bf16)],
            [SMEM, ANY, VMEM, VMEM],
            [pltpu.SemaphoreType.DMA((16,))],
            out_specs=ANY,
            aliases={1: 0},
        )(pos, out, fin, back)
    return out


def solution(mesh):
    return jax.shard_map(
        shards,
        mesh=mesh,
        in_specs=(P(None, "rows", None, None, "freq"), P("rows", None)),
        out_specs=P(None, "rows", None, "freq", None),
        check_vma=False,
    )
```

time: 147 us -> 88.2 us (0.60)
  the two profiles are of different devices: /device:TPU:25 before, /device:TPU:379 now
where the time goes in v1:
time: 88.2 us; the launch traced here: 87.7 us
  waiting for transfers between devices  35 us (40%)
  starting transfers between devices  30.7 us (35%)
  Pallas kernels  19.5 us (22%)
  local copies, waits for them, and re-layouts  2.24 us (3%)
    ppermute x2, waiting for transfers between devices, shards(): got = lax.ppermute(given, 'freq', swap)  13 us
    pallas_call x5, Pallas kernels, call(): return run if after is None else lambda *args: run(after, *args)  11.3 us
    ppermute x2, waiting for transfers between devices, shards(): back = lax.ppermute(fin, 'rows', back_route)  9.81 us
    ppermute x1, waiting for transfers between devices, shards(): far_message = lax.ppermute(message, 'rows', far_route)  8.58 us
    ppermute x1, starting transfers between devices, shards(): near_message = lax.ppermute(message, 'rows', pair)  6.08 us
    ppermute x2, starting transfers between devices, shards(): far = [lax.ppermute(chunk, 'rows', far_route) for chunk in (chunk0, chunk1)]  5.5 us
    ppermute x2, starting transfers between devices, shards(): got = lax.ppermute(given, 'freq', swap)  5.31 us
    ppermute x2, starting transfers between devices, shards(): back = lax.ppermute(fin, 'rows', back_route)  3.84 us
  transfers between devices with their start and end apart: 11, of which 7 were waited for; matrix products, arithmetic and copies ran while one was open for 0% of the time, Pallas kernels for 21%

profile of v1, /device:TPU:379, one launch (start us, length us, event | category | flops | bytes accessed | tf_op | source)
XLA Modules:
  0.0 87.7 jit_solution(6743251478453177008)
XLA Ops:
  0.0 2.6 %collective-permute-start.3 = (bf16[2,4,512,256]{3,2,1,0:T(8,128)(2,1)}, bf16[2,4,512,256]{3,2,1,0:T(8,128)(2,1)}, u32[]{:S(2)}, u32[]{:S(2)}) collective-permute-start(bf16[2,4,512,256]{3,2,1,0:T(8,128)(2,1)} %bitcast.3), channel_id=1, source_target_pairs={{0,4},{4,0},{8,12},{12,8},{16,20},{20,16},{24,28},{28,24},{32,36},... | collective-permute-start | bytes 6291464 | tf_op jit(solution)/shard_map/ppermute | solution.py:288
  2.6 0.0 copy-start
  2.6 1.6 %copy-done = bf16[2,1,4,512,256]{4,3,2,1,0:T(8,128)(2,1)S(1)} copy-done((bf16[2,1,4,512,256]{4,3,2,1,0:T(8,128)(2,1)S(1)}, bf16[2,1,4,512,256]{4,3,2,1,0:T(8,128)(2,1)}, u32[]{:S(2)}) %copy-start) | copy-done | bytes 2097176
  4.2 0.0 copy-start.2
  4.2 0.7 copy-done.2
  4.8 0.0 copy-start.1
  4.8 2.2 %shard_map.28 = (bf16[2,4,2,128,256]{4,3,2,1,0:T(8,128)(2,1)}, bf16[2,4,2,128,256]{4,3,2,1,0:T(8,128)(2,1)}, f32[8,512]{1,0:T(8,128)S(1)}) custom-call(bf16[2,4,512,256]{3,2,1,0:T(8,128)(2,1)S(1)} %bitcast.4, s32[1,4]{1,0:T(1,128)S(1)} %copy-done.2), custom_call_target="tpu_custom_call" | custom-call | bytes 2097152 | tf_op jit(solution)/shard_map/pallas_call | solution.py:282
  7.0 2.3 %collective-permute-start.4 = (bf16[2,4,2,128,256]{4,3,2,1,0:T(8,128)(2,1)}, bf16[2,4,2,128,256]{4,3,2,1,0:T(8,128)(2,1)}, u32[]{:S(2)}, u32[]{:S(2)}) collective-permute-start(bf16[2,4,2,128,256]{4,3,2,1,0:T(8,128)(2,1)} %get-tuple-element.18), channel_id=1, source_target_pairs={{8,0},{16,8},{24,16},{32,24},{40,32},{48,40},{56,48},{64,56},{72,6... | collective-permute-start | bytes 3145736 | tf_op jit(solution)/shard_map/ppermute | solution.py:287
  9.3 3.2 %collective-permute-start.8 = (bf16[2,4,2,128,256]{4,3,2,1,0:T(8,128)(2,1)}, bf16[2,4,2,128,256]{4,3,2,1,0:T(8,128)(2,1)S(1)}, u32[]{:S(2)}, u32[]{:S(2)}) collective-permute-start(bf16[2,4,2,128,256]{4,3,2,1,0:T(8,128)(2,1)} %get-tuple-element.24), channel_id=1, source_target_pairs={{8,0},{16,8},{24,16},{32,24},{40,32},{48,40},{56,48},{64,56},{72,6... | collective-permute-start | bytes 3145736 | tf_op jit(solution)/shard_map/ppermute | solution.py:287
  12.5 2.2 %collective-permute-start = (f32[8,512]{1,0:T(8,128)S(1)}, f32[8,512]{1,0:T(8,128)S(1)}, u32[]{:S(2)}, u32[]{:S(2)}) collective-permute-start(f32[8,512]{1,0:T(8,128)S(1)} %get-tuple-element.16), channel_id=1, source_target_pairs={{0,1},{1,0},{2,3},{3,2},{4,5},{5,4},{6,7},{7,6},{8,9},{9,8},{10,11... | collective-permute-start | bytes 49160 | tf_op jit(solution)/shard_map/ppermute | solution.py:289
  14.7 0.1 pad_add_fusion.pos_ref.refs_0_
  14.8 2.8 %collective-permute-done = f32[8,512]{1,0:T(8,128)S(1)} collective-permute-done((f32[8,512]{1,0:T(8,128)S(1)}, f32[8,512]{1,0:T(8,128)S(1)}, u32[]{:S(2)}, u32[]{:S(2)}) %collective-permute-start) | collective-permute-done | bytes 16416 | tf_op jit(solution)/shard_map/ppermute | solution.py:289
  17.5 0.0 copy-done.1
  17.5 3.1 %shard_map.29 = (f32[2,256,512]{2,1,0:T(8,128)S(1)}, bf16[2,256,512]{2,1,0:T(8,128)(2,1)S(1)}) custom-call(s32[2]{0:T(128)S(1)} %pad_add_fusion.pos_ref.refs_0_, bf16[2,4,512,256]{3,2,1,0:T(8,128)(2,1)S(1)} %bitcast.5, f32[8,512]{1,0:T(8,128)S(1)} %add.12.msg_ref.refs_1_.refs_7_), custom_call_target="tpu_custom_call" | custom-call | bytes 2097152 | tf_op jit(solution)/shard_map/pallas_call | solution.py:292
  20.6 2.2 %collective-permute-start.5 = (bf16[2,256,512]{2,1,0:T(8,128)(2,1)S(1)}, bf16[2,256,512]{2,1,0:T(8,128)(2,1)S(1)}, u32[]{:S(2)}, u32[]{:S(2)}) collective-permute-start(bf16[2,256,512]{2,1,0:T(8,128)(2,1)S(1)} %get-tuple-element.20), channel_id=1, source_target_pairs={{0,1},{1,0},{2,3},{3,2},{4,5},{5,4},{6,7},{7,6},{8,9},{9,8},{10,11... | collective-permute-start | bytes 1572872 | tf_op jit(solution)/shard_map/ppermute | solution.py:298
  22.8 3.1 %collective-permute-start.2 = (f32[8,512]{1,0:T(8,128)S(1)}, f32[8,512]{1,0:T(8,128)S(1)}, u32[]{:S(2)}, u32[]{:S(2)}) collective-permute-start(f32[8,512]{1,0:T(8,128)S(1)} %add.12.msg_ref.refs_1_.refs_7_), channel_id=1, source_target_pairs={{8,0},{16,8},{24,16},{32,24},{40,32},{48,40},{56,48},{64,56},{72,6... | collective-permute-start | bytes 49160 | tf_op jit(solution)/shard_map/ppermute | solution.py:291
  25.9 8.6 %collective-permute-done.2.refs_3_.refs_9_ = f32[8,512]{1,0:T(8,128)S(1)} collective-permute-done((f32[8,512]{1,0:T(8,128)S(1)}, f32[8,512]{1,0:T(8,128)S(1)}, u32[]{:S(2)}, u32[]{:S(2)}) %collective-permute-start.2) | collective-permute-done | bytes 16416 | tf_op jit(solution)/shard_map/ppermute | solution.py:291
  34.4 6.1 %collective-permute-start.1 = (f32[8,512]{1,0:T(8,128)S(1)}, f32[8,512]{1,0:T(8,128)S(1)}, u32[]{:S(2)}, u32[]{:S(2)}) collective-permute-start(f32[8,512]{1,0:T(8,128)S(1)} %add.12.msg_ref.refs_1_.refs_7_), channel_id=1, source_target_pairs={{0,4},{4,0},{8,12},{12,8},{16,20},{20,16},{24,28},{28,24},{32,36},... | collective-permute-start | bytes 49160 | tf_op jit(solution)/shard_map/ppermute | solution.py:290
  40.5 0.8 collective-permute-done.1.refs_2_.refs_8_
  41.3 0.0 collective-permute-done.4.refs_6_
  41.3 0.0 collective-permute-done.3.refs_5_
  41.4 4.5 %shard_map.30 = (f32[2,2,2,128,256]{4,3,2,1,0:T(8,128)S(1)}, bf16[2,2,2,128,256]{4,3,2,1,0:T(8,128)(2,1)S(1)}) custom-call(f32[2,256,512]{2,1,0:T(8,128)S(1)} %get-tuple-element.17._.refs_0_, s32[2]{0:T(128)S(1)} %pad_add_fusion.pos_ref.refs_0_, f32[8,512]{1,0:T(8,128)S(1)} %add.12.msg_ref.refs_1_.refs_7_, ...), custom_call_target="tpu_custom_call" | custom-call | flops 268435456 | bytes 2097152 | tf_op jit(solution)/shard_map/pallas_call | solution.py:266
  45.9 2.1 %collective-permute-start.6 = (bf16[2,2,2,128,256]{4,3,2,1,0:T(8,128)(2,1)S(1)}, bf16[2,2,2,128,256]{4,3,2,1,0:T(8,128)(2,1)S(1)}, u32[]{:S(2)}, u32[]{:S(2)}) collective-permute-start(bf16[2,2,2,128,256]{4,3,2,1,0:T(8,128)(2,1)S(1)} %get-tuple-element.23), channel_id=1, source_target_pairs={{0,1},{1,0},{2,3},{3,2},{4,5},{5,4},{6,7},{7,6},{8,9},{9,8},{10,11... | collective-permute-start | bytes 1572872 | tf_op jit(solution)/shard_map/ppermute | solution.py:312
  48.0 0.0 collective-permute-done.5.refs_1_
  48.1 1.4 %shard_map.31 = (bf16[2,1,3,256,512]{4,3,2,1,0:T(8,128)(2,1)}, f32[8,128]{1,0:T(8,128)S(1)}) custom-call(f32[2,2,2,128,256]{4,3,2,1,0:T(8,128)S(1)} %get-tuple-element.19._.refs_0_, f32[2,256,512]{2,1,0:T(8,128)S(1)} %get-tuple-element.17._.refs_0_, bf16[2,256,512]{2,1,0:T(8,128)(2,1)S(1)} %collective-permute-done.5.refs_1_), custom_call_target="tpu_custom_call" | custom-call | bytes 2097152 | tf_op jit(solution)/shard_map/pallas_call | solution.py:266
  49.4 0.0 collective-permute-done.8.refs_6_
  49.4 4.3 %shard_map.34 = (f32[2,2,2,128,256]{4,3,2,1,0:T(8,128)S(1)}, bf16[2,2,2,128,256]{4,3,2,1,0:T(8,128)(2,1)S(1)}) custom-call(f32[8,128]{1,0:T(8,128)S(1)} %get-tuple-element.22._, s32[2]{0:T(128)S(1)} %pad_add_fusion.pos_ref.refs_0_, f32[8,512]{1,0:T(8,128)S(1)} %add.12.msg_ref.refs_1_.refs_7_, f32[8,512]{1,0:T(8,128)S(1)} %collective-permute-done.1.refs_2_.refs_8_, ...), custom_call_target="tpu_custom_call" | custom-call | flops 268435456 | bytes 2097152 | tf_op jit(solution)/shard_map/pallas_call | solution.py:266
  53.7 3.2 %collective-permute-start.9 = (bf16[2,2,2,128,256]{4,3,2,1,0:T(8,128)(2,1)S(1)}, bf16[2,2,2,128,256]{4,3,2,1,0:T(8,128)(2,1)S(1)}, u32[]{:S(2)}, u32[]{:S(2)}) collective-permute-start(bf16[2,2,2,128,256]{4,3,2,1,0:T(8,128)(2,1)S(1)} %get-tuple-element.26), channel_id=1, source_target_pairs={{0,1},{1,0},{2,3},{3,2},{4,5},{5,4},{6,7},{7,6},{8,9},{9,8},{10,11... | collective-permute-start | bytes 1572872 | tf_op jit(solution)/shard_map/ppermute | solution.py:312
  56.9 4.3 %collective-permute-done.6.refs_1_ = bf16[2,2,2,128,256]{4,3,2,1,0:T(8,128)(2,1)S(1)} collective-permute-done((bf16[2,2,2,128,256]{4,3,2,1,0:T(8,128)(2,1)S(1)}, bf16[2,2,2,128,256]{4,3,2,1,0:T(8,128)(2,1)S(1)}, u32[]{:S(2)}, u32[]{:S(2)}) %collective-permute-start.6) | collective-permute-done | bytes 524320 | tf_op jit(solution)/shard_map/ppermute | solution.py:312
  61.2 0.6 shard_map.32.refs_2_._
  61.7 1.9 %collective-permute-start.7 = (bf16[2,2,2,128,256]{4,3,2,1,0:T(8,128)(2,1)S(1)}, bf16[2,2,2,128,256]{4,3,2,1,0:T(8,128)(2,1)S(1)}, u32[]{:S(2)}, u32[]{:S(2)}) collective-permute-start(bf16[2,2,2,128,256]{4,3,2,1,0:T(8,128)(2,1)S(1)} %shard_map.32.refs_2_._), channel_id=1, source_target_pairs={{12,4},{20,12},{28,20},{36,28},{44,36},{52,44},{60,52},{68,60},{76... | collective-permute-start | bytes 1572872 | tf_op jit(solution)/shard_map/ppermute | solution.py:326
  63.7 8.7 %collective-permute-done.9.refs_1_ = bf16[2,2,2,128,256]{4,3,2,1,0:T(8,128)(2,1)S(1)} collective-permute-done((bf16[2,2,2,128,256]{4,3,2,1,0:T(8,128)(2,1)S(1)}, bf16[2,2,2,128,256]{4,3,2,1,0:T(8,128)(2,1)S(1)}, u32[]{:S(2)}, u32[]{:S(2)}) %collective-permute-start.9) | collective-permute-done | bytes 524320 | tf_op jit(solution)/shard_map/ppermute | solution.py:312
  72.4 0.6 shard_map.35.refs_2_
  73.0 1.9 %collective-permute-start.10 = (bf16[2,2,2,128,256]{4,3,2,1,0:T(8,128)(2,1)S(1)}, bf16[2,2,2,128,256]{4,3,2,1,0:T(8,128)(2,1)S(1)}, u32[]{:S(2)}, u32[]{:S(2)}) collective-permute-start(bf16[2,2,2,128,256]{4,3,2,1,0:T(8,128)(2,1)S(1)} %shard_map.35.refs_2_), channel_id=1, source_target_pairs={{12,4},{20,12},{28,20},{36,28},{44,36},{52,44},{60,52},{68,60},{76... | collective-permute-start | bytes 1572872 | tf_op jit(solution)/shard_map/ppermute | solution.py:326
  74.9 0.1 collective-permute-done.7.refs_3_
  75.0 1.5 %shard_map.33.refs_1_ = bf16[2,1,3,256,512]{4,3,2,1,0:T(8,128)(2,1)} custom-call(s32[2]{0:T(128)S(1)} %pad_add_fusion.pos_ref.refs_0_, bf16[2,1,3,256,512]{4,3,2,1,0:T(8,128)(2,1)} %get-tuple-element.21.refs_1_, bf16[2,2,2,128,256]{4,3,2,1,0:T(8,128)(2,1)S(1)} %shard_map.32.refs_2_._, ...), custom_call_target="tpu_custom_call", output_to_operand_aliasing={{}: (1, {})} | custom-call | bytes 2097152 | tf_op jit(solution)/shard_map/pallas_call | solution.py:327
  76.5 9.7 %collective-permute-done.10.refs_3_ = bf16[2,2,2,128,256]{4,3,2,1,0:T(8,128)(2,1)S(1)} collective-permute-done((bf16[2,2,2,128,256]{4,3,2,1,0:T(8,128)(2,1)S(1)}, bf16[2,2,2,128,256]{4,3,2,1,0:T(8,128)(2,1)S(1)}, u32[]{:S(2)}, u32[]{:S(2)}) %collective-permute-start.10) | collective-permute-done | bytes 524320 | tf_op jit(solution)/shard_map/ppermute | solution.py:326
  86.2 1.5 %shard_map.36 = bf16[2,1,3,256,512]{4,3,2,1,0:T(8,128)(2,1)} custom-call(s32[2]{0:T(128)S(1)} %pad_add_fusion.pos_ref.refs_0_, bf16[2,1,3,256,512]{4,3,2,1,0:T(8,128)(2,1)} %shard_map.33.refs_1_, bf16[2,2,2,128,256]{4,3,2,1,0:T(8,128)(2,1)S(1)} %shard_map.35.refs_2_, ...), custom_call_target="tpu_custom_call", output_to_operand_aliasing={{}: (1, {})} | custom-call | bytes 2097152 | tf_op jit(solution)/shard_map/pallas_call | solution.py:327
  (1 shorter events, 0.0 us)
Async XLA Ops:
  0.0 41.4 %collective-permute-start.3 = (bf16[2,4,512,256]{3,2,1,0:T(8,128)(2,1)}, bf16[2,4,512,256]{3,2,1,0:T(8,128)(2,1)}, u32[]{:S(2)}, u32[]{:S(2)}) collective-permute-start(bf16[2,4,512,256]{3,2,1,0:T(8,128)(2,1)} %bitcast.3), channel_id=1, source_target_pairs={{0,4},{4,0},{8,12},{12,8},{16,20},{20,16},{24,28},{28,24},{32,36},... | collective-permute-start | bytes 6291464 | tf_op jit(solution)/shard_map/ppermute | solution.py:288
  2.6 1.6 %copy-start = (bf16[2,1,4,512,256]{4,3,2,1,0:T(8,128)(2,1)S(1)}, bf16[2,1,4,512,256]{4,3,2,1,0:T(8,128)(2,1)}, u32[]{:S(2)}) copy-start(bf16[2,1,4,512,256]{4,3,2,1,0:T(8,128)(2,1)} %param.2) | copy-start | bytes 6291460
  4.2 0.7 copy-start.2
  4.8 12.7 %copy-start.1 = (bf16[2,1,4,512,256]{4,3,2,1,0:T(8,128)(2,1)S(1)}, bf16[2,1,4,512,256]{4,3,2,1,0:T(8,128)(2,1)}, u32[]{:S(2)}) copy-start(bf16[2,1,4,512,256]{4,3,2,1,0:T(8,128)(2,1)} %param.2) | copy-start | bytes 6291460
  7.0 34.4 %collective-permute-start.4 = (bf16[2,4,2,128,256]{4,3,2,1,0:T(8,128)(2,1)}, bf16[2,4,2,128,256]{4,3,2,1,0:T(8,128)(2,1)}, u32[]{:S(2)}, u32[]{:S(2)}) collective-permute-start(bf16[2,4,2,128,256]{4,3,2,1,0:T(8,128)(2,1)} %get-tuple-element.18), channel_id=1, source_target_pairs={{8,0},{16,8},{24,16},{32,24},{40,32},{48,40},{56,48},{64,56},{72,6... | collective-permute-start | bytes 3145736 | tf_op jit(solution)/shard_map/ppermute | solution.py:287
  9.3 40.2 %collective-permute-start.8 = (bf16[2,4,2,128,256]{4,3,2,1,0:T(8,128)(2,1)}, bf16[2,4,2,128,256]{4,3,2,1,0:T(8,128)(2,1)S(1)}, u32[]{:S(2)}, u32[]{:S(2)}) collective-permute-start(bf16[2,4,2,128,256]{4,3,2,1,0:T(8,128)(2,1)} %get-tuple-element.24), channel_id=1, source_target_pairs={{8,0},{16,8},{24,16},{32,24},{40,32},{48,40},{56,48},{64,56},{72,6... | collective-permute-start | bytes 3145736 | tf_op jit(solution)/shard_map/ppermute | solution.py:287
  12.5 5.0 %collective-permute-start = (f32[8,512]{1,0:T(8,128)S(1)}, f32[8,512]{1,0:T(8,128)S(1)}, u32[]{:S(2)}, u32[]{:S(2)}) collective-permute-start(f32[8,512]{1,0:T(8,128)S(1)} %get-tuple-element.16), channel_id=1, source_target_pairs={{0,1},{1,0},{2,3},{3,2},{4,5},{5,4},{6,7},{7,6},{8,9},{9,8},{10,11... | collective-permute-start | bytes 49160 | tf_op jit(solution)/shard_map/ppermute | solution.py:289
  20.6 27.4 %collective-permute-start.5 = (bf16[2,256,512]{2,1,0:T(8,128)(2,1)S(1)}, bf16[2,256,512]{2,1,0:T(8,128)(2,1)S(1)}, u32[]{:S(2)}, u32[]{:S(2)}) collective-permute-start(bf16[2,256,512]{2,1,0:T(8,128)(2,1)S(1)} %get-tuple-element.20), channel_id=1, source_target_pairs={{0,1},{1,0},{2,3},{3,2},{4,5},{5,4},{6,7},{7,6},{8,9},{9,8},{10,11... | collective-permute-start | bytes 1572872 | tf_op jit(solution)/shard_map/ppermute | solution.py:298
  22.8 11.6 %collective-permute-start.2 = (f32[8,512]{1,0:T(8,128)S(1)}, f32[8,512]{1,0:T(8,128)S(1)}, u32[]{:S(2)}, u32[]{:S(2)}) collective-permute-start(f32[8,512]{1,0:T(8,128)S(1)} %add.12.msg_ref.refs_1_.refs_7_), channel_id=1, source_target_pairs={{8,0},{16,8},{24,16},{32,24},{40,32},{48,40},{56,48},{64,56},{72,6... | collective-permute-start | bytes 49160 | tf_op jit(solution)/shard_map/ppermute | solution.py:291
  34.4 6.9 %collective-permute-start.1 = (f32[8,512]{1,0:T(8,128)S(1)}, f32[8,512]{1,0:T(8,128)S(1)}, u32[]{:S(2)}, u32[]{:S(2)}) collective-permute-start(f32[8,512]{1,0:T(8,128)S(1)} %add.12.msg_ref.refs_1_.refs_7_), channel_id=1, source_target_pairs={{0,4},{4,0},{8,12},{12,8},{16,20},{20,16},{24,28},{28,24},{32,36},... | collective-permute-start | bytes 49160 | tf_op jit(solution)/shard_map/ppermute | solution.py:290
  45.9 15.3 %collective-permute-start.6 = (bf16[2,2,2,128,256]{4,3,2,1,0:T(8,128)(2,1)S(1)}, bf16[2,2,2,128,256]{4,3,2,1,0:T(8,128)(2,1)S(1)}, u32[]{:S(2)}, u32[]{:S(2)}) collective-permute-start(bf16[2,2,2,128,256]{4,3,2,1,0:T(8,128)(2,1)S(1)} %get-tuple-element.23), channel_id=1, source_target_pairs={{0,1},{1,0},{2,3},{3,2},{4,5},{5,4},{6,7},{7,6},{8,9},{9,8},{10,11... | collective-permute-start | bytes 1572872 | tf_op jit(solution)/shard_map/ppermute | solution.py:312
  53.7 18.7 %collective-permute-start.9 = (bf16[2,2,2,128,256]{4,3,2,1,0:T(8,128)(2,1)S(1)}, bf16[2,2,2,128,256]{4,3,2,1,0:T(8,128)(2,1)S(1)}, u32[]{:S(2)}, u32[]{:S(2)}) collective-permute-start(bf16[2,2,2,128,256]{4,3,2,1,0:T(8,128)(2,1)S(1)} %get-tuple-element.26), channel_id=1, source_target_pairs={{0,1},{1,0},{2,3},{3,2},{4,5},{5,4},{6,7},{7,6},{8,9},{9,8},{10,11... | collective-permute-start | bytes 1572872 | tf_op jit(solution)/shard_map/ppermute | solution.py:312
  61.7 13.2 %collective-permute-start.7 = (bf16[2,2,2,128,256]{4,3,2,1,0:T(8,128)(2,1)S(1)}, bf16[2,2,2,128,256]{4,3,2,1,0:T(8,128)(2,1)S(1)}, u32[]{:S(2)}, u32[]{:S(2)}) collective-permute-start(bf16[2,2,2,128,256]{4,3,2,1,0:T(8,128)(2,1)S(1)} %shard_map.32.refs_2_._), channel_id=1, source_target_pairs={{12,4},{20,12},{28,20},{36,28},{44,36},{52,44},{60,52},{68,60},{76... | collective-permute-start | bytes 1572872 | tf_op jit(solution)/shard_map/ppermute | solution.py:326
  73.0 13.2 %collective-permute-start.10 = (bf16[2,2,2,128,256]{4,3,2,1,0:T(8,128)(2,1)S(1)}, bf16[2,2,2,128,256]{4,3,2,1,0:T(8,128)(2,1)S(1)}, u32[]{:S(2)}, u32[]{:S(2)}) collective-permute-start(bf16[2,2,2,128,256]{4,3,2,1,0:T(8,128)(2,1)S(1)} %shard_map.35.refs_2_), channel_id=1, source_target_pairs={{12,4},{20,12},{28,20},{36,28},{44,36},{52,44},{60,52},{68,60},{76... | collective-permute-start | bytes 1572872 | tf_op jit(solution)/shard_map/ppermute | solution.py:326

commit v2 on v1

--- a/solution.py
+++ b/solution.py
@@ -11,11 +11,16 @@
 CHUNKS = 2
 CR = HALF // CHUNKS
 EPSILON = 1e-06
+TINY = 1e-30
 CODE = 2.0**7.5
 VMEM = pl.BlockSpec(memory_space=pltpu.VMEM)
 ANY = pl.BlockSpec(memory_space=pl.ANY)
 SMEM = pl.BlockSpec(memory_space=pltpu.SMEM)
-PARAMS = pltpu.CompilerParams(vmem_limit_bytes=40 * 1024 * 1024)
+MIB = 1024 * 1024
+MCOST = 2**33
+PCOST = 0
+TCOST = 0
+FCOST = 2**36
 
 
 def encode(x):
@@ -46,50 +51,75 @@
     return with_re[:rows] + with_im[rows:], with_re[rows:] - with_im[:rows]
 
 
-def pack_kernel(own_ref, band_ref, chunk0_ref, chunk1_ref, msg_ref):
-    chunks = (chunk0_ref, chunk1_ref)
+def chunk_copies(j, own_ref, chunk_ref, sem):
+    return [
+        pltpu.make_async_copy(
+            own_ref.at[:, :, pl.ds(half * HALF + j * CR, CR), :],
+            chunk_ref.at[:, :, half],
+            sem.at[half],
+        )
+        for half in range(2)
+    ]
+
+
+def pack_kernel(own_ref, chunk_ref, token_ref, sem):
+    copies = chunk_copies(0, own_ref, chunk_ref, sem)
+    for copy in copies:
+        copy.start()
+    token_ref[...] = jnp.zeros_like(token_ref)
+    for copy in copies:
+        copy.wait()
+
+
+def order_kernel(_, token_ref):
+    token_ref[...] = jnp.zeros_like(token_ref)
+
+
+def message_kernel(own_ref, mine_ref, other_ref, msg_ref, chunk_ref, sem):
+    copies = chunk_copies(1, own_ref, chunk_ref, sem)
+    for copy in copies:
+        copy.start()
+    msg_ref[...] = mine_ref[...] + other_ref[...]
+    for copy in copies:
+        copy.wait()
+
+
+def self_kernel(pos_ref, band_ref, own_ref, kept_ref, given_ref, msg_ref, product_ref, col_ref):
+    mine = pos_ref[1]
     msg_ref[...] = jnp.zeros_like(msg_ref)
     for d in range(BAND):
         msg_ref[1 + d : 2 + d, :] = jnp.full((1, TS), band_ref[0, d].astype(jnp.float32))
-    for half in range(2):
-        for j in range(CHUNKS):
-            start = half * HALF + j * CR
-            total = jnp.zeros((CR, HALF), jnp.float32)
-            for part in range(2):
-                for d in range(BAND):
-                    block = own_ref[part, d, start : start + CR, :]
-                    chunks[j][part, d, half] = block
-                    wide = block.astype(jnp.float32)
-                    total += wide * wide
-            folded = jnp.transpose(total[:, :128] + total[:, 128:])
-            msg_ref[0:1, start : start + CR] = jnp.sum(folded, axis=0, keepdims=True)
-
-
-def self_kernel(pos_ref, own_ref, msg_ref, kept_ref, given_ref, col_ref):
-    mine = pos_ref[1]
-    row = msg_ref[0:1, :]
-    col_ref[...] = column(row)
     right_re = jnp.concatenate([own_ref[0, d] for d in range(BAND)], axis=1)
     right_im = jnp.concatenate([own_ref[1, d] for d in range(BAND)], axis=1)
-    for keep in (False, True):
-        start = pl.multiple_of((mine if keep else 1 - mine) * HALF, HALF)
+    diagonal = lax.broadcasted_iota(jnp.int32, (HALF, HALF), 0) == lax.broadcasted_iota(
+        jnp.int32, (HALF, HALF), 1
+    )
+    for half in range(2):
+        start = half * HALF
         left = jnp.concatenate(
             [
                 jnp.concatenate(
-                    [own_ref[part, d, pl.ds(start, HALF), :] for d in range(BAND)], axis=1
+                    [own_ref[part, d, start : start + HALF, :] for d in range(BAND)], axis=1
                 )
                 for part in range(2)
             ],
             axis=0,
         )
         real, imag = complex_product(left, right_re, right_im)
-        scale = lax.rsqrt(col_ref[pl.ds(start, HALF), 0:1] * row + EPSILON)
-        if keep:
-            kept_ref[0] = real * scale
-            kept_ref[1] = imag * scale
-        else:
-            given_ref[0] = encode(real * scale)
-            given_ref[1] = encode(imag * scale)
+        product_ref[half, 0] = real
+        product_ref[half, 1] = imag
+        energies = jnp.where(diagonal, real[:, start : start + HALF], 0.0)
+        msg_ref[0:1, start : start + HALF] = jnp.sum(energies, axis=0, keepdims=True)
+        col_ref[start : start + HALF, :] = jnp.broadcast_to(
+            jnp.sum(energies, axis=1, keepdims=True), (HALF, 128)
+        )
+    other = pl.multiple_of((1 - mine) * HALF, HALF)
+    scale = lax.rsqrt(jnp.maximum(col_ref[pl.ds(other, HALF), 0:1], TINY)) * lax.rsqrt(
+        jnp.maximum(msg_ref[0:1, :], TINY)
+    )
+    for part in range(2):
+        given_ref[part] = encode(product_ref[1 - mine, part] * scale)
+        kept_ref[part] = product_ref[mine, part]
 
 
 def pair_kernel(
@@ -187,10 +217,20 @@
                 emit(unit, keep, real, imag, scale, lambda v, t: v[:, t * HALF : t * HALF + HALF])
 
 
-def self_finish_kernel(kept_ref, got_ref, out_ref, token_ref, fin_ref, sem):
+def self_finish_kernel(
+    pos_ref, kept_ref, got_ref, mine_ref, other_ref, out_ref, token_ref, fin_ref, col_ref, sem
+):
     token_ref[...] = jnp.zeros_like(token_ref)
+    start = pl.multiple_of(pos_ref[1] * HALF, HALF)
+    other = jnp.sqrt(jnp.maximum(other_ref[0:1, :], TINY))
+    total = mine_ref[0:1, :] + other_ref[0:1, :]
+    col_ref[0] = column(other)
+    col_ref[1] = column(total)
+    scale = lax.rsqrt(col_ref[1, pl.ds(start, HALF), 0:1] * total + EPSILON)
+    back = col_ref[0, pl.ds(start, HALF), 0:1] * other
     for part in range(2):
-        fin_ref[part] = (kept_ref[part] + decode(got_ref[part])).astype(jnp.bfloat16)
+        value = (kept_ref[part] + decode(got_ref[part]) * back) * scale
+        fin_ref[part] = value.astype(jnp.bfloat16)
     copies = [
         pltpu.make_async_copy(fin_ref.at[part], out_ref.at[part, 0, 0], sem.at[part])
         for part in range(2)
@@ -250,16 +290,17 @@
         )
 
 
-def call(kernel, outs, specs, scratch=(), flops=0, after=None, out_specs=None, aliases=None):
+def call(name, kernel, outs, specs, scratch=(), flops=0, after=None, out_specs=None, aliases=None, vmem=40):
     shapes = [jax.ShapeDtypeStruct(shape, dtype) for shape, dtype in outs]
     body = kernel if after is None else lambda _, *refs: kernel(*refs)
     run = pl.pallas_call(
         body,
+        name=name,
         out_shape=shapes if len(shapes) > 1 else shapes[0],
         in_specs=specs if after is None else [ANY, *specs],
         out_specs=out_specs or ([VMEM] * len(shapes) if len(shapes) > 1 else VMEM),
         scratch_shapes=list(scratch),
-        compiler_params=PARAMS,
+        compiler_params=pltpu.CompilerParams(vmem_limit_bytes=vmem * MIB),
         input_output_aliases=aliases or {},
         cost_estimate=pl.CostEstimate(flops=flops, bytes_accessed=2**21, transcendentals=0),
     )
@@ -276,55 +317,82 @@
     swap = [(i, i ^ 1) for i in range(lax.axis_size("freq"))]
     pair = [(i, i ^ 1) for i in range(count)]
     far_route = [(i + 2, i) for i in range(0, count - 2, 2)] + [(i - 2, i) for i in range(3, count, 2)]
+    across_route = [(i + 3, i) for i in range(0, count - 2, 2)] + [(i - 3, i) for i in range(3, count, 2)]
     back_route = [(i, i - 2) for i in range(3, count, 2)]
 
     chunk_shape = (2, BAND, 2, CR, HALF)
-    chunk0, chunk1, my_energy = call(
+    half_shape = (2, HALF, TS)
+    token = ((8, 128), f32)
+    chunk0, after = call(
+        "pack",
         pack_kernel,
-        [(chunk_shape, bf16), (chunk_shape, bf16), ((8, TS), f32)],
-        [VMEM, SMEM],
-    )(own, band_tiles)
-    far = [lax.ppermute(chunk, "rows", far_route) for chunk in (chunk0, chunk1)]
+        [(chunk_shape, bf16), token],
+        [ANY],
+        [pltpu.SemaphoreType.DMA((2,))],
+        out_specs=[ANY, VMEM],
+        vmem=52,
+    )(own)
+    far0 = lax.ppermute(chunk0, "rows", far_route)
+    kept_self, given_self, my_energy = call(
+        "self",
+        self_kernel,
+        [(half_shape, f32), (half_shape, bf16), ((8, TS), f32)],
+        [SMEM, SMEM, VMEM],
+        [pltpu.VMEM((2, 2, HALF, TS), f32), pltpu.VMEM((TS, 128), f32)],
+        after=after,
+    )(pos, band_tiles, own)
+    other_energy = lax.ppermute(my_energy, "freq", swap)
+    got_self = lax.ppermute(given_self, "freq", swap)
+    message, chunk1 = call(
+        "message",
+        message_kernel,
+        [((8, TS), f32), (chunk_shape, bf16)],
+        [VMEM] * 3,
+        [pltpu.SemaphoreType.DMA((2,))],
+        flops=MCOST,
+    )(own, my_energy, other_energy)
+    far1 = lax.ppermute(chunk1, "rows", far_route)
     near = lax.ppermute(own, "rows", pair)
-    message = my_energy + lax.ppermute(my_energy, "freq", swap)
+    far = (far0, far1)
     near_message = lax.ppermute(message, "rows", pair)
-    far_message = lax.ppermute(message, "rows", far_route)
-    kept_self, given_self = call(
-        self_kernel,
-        [((2, HALF, TS), f32), ((2, HALF, TS), bf16)],
-        [SMEM, VMEM, VMEM],
-        [pltpu.VMEM((TS, 128), f32)],
-    )(pos, own, message)
-    got_self = lax.ppermute(given_self, "freq", swap)
+    far_message = lax.ppermute(near_message, "rows", across_route)
 
     unit_shape = (2, 2, 2, CR, HALF)
-    after = kept_self
+    after = call("order", order_kernel, [token], [ANY], flops=TCOST)(far0)
     out, products = None, []
     for j in range(CHUNKS):
         kept, given = call(
+            f"pair{j}",
             lambda *refs, j=j: pair_kernel(j, *refs),
             [(unit_shape, f32), (unit_shape, bf16)],
             [SMEM] * 4 + [VMEM] * 6,
             [pltpu.VMEM((TS, 128), f32)],
-            flops=2**28,
+            flops=PCOST,
             after=after,
         )(pos, message, near_message, far_message, own, near, far[j], message, near_message, far_message)
         got = lax.ppermute(given, "freq", swap)
         if j == 0:
             out, after = call(
+                "finish",
                 self_finish_kernel,
-                [((2, 1, 3, HALF, TS), bf16), ((8, 128), f32)],
-                [VMEM, VMEM],
-                [pltpu.VMEM((2, HALF, TS), bf16), pltpu.SemaphoreType.DMA((2,))],
+                [((2, 1, 3, HALF, TS), bf16), token],
+                [SMEM] + [VMEM] * 4,
+                [
+                    pltpu.VMEM((2, HALF, TS), bf16),
+                    pltpu.VMEM((2, TS, 128), f32),
+                    pltpu.SemaphoreType.DMA((2,)),
+                ],
+                flops=FCOST,
                 after=kept,
                 out_specs=[ANY, VMEM],
-            )(kept_self, got_self)
+            )(pos, kept_self, got_self, my_energy, other_energy)
         products.append((kept, got))
     for j, (kept, got) in enumerate(products):
-        fin = call(pair_finish_kernel, [(unit_shape, bf16)], [VMEM, VMEM], after=after)(kept, got)
+        fin = call("decode", pair_finish_kernel, [(unit_shape, bf16)], [VMEM, VMEM], after=after)(kept, got)
         after = fin
         back = lax.ppermute(fin, "rows", back_route)
         out = call(
+            f"place{j}",
             lambda *refs, j=j: place_kernel(j, *refs),
             [((2, 1, 3, HALF, TS), bf16)],
             [SMEM, ANY, VMEM, VMEM],

time: 88.2 us -> 108 us (1.22)
  the two profiles are of different devices: /device:TPU:379 before, /device:TPU:391 now
where the time goes in v2:
time: 108 us
  Pallas kernels  51.4 us (48%)
  starting transfers between devices  32.3 us (30%)
  waiting for transfers between devices  23.8 us (22%)
    pallas_call x1, Pallas kernels, shards(): call('pack', pack_kernel, [(chunk_shape, bf16), token], [ANY], [pltpu.Sem...  32.9 us
    pallas_call x6, Pallas kernels, call(): return run if after is None else lambda *args: run(after, *args)  15.4 us
    ppermute x2, waiting for transfers between devices, shards(): got = lax.ppermute(given, 'freq', swap)  9.55 us
    ppermute x2, waiting for transfers between devices, shards(): back = lax.ppermute(fin, 'rows', back_route)  6.48 us
    ppermute x1, starting transfers between devices, shards(): near_message = lax.ppermute(message, 'rows', pair)  5.85 us
    ppermute x2, starting transfers between devices, shards(): back = lax.ppermute(fin, 'rows', back_route)  4.9 us
    ppermute x2, starting transfers between devices, shards(): got = lax.ppermute(given, 'freq', swap)  4.9 us
    ppermute x1, waiting for transfers between devices, shards(): far1 = lax.ppermute(chunk1, 'rows', far_route)  4.12 us
  transfers between devices with their start and end apart: 11, of which 5 were waited for; matrix products, arithmetic and copies ran while one was open for 0% of the time, Pallas kernels for 46%

profile of v2, /device:TPU:391, one launch (start us, length us, event | category | flops | bytes accessed | tf_op | source)
XLA Modules:
  0.0 107.8 jit_solution(10828287304218148071)
XLA Ops:
  0.0 0.0 copy-start
  0.0 0.0 copy-start.1
  0.0 2.7 %collective-permute-start.4 = (bf16[2,4,512,256]{3,2,1,0:T(8,128)(2,1)}, bf16[2,4,512,256]{3,2,1,0:T(8,128)(2,1)}, u32[]{:S(2)}, u32[]{:S(2)}) collective-permute-start(bf16[2,4,512,256]{3,2,1,0:T(8,128)(2,1)} %bitcast.3), channel_id=1, source_target_pairs={{0,4},{4,0},{8,12},{12,8},{16,20},{20,16},{24,28},{28,24},{32,36},... | collective-permute-start | bytes 6291464 | tf_op jit(solution)/shard_map/ppermute | solution.py:355
  2.7 32.9 %pack.1 = (bf16[2,4,2,128,256]{4,3,2,1,0:T(8,128)(2,1)}, f32[8,128]{1,0:T(8,128)S(1)}) custom-call(bf16[2,4,512,256]{3,2,1,0:T(8,128)(2,1)} %bitcast.4), custom_call_target="tpu_custom_call" | custom-call | bytes 2097152 | tf_op jit(solution)/shard_map/pack/pallas_call | solution.py:326
  35.6 3.2 %collective-permute-start = (bf16[2,4,2,128,256]{4,3,2,1,0:T(8,128)(2,1)}, bf16[2,4,2,128,256]{4,3,2,1,0:T(8,128)(2,1)S(1)}, u32[]{:S(2)}, u32[]{:S(2)}) collective-permute-start(bf16[2,4,2,128,256]{4,3,2,1,0:T(8,128)(2,1)} %get-tuple-element.18), channel_id=1, source_target_pairs={{8,0},{16,8},{24,16},{32,24},{40,32},{48,40},{56,48},{64,56},{72,6... | collective-permute-start | bytes 3145736 | tf_op jit(solution)/shard_map/ppermute | solution.py:335
  38.8 0.1 pad_add_fusion.refs_0_
  38.9 0.0 copy-done
  38.9 0.0 copy-done.1
  38.9 3.4 %self.1 = (f32[2,256,512]{2,1,0:T(8,128)S(1)}, bf16[2,256,512]{2,1,0:T(8,128)(2,1)S(1)}, f32[8,512]{1,0:T(8,128)S(1)}) custom-call(f32[8,128]{1,0:T(8,128)S(1)} %get-tuple-element.19._, s32[2]{0:T(128)S(1)} %pad_add_fusion.refs_0_, s32[1,4]{1,0:T(1,128)S(1)} %copy-done.1, bf16[2,4,512,256]{3,2,1,0:T(8,128)(2,1)S(1)} %bitcast.5), custom_call_target="tpu_custom_call" | custom-call | bytes 2097152 | tf_op jit(solution)/shard_map/self/pallas_call | solution.py:307
  42.4 2.4 %collective-permute-start.1 = (f32[8,512]{1,0:T(8,128)S(1)}, f32[8,512]{1,0:T(8,128)S(1)}, u32[]{:S(2)}, u32[]{:S(2)}) collective-permute-start(f32[8,512]{1,0:T(8,128)S(1)} %get-tuple-element.20.mine_ref.refs_3_), channel_id=1, source_target_pairs={{0,1},{1,0},{2,3},{3,2},{4,5},{5,4},{6,7},{7,6},{8,9},{9,8},{10,11... | collective-permute-start | bytes 49160 | tf_op jit(solution)/shard_map/ppermute | solution.py:344
  44.8 2.8 %collective-permute-start.5 = (bf16[2,256,512]{2,1,0:T(8,128)(2,1)S(1)}, bf16[2,256,512]{2,1,0:T(8,128)(2,1)S(1)}, u32[]{:S(2)}, u32[]{:S(2)}) collective-permute-start(bf16[2,256,512]{2,1,0:T(8,128)(2,1)S(1)} %get-tuple-element.24), channel_id=1, source_target_pairs={{0,1},{1,0},{2,3},{3,2},{4,5},{5,4},{6,7},{7,6},{8,9},{9,8},{10,11... | collective-permute-start | bytes 1572872 | tf_op jit(solution)/shard_map/ppermute | solution.py:345
  47.7 0.0 collective-permute-done.1.other_ref.refs_4_
  47.7 0.1 message.1
  47.8 5.9 %collective-permute-start.2 = (f32[8,512]{1,0:T(8,128)S(1)}, f32[8,512]{1,0:T(8,128)S(1)}, u32[]{:S(2)}, u32[]{:S(2)}) collective-permute-start(f32[8,512]{1,0:T(8,128)S(1)} %get-tuple-element.21.refs_1_.refs_7_), channel_id=1, source_target_pairs={{0,4},{4,0},{8,12},{12,8},{16,20},{20,16},{24,28},{28,24},{32,36},... | collective-permute-start | bytes 49160 | tf_op jit(solution)/shard_map/ppermute | solution.py:357
  53.6 0.8 collective-permute-done.2.refs_2_.refs_8_
  54.5 2.6 %collective-permute-start.3 = (f32[8,512]{1,0:T(8,128)S(1)}, f32[8,512]{1,0:T(8,128)S(1)}, u32[]{:S(2)}, u32[]{:S(2)}) collective-permute-start(f32[8,512]{1,0:T(8,128)S(1)} %collective-permute-done.2.refs_2_.refs_8_), channel_id=1, source_target_pairs={{12,0},{20,8},{28,16},{36,24},{44,32},{52,40},{60,48},{68,56},{76,... | collective-permute-start | bytes 49160 | tf_op jit(solution)/shard_map/ppermute | solution.py:358
  57.1 2.9 %collective-permute-start.8 = (bf16[2,4,2,128,256]{4,3,2,1,0:T(8,128)(2,1)S(1)}, bf16[2,4,2,128,256]{4,3,2,1,0:T(8,128)(2,1)S(1)}, u32[]{:S(2)}, u32[]{:S(2)}) collective-permute-start(bf16[2,4,2,128,256]{4,3,2,1,0:T(8,128)(2,1)S(1)} %get-tuple-element.28), channel_id=1, source_target_pairs={{8,0},{16,8},{24,16},{32,24},{40,32},{48,40},{56,48},{64,56},{72,6... | collective-permute-start | bytes 3145736 | tf_op jit(solution)/shard_map/ppermute | solution.py:354
  60.0 0.0 collective-permute-done._.refs_6_
  60.0 2.8 %collective-permute-done.3.refs_3_.refs_9_ = f32[8,512]{1,0:T(8,128)S(1)} collective-permute-done((f32[8,512]{1,0:T(8,128)S(1)}, f32[8,512]{1,0:T(8,128)S(1)}, u32[]{:S(2)}, u32[]{:S(2)}) %collective-permute-start.3) | collective-permute-done | bytes 16416 | tf_op jit(solution)/shard_map/ppermute | solution.py:358
  62.8 0.0 collective-permute-done.4.refs_5_
  62.8 4.3 %pair0.1 = (f32[2,2,2,128,256]{4,3,2,1,0:T(8,128)S(1)}, bf16[2,2,2,128,256]{4,3,2,1,0:T(8,128)(2,1)S(1)}) custom-call(f32[8,128]{1,0:T(8,128)S(1)} %order.1._, s32[2]{0:T(128)S(1)} %pad_add_fusion.refs_0_, f32[8,512]{1,0:T(8,128)S(1)} %get-tuple-element.21.refs_1_.refs_7_, f32[8,512]{1,0:T(8,128)S(1)} %collective-permute-done.2.refs_2_.refs_8_, ...), custom_call_target="tpu_custom_call" | custom-call | bytes 2097152 | tf_op jit(solution)/shard_map/pair0/pallas_call | solution.py:307
  67.1 2.4 %collective-permute-start.6 = (bf16[2,2,2,128,256]{4,3,2,1,0:T(8,128)(2,1)S(1)}, bf16[2,2,2,128,256]{4,3,2,1,0:T(8,128)(2,1)S(1)}, u32[]{:S(2)}, u32[]{:S(2)}) collective-permute-start(bf16[2,2,2,128,256]{4,3,2,1,0:T(8,128)(2,1)S(1)} %get-tuple-element.27), channel_id=1, source_target_pairs={{0,1},{1,0},{2,3},{3,2},{4,5},{5,4},{6,7},{7,6},{8,9},{9,8},{10,11... | collective-permute-start | bytes 1572872 | tf_op jit(solution)/shard_map/ppermute | solution.py:373
  69.5 0.0 collective-permute-done.5.refs_2_
  69.5 2.2 %finish.1 = (bf16[2,1,3,256,512]{4,3,2,1,0:T(8,128)(2,1)}, f32[8,128]{1,0:T(8,128)S(1)}) custom-call(f32[2,2,2,128,256]{4,3,2,1,0:T(8,128)S(1)} %get-tuple-element.22._.refs_0_, s32[2]{0:T(128)S(1)} %pad_add_fusion.refs_0_, f32[2,256,512]{2,1,0:T(8,128)S(1)} %get-tuple-element.23.refs_1_, bf16[2,256,512]{2,1,0:T(8,128)(2,1)S(1)} %collective-permute-done.5.refs_2_, ...), custom_call_target="tpu_custom_call" | custom-call | flops 68719476736 | bytes 2097152 | tf_op jit(solution)/shard_map/finish/pallas_call | solution.py:307
  71.8 4.1 %collective-permute-done.8.refs_6_ = bf16[2,4,2,128,256]{4,3,2,1,0:T(8,128)(2,1)S(1)} collective-permute-done((bf16[2,4,2,128,256]{4,3,2,1,0:T(8,128)(2,1)S(1)}, bf16[2,4,2,128,256]{4,3,2,1,0:T(8,128)(2,1)S(1)}, u32[]{:S(2)}, u32[]{:S(2)}) %collective-permute-start.8) | collective-permute-done | bytes 1048608 | tf_op jit(solution)/shard_map/ppermute | solution.py:354
  75.9 4.3 %pair1.1 = (f32[2,2,2,128,256]{4,3,2,1,0:T(8,128)S(1)}, bf16[2,2,2,128,256]{4,3,2,1,0:T(8,128)(2,1)S(1)}) custom-call(f32[8,128]{1,0:T(8,128)S(1)} %get-tuple-element.26._, s32[2]{0:T(128)S(1)} %pad_add_fusion.refs_0_, f32[8,512]{1,0:T(8,128)S(1)} %get-tuple-element.21.refs_1_.refs_7_, f32[8,512]{1,0:T(8,128)S(1)} %collective-permute-done.2.refs_2_.refs_8_, ...), custom_call_target="tpu_custom_call" | custom-call | bytes 2097152 | tf_op jit(solution)/shard_map/pair1/pallas_call | solution.py:307
  80.2 2.5 %collective-permute-start.9 = (bf16[2,2,2,128,256]{4,3,2,1,0:T(8,128)(2,1)S(1)}, bf16[2,2,2,128,256]{4,3,2,1,0:T(8,128)(2,1)S(1)}, u32[]{:S(2)}, u32[]{:S(2)}) collective-permute-start(bf16[2,2,2,128,256]{4,3,2,1,0:T(8,128)(2,1)S(1)} %get-tuple-element.30), channel_id=1, source_target_pairs={{0,1},{1,0},{2,3},{3,2},{4,5},{5,4},{6,7},{7,6},{8,9},{9,8},{10,11... | collective-permute-start | bytes 1572872 | tf_op jit(solution)/shard_map/ppermute | solution.py:373
  82.7 0.0 collective-permute-done.6.refs_1_
  82.7 0.6 decode.2.refs_2_._
  83.3 3.0 %collective-permute-start.7 = (bf16[2,2,2,128,256]{4,3,2,1,0:T(8,128)(2,1)S(1)}, bf16[2,2,2,128,256]{4,3,2,1,0:T(8,128)(2,1)S(1)}, u32[]{:S(2)}, u32[]{:S(2)}) collective-permute-start(bf16[2,2,2,128,256]{4,3,2,1,0:T(8,128)(2,1)S(1)} %decode.2.refs_2_._), channel_id=1, source_target_pairs={{12,4},{20,12},{28,20},{36,28},{44,36},{52,44},{60,52},{68,60},{76... | collective-permute-start | bytes 1572872 | tf_op jit(solution)/shard_map/ppermute | solution.py:393
  86.3 9.5 %collective-permute-done.9.refs_1_ = bf16[2,2,2,128,256]{4,3,2,1,0:T(8,128)(2,1)S(1)} collective-permute-done((bf16[2,2,2,128,256]{4,3,2,1,0:T(8,128)(2,1)S(1)}, bf16[2,2,2,128,256]{4,3,2,1,0:T(8,128)(2,1)S(1)}, u32[]{:S(2)}, u32[]{:S(2)}) %collective-permute-start.9) | collective-permute-done | bytes 524320 | tf_op jit(solution)/shard_map/ppermute | solution.py:373
  95.8 0.6 decode.3.refs_2_
  96.4 1.9 %collective-permute-start.10 = (bf16[2,2,2,128,256]{4,3,2,1,0:T(8,128)(2,1)S(1)}, bf16[2,2,2,128,256]{4,3,2,1,0:T(8,128)(2,1)S(1)}, u32[]{:S(2)}, u32[]{:S(2)}) collective-permute-start(bf16[2,2,2,128,256]{4,3,2,1,0:T(8,128)(2,1)S(1)} %decode.3.refs_2_), channel_id=1, source_target_pairs={{12,4},{20,12},{28,20},{36,28},{44,36},{52,44},{60,52},{68,60},{76... | collective-permute-start | bytes 1572872 | tf_op jit(solution)/shard_map/ppermute | solution.py:393
  98.3 0.0 collective-permute-done.7.refs_3_
  98.3 1.5 %place0.1.refs_1_ = bf16[2,1,3,256,512]{4,3,2,1,0:T(8,128)(2,1)} custom-call(s32[2]{0:T(128)S(1)} %pad_add_fusion.refs_0_, bf16[2,1,3,256,512]{4,3,2,1,0:T(8,128)(2,1)} %get-tuple-element.25.refs_1_, bf16[2,2,2,128,256]{4,3,2,1,0:T(8,128)(2,1)S(1)} %decode.2.refs_2_._, ...), custom_call_target="tpu_custom_call", output_to_operand_aliasing={{}: (1, {})} | custom-call | bytes 2097152 | tf_op jit(solution)/shard_map/place0/pallas_call | solution.py:394
  99.8 6.5 %collective-permute-done.10.refs_3_ = bf16[2,2,2,128,256]{4,3,2,1,0:T(8,128)(2,1)S(1)} collective-permute-done((bf16[2,2,2,128,256]{4,3,2,1,0:T(8,128)(2,1)S(1)}, bf16[2,2,2,128,256]{4,3,2,1,0:T(8,128)(2,1)S(1)}, u32[]{:S(2)}, u32[]{:S(2)}) %collective-permute-start.10) | collective-permute-done | bytes 524320 | tf_op jit(solution)/shard_map/ppermute | solution.py:393
  106.3 1.5 %place1.1 = bf16[2,1,3,256,512]{4,3,2,1,0:T(8,128)(2,1)} custom-call(s32[2]{0:T(128)S(1)} %pad_add_fusion.refs_0_, bf16[2,1,3,256,512]{4,3,2,1,0:T(8,128)(2,1)} %place0.1.refs_1_, bf16[2,2,2,128,256]{4,3,2,1,0:T(8,128)(2,1)S(1)} %decode.3.refs_2_, bf16[2,2,2,128,256]{4,3,2,1,0:T(8,128)(2,1)S(1)} %collective-permute-done.10.refs_3_), custom_call_target="tpu_custom_call", output_to_operand_aliasing={{}: (1, {})} | custom-call | bytes 2097152 | tf_op jit(solution)/shard_map/place1/pallas_call | solution.py:394
  (1 shorter events, 0.0 us)
Async XLA Ops:
  0.0 38.9 %copy-start = (bf16[2,1,4,512,256]{4,3,2,1,0:T(8,128)(2,1)S(1)}, bf16[2,1,4,512,256]{4,3,2,1,0:T(8,128)(2,1)}, u32[]{:S(2)}) copy-start(bf16[2,1,4,512,256]{4,3,2,1,0:T(8,128)(2,1)} %param.2) | copy-start | bytes 6291460
  0.0 38.9 %copy-start.1 = (s32[1,4]{1,0:T(1,128)S(1)}, s32[1,4]{1,0:T(1,128)}, u32[]{:S(2)}) copy-start(s32[1,4]{1,0:T(1,128)} %refs_1_.1) | copy-start | bytes 52
  0.0 62.8 %collective-permute-start.4 = (bf16[2,4,512,256]{3,2,1,0:T(8,128)(2,1)}, bf16[2,4,512,256]{3,2,1,0:T(8,128)(2,1)}, u32[]{:S(2)}, u32[]{:S(2)}) collective-permute-start(bf16[2,4,512,256]{3,2,1,0:T(8,128)(2,1)} %bitcast.3), channel_id=1, source_target_pairs={{0,4},{4,0},{8,12},{12,8},{16,20},{20,16},{24,28},{28,24},{32,36},... | collective-permute-start | bytes 6291464 | tf_op jit(solution)/shard_map/ppermute | solution.py:355
  35.6 24.4 %collective-permute-start = (bf16[2,4,2,128,256]{4,3,2,1,0:T(8,128)(2,1)}, bf16[2,4,2,128,256]{4,3,2,1,0:T(8,128)(2,1)S(1)}, u32[]{:S(2)}, u32[]{:S(2)}) collective-permute-start(bf16[2,4,2,128,256]{4,3,2,1,0:T(8,128)(2,1)} %get-tuple-element.18), channel_id=1, source_target_pairs={{8,0},{16,8},{24,16},{32,24},{40,32},{48,40},{56,48},{64,56},{72,6... | collective-permute-start | bytes 3145736 | tf_op jit(solution)/shard_map/ppermute | solution.py:335
  42.4 5.3 %collective-permute-start.1 = (f32[8,512]{1,0:T(8,128)S(1)}, f32[8,512]{1,0:T(8,128)S(1)}, u32[]{:S(2)}, u32[]{:S(2)}) collective-permute-start(f32[8,512]{1,0:T(8,128)S(1)} %get-tuple-element.20.mine_ref.refs_3_), channel_id=1, source_target_pairs={{0,1},{1,0},{2,3},{3,2},{4,5},{5,4},{6,7},{7,6},{8,9},{9,8},{10,11... | collective-permute-start | bytes 49160 | tf_op jit(solution)/shard_map/ppermute | solution.py:344
  44.8 24.7 %collective-permute-start.5 = (bf16[2,256,512]{2,1,0:T(8,128)(2,1)S(1)}, bf16[2,256,512]{2,1,0:T(8,128)(2,1)S(1)}, u32[]{:S(2)}, u32[]{:S(2)}) collective-permute-start(bf16[2,256,512]{2,1,0:T(8,128)(2,1)S(1)} %get-tuple-element.24), channel_id=1, source_target_pairs={{0,1},{1,0},{2,3},{3,2},{4,5},{5,4},{6,7},{7,6},{8,9},{9,8},{10,11... | collective-permute-start | bytes 1572872 | tf_op jit(solution)/shard_map/ppermute | solution.py:345
  47.8 6.7 %collective-permute-start.2 = (f32[8,512]{1,0:T(8,128)S(1)}, f32[8,512]{1,0:T(8,128)S(1)}, u32[]{:S(2)}, u32[]{:S(2)}) collective-permute-start(f32[8,512]{1,0:T(8,128)S(1)} %get-tuple-element.21.refs_1_.refs_7_), channel_id=1, source_target_pairs={{0,4},{4,0},{8,12},{12,8},{16,20},{20,16},{24,28},{28,24},{32,36},... | collective-permute-start | bytes 49160 | tf_op jit(solution)/shard_map/ppermute | solution.py:357
  54.5 8.4 %collective-permute-start.3 = (f32[8,512]{1,0:T(8,128)S(1)}, f32[8,512]{1,0:T(8,128)S(1)}, u32[]{:S(2)}, u32[]{:S(2)}) collective-permute-start(f32[8,512]{1,0:T(8,128)S(1)} %collective-permute-done.2.refs_2_.refs_8_), channel_id=1, source_target_pairs={{12,0},{20,8},{28,16},{36,24},{44,32},{52,40},{60,48},{68,56},{76,... | collective-permute-start | bytes 49160 | tf_op jit(solution)/shard_map/ppermute | solution.py:358
  57.1 18.9 %collective-permute-start.8 = (bf16[2,4,2,128,256]{4,3,2,1,0:T(8,128)(2,1)S(1)}, bf16[2,4,2,128,256]{4,3,2,1,0:T(8,128)(2,1)S(1)}, u32[]{:S(2)}, u32[]{:S(2)}) collective-permute-start(bf16[2,4,2,128,256]{4,3,2,1,0:T(8,128)(2,1)S(1)} %get-tuple-element.28), channel_id=1, source_target_pairs={{8,0},{16,8},{24,16},{32,24},{40,32},{48,40},{56,48},{64,56},{72,6... | collective-permute-start | bytes 3145736 | tf_op jit(solution)/shard_map/ppermute | solution.py:354
  67.1 15.6 %collective-permute-start.6 = (bf16[2,2,2,128,256]{4,3,2,1,0:T(8,128)(2,1)S(1)}, bf16[2,2,2,128,256]{4,3,2,1,0:T(8,128)(2,1)S(1)}, u32[]{:S(2)}, u32[]{:S(2)}) collective-permute-start(bf16[2,2,2,128,256]{4,3,2,1,0:T(8,128)(2,1)S(1)} %get-tuple-element.27), channel_id=1, source_target_pairs={{0,1},{1,0},{2,3},{3,2},{4,5},{5,4},{6,7},{7,6},{8,9},{9,8},{10,11... | collective-permute-start | bytes 1572872 | tf_op jit(solution)/shard_map/ppermute | solution.py:373
  80.2 15.6 %collective-permute-start.9 = (bf16[2,2,2,128,256]{4,3,2,1,0:T(8,128)(2,1)S(1)}, bf16[2,2,2,128,256]{4,3,2,1,0:T(8,128)(2,1)S(1)}, u32[]{:S(2)}, u32[]{:S(2)}) collective-permute-start(bf16[2,2,2,128,256]{4,3,2,1,0:T(8,128)(2,1)S(1)} %get-tuple-element.30), channel_id=1, source_target_pairs={{0,1},{1,0},{2,3},{3,2},{4,5},{5,4},{6,7},{7,6},{8,9},{9,8},{10,11... | collective-permute-start | bytes 1572872 | tf_op jit(solution)/shard_map/ppermute | solution.py:373
  83.3 15.0 %collective-permute-start.7 = (bf16[2,2,2,128,256]{4,3,2,1,0:T(8,128)(2,1)S(1)}, bf16[2,2,2,128,256]{4,3,2,1,0:T(8,128)(2,1)S(1)}, u32[]{:S(2)}, u32[]{:S(2)}) collective-permute-start(bf16[2,2,2,128,256]{4,3,2,1,0:T(8,128)(2,1)S(1)} %decode.2.refs_2_._), channel_id=1, source_target_pairs={{12,4},{20,12},{28,20},{36,28},{44,36},{52,44},{60,52},{68,60},{76... | collective-permute-start | bytes 1572872 | tf_op jit(solution)/shard_map/ppermute | solution.py:393
  96.4 9.9 %collective-permute-start.10 = (bf16[2,2,2,128,256]{4,3,2,1,0:T(8,128)(2,1)S(1)}, bf16[2,2,2,128,256]{4,3,2,1,0:T(8,128)(2,1)S(1)}, u32[]{:S(2)}, u32[]{:S(2)}) collective-permute-start(bf16[2,2,2,128,256]{4,3,2,1,0:T(8,128)(2,1)S(1)} %decode.3.refs_2_), channel_id=1, source_target_pairs={{12,4},{20,12},{28,20},{36,28},{44,36},{52,44},{60,52},{68,60},{76... | collective-permute-start | bytes 1572872 | tf_op jit(solution)/shard_map/ppermute | solution.py:393

commit v3 on v2

--- a/solution.py
+++ b/solution.py
@@ -62,8 +62,9 @@
     ]
 
 
-def pack_kernel(own_ref, chunk_ref, token_ref, sem):
-    copies = chunk_copies(0, own_ref, chunk_ref, sem)
+def pack_kernel(own_ref, chunk0_ref, chunk1_ref, token_ref, sem):
+    copies = chunk_copies(0, own_ref, chunk0_ref, sem.at[0])
+    copies += chunk_copies(1, own_ref, chunk1_ref, sem.at[1])
     for copy in copies:
         copy.start()
     token_ref[...] = jnp.zeros_like(token_ref)
@@ -71,17 +72,13 @@
         copy.wait()
 
 
-def order_kernel(_, token_ref):
+def order_kernel(*refs):
+    token_ref = refs[-1]
     token_ref[...] = jnp.zeros_like(token_ref)
 
 
-def message_kernel(own_ref, mine_ref, other_ref, msg_ref, chunk_ref, sem):
-    copies = chunk_copies(1, own_ref, chunk_ref, sem)
-    for copy in copies:
-        copy.start()
+def message_kernel(mine_ref, other_ref, msg_ref):
     msg_ref[...] = mine_ref[...] + other_ref[...]
-    for copy in copies:
-        copy.wait()
 
 
 def self_kernel(pos_ref, band_ref, own_ref, kept_ref, given_ref, msg_ref, product_ref, col_ref):
@@ -323,14 +320,12 @@
     chunk_shape = (2, BAND, 2, CR, HALF)
     half_shape = (2, HALF, TS)
     token = ((8, 128), f32)
-    chunk0, after = call(
+    chunk0, chunk1, after = call(
         "pack",
         pack_kernel,
-        [(chunk_shape, bf16), token],
-        [ANY],
-        [pltpu.SemaphoreType.DMA((2,))],
-        out_specs=[ANY, VMEM],
-        vmem=52,
+        [(chunk_shape, bf16), (chunk_shape, bf16), token],
+        [VMEM],
+        [pltpu.SemaphoreType.DMA((2, 2))],
     )(own)
     far0 = lax.ppermute(chunk0, "rows", far_route)
     kept_self, given_self, my_energy = call(
@@ -343,14 +338,9 @@
     )(pos, band_tiles, own)
     other_energy = lax.ppermute(my_energy, "freq", swap)
     got_self = lax.ppermute(given_self, "freq", swap)
-    message, chunk1 = call(
-        "message",
-        message_kernel,
-        [((8, TS), f32), (chunk_shape, bf16)],
-        [VMEM] * 3,
-        [pltpu.SemaphoreType.DMA((2,))],
-        flops=MCOST,
-    )(own, my_energy, other_energy)
+    message = call("message", message_kernel, [((8, TS), f32)], [VMEM] * 2, flops=MCOST)(
+        my_energy, other_energy
+    )
     far1 = lax.ppermute(chunk1, "rows", far_route)
     near = lax.ppermute(own, "rows", pair)
     far = (far0, far1)
@@ -359,7 +349,7 @@
 
     unit_shape = (2, 2, 2, CR, HALF)
     after = call("order", order_kernel, [token], [ANY], flops=TCOST)(far0)
-    out, products = None, []
+    products = []
     for j in range(CHUNKS):
         kept, given = call(
             f"pair{j}",
@@ -372,21 +362,23 @@
         )(pos, message, near_message, far_message, own, near, far[j], message, near_message, far_message)
         got = lax.ppermute(given, "freq", swap)
         if j == 0:
-            out, after = call(
-                "finish",
-                self_finish_kernel,
-                [((2, 1, 3, HALF, TS), bf16), token],
-                [SMEM] + [VMEM] * 4,
-                [
-                    pltpu.VMEM((2, HALF, TS), bf16),
-                    pltpu.VMEM((2, TS, 128), f32),
-                    pltpu.SemaphoreType.DMA((2,)),
-                ],
-                flops=FCOST,
-                after=kept,
-                out_specs=[ANY, VMEM],
-            )(pos, kept_self, got_self, my_energy, other_energy)
+            after = call(
+                "order1", order_kernel, [token], [ANY, ANY], flops=FCOST, after=kept
+            )(got_self, far[1])
         products.append((kept, got))
+    out, after = call(
+        "finish",
+        self_finish_kernel,
+        [((2, 1, 3, HALF, TS), bf16), token],
+        [SMEM] + [VMEM] * 4,
+        [
+            pltpu.VMEM((2, HALF, TS), bf16),
+            pltpu.VMEM((2, TS, 128), f32),
+            pltpu.SemaphoreType.DMA((2,)),
+        ],
+        after=kept,
+        out_specs=[ANY, VMEM],
+    )(pos, kept_self, got_self, my_energy, other_energy)
     for j, (kept, got) in enumerate(products):
         fin = call("decode", pair_finish_kernel, [(unit_shape, bf16)], [VMEM, VMEM], after=after)(kept, got)
         after = fin

time: 108 us -> 77.6 us (0.72)
  the two profiles are of different devices: /device:TPU:391 before, /device:TPU:25 now
where the time goes in v3:
time: 77.6 us; the launch traced here: 77.2 us
  starting transfers between devices  34.8 us (45%)
  waiting for transfers between devices  20.4 us (26%)
  Pallas kernels  20.1 us (26%)
  local copies, waits for them, and re-layouts  1.59 us (2%)
    pallas_call x7, Pallas kernels, call(): return run if after is None else lambda *args: run(after, *args)  15.6 us
    ppermute x2, waiting for transfers between devices, shards(): got = lax.ppermute(given, 'freq', swap)  10.5 us
    ppermute x2, waiting for transfers between devices, shards(): back = lax.ppermute(fin, 'rows', back_route)  6.68 us
    ppermute x2, starting transfers between devices, shards(): back = lax.ppermute(fin, 'rows', back_route)  6.66 us
    ppermute x1, starting transfers between devices, shards(): far_message = lax.ppermute(near_message, 'rows', across_route)  6.51 us
    ppermute x2, starting transfers between devices, shards(): got = lax.ppermute(given, 'freq', swap)  5.28 us
    ppermute x1, starting transfers between devices, shards(): far1 = lax.ppermute(chunk1, 'rows', far_route)  3.21 us
    ppermute x1, starting transfers between devices, shards(): far0 = lax.ppermute(chunk0, 'rows', far_route)  3.2 us
  transfers between devices with their start and end apart: 11, of which 5 were waited for; matrix products, arithmetic and copies ran while one was open for 0% of the time, Pallas kernels for 24%

profile of v3, /device:TPU:25, one launch (start us, length us, event | category | flops | bytes accessed | tf_op | source)
XLA Modules:
  0.0 77.2 jit_solution(4787660713435470405)
XLA Ops:
  0.0 0.0 copy-start.2
  0.0 2.7 %collective-permute-start.4 = (bf16[2,4,512,256]{3,2,1,0:T(8,128)(2,1)}, bf16[2,4,512,256]{3,2,1,0:T(8,128)(2,1)}, u32[]{:S(2)}, u32[]{:S(2)}) collective-permute-start(bf16[2,4,512,256]{3,2,1,0:T(8,128)(2,1)} %bitcast.3), channel_id=1, source_target_pairs={{0,4},{4,0},{8,12},{12,8},{16,20},{20,16},{24,28},{28,24},{32,36},... | collective-permute-start | bytes 6291464 | tf_op jit(solution)/shard_map/ppermute | solution.py:345
  2.7 0.0 copy-start
  2.7 1.6 %copy-done = bf16[2,1,4,512,256]{4,3,2,1,0:T(8,128)(2,1)S(1)} copy-done((bf16[2,1,4,512,256]{4,3,2,1,0:T(8,128)(2,1)S(1)}, bf16[2,1,4,512,256]{4,3,2,1,0:T(8,128)(2,1)}, u32[]{:S(2)}) %copy-start) | copy-done | bytes 2097176
  4.3 0.0 copy-start.1
  4.3 1.5 %pack.1 = (bf16[2,4,2,128,256]{4,3,2,1,0:T(8,128)(2,1)}, bf16[2,4,2,128,256]{4,3,2,1,0:T(8,128)(2,1)}, f32[8,128]{1,0:T(8,128)S(1)}) custom-call(bf16[2,4,512,256]{3,2,1,0:T(8,128)(2,1)S(1)} %bitcast.4), custom_call_target="tpu_custom_call" | custom-call | bytes 2097152 | tf_op jit(solution)/shard_map/pack/pallas_call | solution.py:323
  5.8 3.2 %collective-permute-start = (bf16[2,4,2,128,256]{4,3,2,1,0:T(8,128)(2,1)}, bf16[2,4,2,128,256]{4,3,2,1,0:T(8,128)(2,1)S(1)}, u32[]{:S(2)}, u32[]{:S(2)}) collective-permute-start(bf16[2,4,2,128,256]{4,3,2,1,0:T(8,128)(2,1)} %get-tuple-element.17), channel_id=1, source_target_pairs={{8,0},{16,8},{24,16},{32,24},{40,32},{48,40},{56,48},{64,56},{72,6... | collective-permute-start | bytes 3145736 | tf_op jit(solution)/shard_map/ppermute | solution.py:330
  9.1 3.2 %collective-permute-start.6 = (bf16[2,4,2,128,256]{4,3,2,1,0:T(8,128)(2,1)}, bf16[2,4,2,128,256]{4,3,2,1,0:T(8,128)(2,1)}, u32[]{:S(2)}, u32[]{:S(2)}) collective-permute-start(bf16[2,4,2,128,256]{4,3,2,1,0:T(8,128)(2,1)} %get-tuple-element.22), channel_id=1, source_target_pairs={{8,0},{16,8},{24,16},{32,24},{40,32},{48,40},{56,48},{64,56},{72,6... | collective-permute-start | bytes 3145736 | tf_op jit(solution)/shard_map/ppermute | solution.py:344
  12.3 0.1 pad_add_fusion.refs_0_
  12.4 0.0 copy-done.2
  12.4 0.0 copy-done.1
  12.4 3.4 %self.1 = (f32[2,256,512]{2,1,0:T(8,128)S(1)}, bf16[2,256,512]{2,1,0:T(8,128)(2,1)S(1)}, f32[8,512]{1,0:T(8,128)S(1)}) custom-call(f32[8,128]{1,0:T(8,128)S(1)} %get-tuple-element.18._, s32[2]{0:T(128)S(1)} %pad_add_fusion.refs_0_, s32[1,4]{1,0:T(1,128)S(1)} %copy-done.2, bf16[2,4,512,256]{3,2,1,0:T(8,128)(2,1)S(1)} %bitcast.5), custom_call_target="tpu_custom_call" | custom-call | bytes 2097152 | tf_op jit(solution)/shard_map/self/pallas_call | solution.py:304
  15.8 3.1 %collective-permute-start.1 = (f32[8,512]{1,0:T(8,128)S(1)}, f32[8,512]{1,0:T(8,128)S(1)}, u32[]{:S(2)}, u32[]{:S(2)}) collective-permute-start(f32[8,512]{1,0:T(8,128)S(1)} %get-tuple-element.19.mine_ref.refs_3_), channel_id=1, source_target_pairs={{0,1},{1,0},{2,3},{3,2},{4,5},{5,4},{6,7},{7,6},{8,9},{9,8},{10,11... | collective-permute-start | bytes 49160 | tf_op jit(solution)/shard_map/ppermute | solution.py:339
  18.9 2.1 %collective-permute-start.5 = (bf16[2,256,512]{2,1,0:T(8,128)(2,1)S(1)}, bf16[2,256,512]{2,1,0:T(8,128)(2,1)S(1)}, u32[]{:S(2)}, u32[]{:S(2)}) collective-permute-start(bf16[2,256,512]{2,1,0:T(8,128)(2,1)S(1)} %get-tuple-element.21), channel_id=1, source_target_pairs={{0,1},{1,0},{2,3},{3,2},{4,5},{5,4},{6,7},{7,6},{8,9},{9,8},{10,11... | collective-permute-start | bytes 1572872 | tf_op jit(solution)/shard_map/ppermute | solution.py:340
  21.1 0.0 collective-permute-done.1.other_ref.refs_4_
  21.1 1.9 %collective-permute-start.2 = (f32[8,512]{1,0:T(8,128)S(1)}, f32[8,512]{1,0:T(8,128)S(1)}, u32[]{:S(2)}, u32[]{:S(2)}) collective-permute-start(f32[8,512]{1,0:T(8,128)S(1)} %message.1.refs_1_.refs_7_), channel_id=1, source_target_pairs={{0,4},{4,0},{8,12},{12,8},{16,20},{20,16},{24,28},{28,24},{32,36},... | collective-permute-start | bytes 49160 | tf_op jit(solution)/shard_map/ppermute | solution.py:347
  23.1 1.1 %collective-permute-done.2.refs_2_.refs_8_ = f32[8,512]{1,0:T(8,128)S(1)} collective-permute-done((f32[8,512]{1,0:T(8,128)S(1)}, f32[8,512]{1,0:T(8,128)S(1)}, u32[]{:S(2)}, u32[]{:S(2)}) %collective-permute-start.2) | collective-permute-done | bytes 16416 | tf_op jit(solution)/shard_map/ppermute | solution.py:347
  24.2 6.5 %collective-permute-start.3 = (f32[8,512]{1,0:T(8,128)S(1)}, f32[8,512]{1,0:T(8,128)S(1)}, u32[]{:S(2)}, u32[]{:S(2)}) collective-permute-start(f32[8,512]{1,0:T(8,128)S(1)} %collective-permute-done.2.refs_2_.refs_8_), channel_id=1, source_target_pairs={{12,0},{20,8},{28,16},{36,24},{44,32},{52,40},{60,48},{68,56},{76,... | collective-permute-start | bytes 49160 | tf_op jit(solution)/shard_map/ppermute | solution.py:348
  30.7 0.0 collective-permute-done.refs_0_.refs_6_
  30.7 2.0 %collective-permute-done.3.refs_3_.refs_9_ = f32[8,512]{1,0:T(8,128)S(1)} collective-permute-done((f32[8,512]{1,0:T(8,128)S(1)}, f32[8,512]{1,0:T(8,128)S(1)}, u32[]{:S(2)}, u32[]{:S(2)}) %collective-permute-start.3) | collective-permute-done | bytes 16416 | tf_op jit(solution)/shard_map/ppermute | solution.py:348
  32.8 0.0 collective-permute-done.4.refs_5_
  32.8 4.3 %pair0.1 = (f32[2,2,2,128,256]{4,3,2,1,0:T(8,128)S(1)}, bf16[2,2,2,128,256]{4,3,2,1,0:T(8,128)(2,1)S(1)}) custom-call(f32[8,128]{1,0:T(8,128)S(1)} %order.1._, s32[2]{0:T(128)S(1)} %pad_add_fusion.refs_0_, f32[8,512]{1,0:T(8,128)S(1)} %message.1.refs_1_.refs_7_, f32[8,512]{1,0:T(8,128)S(1)} %collective-permute-done.2.refs_2_.refs_8_, ...), custom_call_target="tpu_custom_call" | custom-call | bytes 2097152 | tf_op jit(solution)/shard_map/pair0/pallas_call | solution.py:304
  37.0 1.9 %collective-permute-start.7 = (bf16[2,2,2,128,256]{4,3,2,1,0:T(8,128)(2,1)S(1)}, bf16[2,2,2,128,256]{4,3,2,1,0:T(8,128)(2,1)S(1)}, u32[]{:S(2)}, u32[]{:S(2)}) collective-permute-start(bf16[2,2,2,128,256]{4,3,2,1,0:T(8,128)(2,1)S(1)} %get-tuple-element.27), channel_id=1, source_target_pairs={{0,1},{1,0},{2,3},{3,2},{4,5},{5,4},{6,7},{7,6},{8,9},{9,8},{10,11... | collective-permute-start | bytes 1572872 | tf_op jit(solution)/shard_map/ppermute | solution.py:363
  39.0 0.0 collective-permute-done.5.refs_0_.refs_2_
  39.0 0.0 collective-permute-done.6.refs_1_.refs_6_
  39.0 4.5 %pair1.1 = (f32[2,2,2,128,256]{4,3,2,1,0:T(8,128)S(1)}, bf16[2,2,2,128,256]{4,3,2,1,0:T(8,128)(2,1)S(1)}) custom-call(f32[8,128]{1,0:T(8,128)S(1)} %order1.1._, s32[2]{0:T(128)S(1)} %pad_add_fusion.refs_0_, f32[8,512]{1,0:T(8,128)S(1)} %message.1.refs_1_.refs_7_, f32[8,512]{1,0:T(8,128)S(1)} %collective-permute-done.2.refs_2_.refs_8_, ...), custom_call_target="tpu_custom_call" | custom-call | bytes 2097152 | tf_op jit(solution)/shard_map/pair1/pallas_call | solution.py:304
  43.5 3.4 %collective-permute-start.9 = (bf16[2,2,2,128,256]{4,3,2,1,0:T(8,128)(2,1)S(1)}, bf16[2,2,2,128,256]{4,3,2,1,0:T(8,128)(2,1)S(1)}, u32[]{:S(2)}, u32[]{:S(2)}) collective-permute-start(bf16[2,2,2,128,256]{4,3,2,1,0:T(8,128)(2,1)S(1)} %get-tuple-element.28), channel_id=1, source_target_pairs={{0,1},{1,0},{2,3},{3,2},{4,5},{5,4},{6,7},{7,6},{8,9},{9,8},{10,11... | collective-permute-start | bytes 1572872 | tf_op jit(solution)/shard_map/ppermute | solution.py:363
  46.9 2.2 %finish.1 = (bf16[2,1,3,256,512]{4,3,2,1,0:T(8,128)(2,1)}, f32[8,128]{1,0:T(8,128)S(1)}) custom-call(f32[2,2,2,128,256]{4,3,2,1,0:T(8,128)S(1)} %get-tuple-element.23._.refs_0_, s32[2]{0:T(128)S(1)} %pad_add_fusion.refs_0_, f32[2,256,512]{2,1,0:T(8,128)S(1)} %get-tuple-element.24.refs_1_, bf16[2,256,512]{2,1,0:T(8,128)(2,1)S(1)} %collective-permute-done.5.refs_0_.refs_2_, ...), custom_call_target="tpu_custom_call" | custom-call | bytes 2097152 | tf_op jit(solution)/shard_map/finish/pallas_call | solution.py:304
  49.1 3.7 %collective-permute-done.7.refs_1_ = bf16[2,2,2,128,256]{4,3,2,1,0:T(8,128)(2,1)S(1)} collective-permute-done((bf16[2,2,2,128,256]{4,3,2,1,0:T(8,128)(2,1)S(1)}, bf16[2,2,2,128,256]{4,3,2,1,0:T(8,128)(2,1)S(1)}, u32[]{:S(2)}, u32[]{:S(2)}) %collective-permute-start.7) | collective-permute-done | bytes 524320 | tf_op jit(solution)/shard_map/ppermute | solution.py:363
  52.8 0.6 decode.2.refs_2_._
  53.4 2.8 %collective-permute-start.8 = (bf16[2,2,2,128,256]{4,3,2,1,0:T(8,128)(2,1)S(1)}, bf16[2,2,2,128,256]{4,3,2,1,0:T(8,128)(2,1)S(1)}, u32[]{:S(2)}, u32[]{:S(2)}) collective-permute-start(bf16[2,2,2,128,256]{4,3,2,1,0:T(8,128)(2,1)S(1)} %decode.2.refs_2_._), channel_id=1, source_target_pairs={{12,4},{20,12},{28,20},{36,28},{44,36},{52,44},{60,52},{68,60},{76... | collective-permute-start | bytes 1572872 | tf_op jit(solution)/shard_map/ppermute | solution.py:385
  56.2 6.8 %collective-permute-done.9.refs_1_ = bf16[2,2,2,128,256]{4,3,2,1,0:T(8,128)(2,1)S(1)} collective-permute-done((bf16[2,2,2,128,256]{4,3,2,1,0:T(8,128)(2,1)S(1)}, bf16[2,2,2,128,256]{4,3,2,1,0:T(8,128)(2,1)S(1)}, u32[]{:S(2)}, u32[]{:S(2)}) %collective-permute-start.9) | collective-permute-done | bytes 524320 | tf_op jit(solution)/shard_map/ppermute | solution.py:363
  63.1 0.6 decode.3.refs_2_
  63.6 3.8 %collective-permute-start.10 = (bf16[2,2,2,128,256]{4,3,2,1,0:T(8,128)(2,1)S(1)}, bf16[2,2,2,128,256]{4,3,2,1,0:T(8,128)(2,1)S(1)}, u32[]{:S(2)}, u32[]{:S(2)}) collective-permute-start(bf16[2,2,2,128,256]{4,3,2,1,0:T(8,128)(2,1)S(1)} %decode.3.refs_2_), channel_id=1, source_target_pairs={{12,4},{20,12},{28,20},{36,28},{44,36},{52,44},{60,52},{68,60},{76... | collective-permute-start | bytes 1572872 | tf_op jit(solution)/shard_map/ppermute | solution.py:385
  67.5 0.0 collective-permute-done.8.refs_3_
  67.5 1.5 %place0.1.refs_1_ = bf16[2,1,3,256,512]{4,3,2,1,0:T(8,128)(2,1)} custom-call(s32[2]{0:T(128)S(1)} %pad_add_fusion.refs_0_, bf16[2,1,3,256,512]{4,3,2,1,0:T(8,128)(2,1)} %get-tuple-element.25.refs_1_, bf16[2,2,2,128,256]{4,3,2,1,0:T(8,128)(2,1)S(1)} %decode.2.refs_2_._, ...), custom_call_target="tpu_custom_call", output_to_operand_aliasing={{}: (1, {})} | custom-call | bytes 2097152 | tf_op jit(solution)/shard_map/place0/pallas_call | solution.py:386
  69.0 6.7 %collective-permute-done.10.refs_3_ = bf16[2,2,2,128,256]{4,3,2,1,0:T(8,128)(2,1)S(1)} collective-permute-done((bf16[2,2,2,128,256]{4,3,2,1,0:T(8,128)(2,1)S(1)}, bf16[2,2,2,128,256]{4,3,2,1,0:T(8,128)(2,1)S(1)}, u32[]{:S(2)}, u32[]{:S(2)}) %collective-permute-start.10) | collective-permute-done | bytes 524320 | tf_op jit(solution)/shard_map/ppermute | solution.py:385
  75.7 1.5 %place1.1 = bf16[2,1,3,256,512]{4,3,2,1,0:T(8,128)(2,1)} custom-call(s32[2]{0:T(128)S(1)} %pad_add_fusion.refs_0_, bf16[2,1,3,256,512]{4,3,2,1,0:T(8,128)(2,1)} %place0.1.refs_1_, bf16[2,2,2,128,256]{4,3,2,1,0:T(8,128)(2,1)S(1)} %decode.3.refs_2_, bf16[2,2,2,128,256]{4,3,2,1,0:T(8,128)(2,1)S(1)} %collective-permute-done.10.refs_3_), custom_call_target="tpu_custom_call", output_to_operand_aliasing={{}: (1, {})} | custom-call | bytes 2097152 | tf_op jit(solution)/shard_map/place1/pallas_call | solution.py:386
  (3 shorter events, 0.0 us)
Async XLA Ops:
  0.0 12.4 %copy-start.2 = (s32[1,4]{1,0:T(1,128)S(1)}, s32[1,4]{1,0:T(1,128)}, u32[]{:S(2)}) copy-start(s32[1,4]{1,0:T(1,128)} %refs_1_.1) | copy-start | bytes 52
  0.0 32.8 %collective-permute-start.4 = (bf16[2,4,512,256]{3,2,1,0:T(8,128)(2,1)}, bf16[2,4,512,256]{3,2,1,0:T(8,128)(2,1)}, u32[]{:S(2)}, u32[]{:S(2)}) collective-permute-start(bf16[2,4,512,256]{3,2,1,0:T(8,128)(2,1)} %bitcast.3), channel_id=1, source_target_pairs={{0,4},{4,0},{8,12},{12,8},{16,20},{20,16},{24,28},{28,24},{32,36},... | collective-permute-start | bytes 6291464 | tf_op jit(solution)/shard_map/ppermute | solution.py:345
  2.7 1.6 %copy-start = (bf16[2,1,4,512,256]{4,3,2,1,0:T(8,128)(2,1)S(1)}, bf16[2,1,4,512,256]{4,3,2,1,0:T(8,128)(2,1)}, u32[]{:S(2)}) copy-start(bf16[2,1,4,512,256]{4,3,2,1,0:T(8,128)(2,1)} %param.2) | copy-start | bytes 6291460
  4.3 8.1 %copy-start.1 = (bf16[2,1,4,512,256]{4,3,2,1,0:T(8,128)(2,1)S(1)}, bf16[2,1,4,512,256]{4,3,2,1,0:T(8,128)(2,1)}, u32[]{:S(2)}) copy-start(bf16[2,1,4,512,256]{4,3,2,1,0:T(8,128)(2,1)} %param.2) | copy-start | bytes 6291460
  5.8 24.9 %collective-permute-start = (bf16[2,4,2,128,256]{4,3,2,1,0:T(8,128)(2,1)}, bf16[2,4,2,128,256]{4,3,2,1,0:T(8,128)(2,1)S(1)}, u32[]{:S(2)}, u32[]{:S(2)}) collective-permute-start(bf16[2,4,2,128,256]{4,3,2,1,0:T(8,128)(2,1)} %get-tuple-element.17), channel_id=1, source_target_pairs={{8,0},{16,8},{24,16},{32,24},{40,32},{48,40},{56,48},{64,56},{72,6... | collective-permute-start | bytes 3145736 | tf_op jit(solution)/shard_map/ppermute | solution.py:330
  9.1 29.9 %collective-permute-start.6 = (bf16[2,4,2,128,256]{4,3,2,1,0:T(8,128)(2,1)}, bf16[2,4,2,128,256]{4,3,2,1,0:T(8,128)(2,1)}, u32[]{:S(2)}, u32[]{:S(2)}) collective-permute-start(bf16[2,4,2,128,256]{4,3,2,1,0:T(8,128)(2,1)} %get-tuple-element.22), channel_id=1, source_target_pairs={{8,0},{16,8},{24,16},{32,24},{40,32},{48,40},{56,48},{64,56},{72,6... | collective-permute-start | bytes 3145736 | tf_op jit(solution)/shard_map/ppermute | solution.py:344
  15.8 5.3 %collective-permute-start.1 = (f32[8,512]{1,0:T(8,128)S(1)}, f32[8,512]{1,0:T(8,128)S(1)}, u32[]{:S(2)}, u32[]{:S(2)}) collective-permute-start(f32[8,512]{1,0:T(8,128)S(1)} %get-tuple-element.19.mine_ref.refs_3_), channel_id=1, source_target_pairs={{0,1},{1,0},{2,3},{3,2},{4,5},{5,4},{6,7},{7,6},{8,9},{9,8},{10,11... | collective-permute-start | bytes 49160 | tf_op jit(solution)/shard_map/ppermute | solution.py:339
  18.9 20.0 %collective-permute-start.5 = (bf16[2,256,512]{2,1,0:T(8,128)(2,1)S(1)}, bf16[2,256,512]{2,1,0:T(8,128)(2,1)S(1)}, u32[]{:S(2)}, u32[]{:S(2)}) collective-permute-start(bf16[2,256,512]{2,1,0:T(8,128)(2,1)S(1)} %get-tuple-element.21), channel_id=1, source_target_pairs={{0,1},{1,0},{2,3},{3,2},{4,5},{5,4},{6,7},{7,6},{8,9},{9,8},{10,11... | collective-permute-start | bytes 1572872 | tf_op jit(solution)/shard_map/ppermute | solution.py:340
  21.1 3.1 %collective-permute-start.2 = (f32[8,512]{1,0:T(8,128)S(1)}, f32[8,512]{1,0:T(8,128)S(1)}, u32[]{:S(2)}, u32[]{:S(2)}) collective-permute-start(f32[8,512]{1,0:T(8,128)S(1)} %message.1.refs_1_.refs_7_), channel_id=1, source_target_pairs={{0,4},{4,0},{8,12},{12,8},{16,20},{20,16},{24,28},{28,24},{32,36},... | collective-permute-start | bytes 49160 | tf_op jit(solution)/shard_map/ppermute | solution.py:347
  24.2 8.6 %collective-permute-start.3 = (f32[8,512]{1,0:T(8,128)S(1)}, f32[8,512]{1,0:T(8,128)S(1)}, u32[]{:S(2)}, u32[]{:S(2)}) collective-permute-start(f32[8,512]{1,0:T(8,128)S(1)} %collective-permute-done.2.refs_2_.refs_8_), channel_id=1, source_target_pairs={{12,0},{20,8},{28,16},{36,24},{44,32},{52,40},{60,48},{68,56},{76,... | collective-permute-start | bytes 49160 | tf_op jit(solution)/shard_map/ppermute | solution.py:348
  37.0 15.8 %collective-permute-start.7 = (bf16[2,2,2,128,256]{4,3,2,1,0:T(8,128)(2,1)S(1)}, bf16[2,2,2,128,256]{4,3,2,1,0:T(8,128)(2,1)S(1)}, u32[]{:S(2)}, u32[]{:S(2)}) collective-permute-start(bf16[2,2,2,128,256]{4,3,2,1,0:T(8,128)(2,1)S(1)} %get-tuple-element.27), channel_id=1, source_target_pairs={{0,1},{1,0},{2,3},{3,2},{4,5},{5,4},{6,7},{7,6},{8,9},{9,8},{10,11... | collective-permute-start | bytes 1572872 | tf_op jit(solution)/shard_map/ppermute | solution.py:363
  43.5 19.5 %collective-permute-start.9 = (bf16[2,2,2,128,256]{4,3,2,1,0:T(8,128)(2,1)S(1)}, bf16[2,2,2,128,256]{4,3,2,1,0:T(8,128)(2,1)S(1)}, u32[]{:S(2)}, u32[]{:S(2)}) collective-permute-start(bf16[2,2,2,128,256]{4,3,2,1,0:T(8,128)(2,1)S(1)} %get-tuple-element.28), channel_id=1, source_target_pairs={{0,1},{1,0},{2,3},{3,2},{4,5},{5,4},{6,7},{7,6},{8,9},{9,8},{10,11... | collective-permute-start | bytes 1572872 | tf_op jit(solution)/shard_map/ppermute | solution.py:363
  53.4 14.1 %collective-permute-start.8 = (bf16[2,2,2,128,256]{4,3,2,1,0:T(8,128)(2,1)S(1)}, bf16[2,2,2,128,256]{4,3,2,1,0:T(8,128)(2,1)S(1)}, u32[]{:S(2)}, u32[]{:S(2)}) collective-permute-start(bf16[2,2,2,128,256]{4,3,2,1,0:T(8,128)(2,1)S(1)} %decode.2.refs_2_._), channel_id=1, source_target_pairs={{12,4},{20,12},{28,20},{36,28},{44,36},{52,44},{60,52},{68,60},{76... | collective-permute-start | bytes 1572872 | tf_op jit(solution)/shard_map/ppermute | solution.py:385
  63.6 12.0 %collective-permute-start.10 = (bf16[2,2,2,128,256]{4,3,2,1,0:T(8,128)(2,1)S(1)}, bf16[2,2,2,128,256]{4,3,2,1,0:T(8,128)(2,1)S(1)}, u32[]{:S(2)}, u32[]{:S(2)}) collective-permute-start(bf16[2,2,2,128,256]{4,3,2,1,0:T(8,128)(2,1)S(1)} %decode.3.refs_2_), channel_id=1, source_target_pairs={{12,4},{20,12},{28,20},{36,28},{44,36},{52,44},{60,52},{68,60},{76... | collective-permute-start | bytes 1572872 | tf_op jit(solution)/shard_map/ppermute | solution.py:385

commit v4 on v2

--- a/solution.py
+++ b/solution.py
@@ -10,6 +10,7 @@
 BAND = 4
 CHUNKS = 2
 CR = HALF // CHUNKS
+TILES = 8
 EPSILON = 1e-06
 TINY = 1e-30
 CODE = 2.0**7.5
@@ -17,10 +18,10 @@
 ANY = pl.BlockSpec(memory_space=pl.ANY)
 SMEM = pl.BlockSpec(memory_space=pltpu.SMEM)
 MIB = 1024 * 1024
-MCOST = 2**33
+MCOST = 0
 PCOST = 0
-TCOST = 0
-FCOST = 2**36
+TCOST = 2**32
+FCOST = 2**33
 
 
 def encode(x):
@@ -43,6 +44,40 @@
     return jnp.transpose(jnp.broadcast_to(row, (128, width)))
 
 
+def tile_rows(unit, part, tile):
+    return pl.ds(((unit * 2 + part) * 2 + tile) * CR, CR)
+
+
+def put_energies(messages, given_ref):
+    for i, message in enumerate(messages):
+        rest = message[0:1, :]
+        for level in range(3):
+            term = rest.astype(jnp.bfloat16)
+            rest = rest - term.astype(jnp.float32)
+            for h in range(2):
+                row = TILES * CR + (i * 3 + level) * 2 + h
+                given_ref[row : row + 1, :] = term[:, h * HALF : h * HALF + HALF]
+
+
+def get_energy(got_ref, i):
+    tail = got_ref[TILES * CR :, :].astype(jnp.float32)
+    halves = []
+    for h in range(2):
+        rows = [tail[(i * 3 + level) * 2 + h :][:1] for level in range(3)]
+        halves.append(rows[0] + (rows[1] + rows[2]))
+    return jnp.concatenate(halves, axis=1)
+
+
+def inverse(energy):
+    return lax.rsqrt(jnp.maximum(energy, TINY))
+
+
+def chunk_of_lanes(row, j):
+    return jnp.concatenate(
+        [row[:, h * HALF + j * CR : h * HALF + j * CR + CR] for h in range(2)], axis=1
+    )
+
+
 def complex_product(left, right_re, right_im):
     dims = (((1,), (1,)), ((), ()))
     with_re = lax.dot_general(left, right_re, dims, preferred_element_type=jnp.float32)
@@ -62,26 +97,25 @@
     ]
 
 
-def pack_kernel(own_ref, chunk_ref, token_ref, sem):
-    copies = chunk_copies(0, own_ref, chunk_ref, sem)
+def run(copies):
     for copy in copies:
         copy.start()
-    token_ref[...] = jnp.zeros_like(token_ref)
     for copy in copies:
         copy.wait()
 
 
-def order_kernel(_, token_ref):
+def pack_kernel(own_ref, chunk0_ref, token_ref, sem):
     token_ref[...] = jnp.zeros_like(token_ref)
-
-
-def message_kernel(own_ref, mine_ref, other_ref, msg_ref, chunk_ref, sem):
-    copies = chunk_copies(1, own_ref, chunk_ref, sem)
-    for copy in copies:
-        copy.start()
-    msg_ref[...] = mine_ref[...] + other_ref[...]
-    for copy in copies:
-        copy.wait()
+    run(chunk_copies(0, own_ref, chunk0_ref, sem))
+
+
+def order_kernel(*refs):
+    token_ref = refs[-1]
+    token_ref[...] = jnp.zeros_like(token_ref)
+
+
+def second_kernel(own_ref, chunk1_ref, sem):
+    run(chunk_copies(1, own_ref, chunk1_ref, sem))
 
 
 def self_kernel(pos_ref, band_ref, own_ref, kept_ref, given_ref, msg_ref, product_ref, col_ref):
@@ -128,6 +162,9 @@
 ):
     core = pos_ref[0]
     mine = pos_ref[1]
+    if j == 0:
+        given_ref[TILES * CR :, :] = jnp.zeros((32, HALF), jnp.bfloat16)
+        put_energies((own_m, near_m, far_m), given_ref)
 
     def shift(left_s, right_s):
         first = right_s[1, 0]
@@ -150,24 +187,20 @@
             )
         return load
 
-    def chunk_of_lanes(ref):
-        return jnp.concatenate(
-            [ref[0:1, h * HALF + j * CR : h * HALF + j * CR + CR] for h in range(2)], axis=1
-        )
-
-    def emit(unit, keep, real, imag, scale, split):
+    def emit(unit, keep, real, imag, start, rows, row, split):
         for part, value in enumerate((real, imag)):
-            value = value * scale
+            if not keep:
+                value = encode(value * (col_ref[pl.ds(start, rows), 0:1] * row))
             for tile in range(2):
                 piece = split(value, tile)
                 if keep:
                     kept_ref[unit, part, tile] = piece
                 else:
-                    given_ref[unit, part, tile] = encode(piece)
+                    given_ref[tile_rows(unit, part, tile), :] = piece
 
     @pl.when(core == 0)
     def _():
-        col_ref[...] = column(own_m[0:1, :])
+        col_ref[...] = column(inverse(own_m[0:1, :]))
         units = (
             (near_s, chunk_of_rows(near_ref), near_m),
             (far_s, lambda part, k: far_ref[part, k].reshape(2 * CR, HALF), far_m),
@@ -176,7 +209,7 @@
             s = shift(own_s, right_s)
             right_re = aligned(load, 0, s)
             right_im = aligned(load, 1, s)
-            row = chunk_of_lanes(right_m)
+            row = inverse(chunk_of_lanes(right_m[0:1, :], j))
             for keep in (False, True):
                 start = pl.multiple_of((mine if keep else 1 - mine) * HALF, HALF)
                 left = jnp.concatenate(
@@ -189,19 +222,18 @@
                     axis=0,
                 )
                 real, imag = complex_product(left, right_re, right_im)
-                scale = lax.rsqrt(col_ref[pl.ds(start, HALF), 0:1] * row + EPSILON)
-                emit(unit, keep, real, imag, scale, lambda v, t: v[t * CR : t * CR + CR])
+                emit(unit, keep, real, imag, start, HALF, row, lambda v, t: v[t * CR : t * CR + CR])
 
     @pl.when(core == 1)
     def _():
-        col_ref[...] = column(far_m[0:1, :])
+        col_ref[...] = column(inverse(far_m[0:1, :]))
         units = ((near_s, near_ref, near_m), (own_s, own_ref, own_m))
         for unit, (right_s, right_ref, right_m) in enumerate(units):
             s = shift(far_s, right_s)
             load = lambda part, k: right_ref[part, k]
             right_re = aligned(load, 0, s)
             right_im = aligned(load, 1, s)
-            row = right_m[0:1, :]
+            row = inverse(right_m[0:1, :])
             for keep in (False, True):
                 half = mine if keep else 1 - mine
                 left = jnp.concatenate(
@@ -213,17 +245,17 @@
                 )
                 real, imag = complex_product(left, right_re, right_im)
                 start = pl.multiple_of(half * HALF + j * CR, CR)
-                scale = lax.rsqrt(col_ref[pl.ds(start, CR), 0:1] * row + EPSILON)
-                emit(unit, keep, real, imag, scale, lambda v, t: v[:, t * HALF : t * HALF + HALF])
+                emit(unit, keep, real, imag, start, CR, row, lambda v, t: v[:, t * HALF : t * HALF + HALF])
 
 
 def self_finish_kernel(
-    pos_ref, kept_ref, got_ref, mine_ref, other_ref, out_ref, token_ref, fin_ref, col_ref, sem
+    pos_ref, kept_ref, got_ref, mine_ref, first_ref, out_ref, token_ref, fin_ref, col_ref, sem
 ):
     token_ref[...] = jnp.zeros_like(token_ref)
     start = pl.multiple_of(pos_ref[1] * HALF, HALF)
-    other = jnp.sqrt(jnp.maximum(other_ref[0:1, :], TINY))
-    total = mine_ref[0:1, :] + other_ref[0:1, :]
+    energy = get_energy(first_ref, 0)
+    other = jnp.sqrt(jnp.maximum(energy, TINY))
+    total = mine_ref[0:1, :] + energy
     col_ref[0] = column(other)
     col_ref[1] = column(total)
     scale = lax.rsqrt(col_ref[1, pl.ds(start, HALF), 0:1] * total + EPSILON)
@@ -241,24 +273,46 @@
         copy.wait()
 
 
-def pair_finish_kernel(kept_ref, got_ref, fin_ref):
-    for unit in range(2):
+def pair_finish_kernel(
+    j, pos_ref, kept_ref, got_ref, own_m, near_m, far_m, first_ref, fin_ref, col_ref
+):
+    core = pos_ref[0]
+    mine = pos_ref[1]
+    other = [get_energy(first_ref, i) for i in range(3)]
+    total = [m[0:1, :] + o for m, o in zip((own_m, near_m, far_m), other)]
+    root = [jnp.sqrt(jnp.maximum(o, TINY)) for o in other]
+
+    def emit(unit, tile, start, root_row, total_row):
+        back = col_ref[0, pl.ds(start, CR), 0:1] * root_row
+        scale = lax.rsqrt(col_ref[1, pl.ds(start, CR), 0:1] * total_row + EPSILON)
         for part in range(2):
+            value = kept_ref[unit, part, tile] + decode(got_ref[tile_rows(unit, part, tile), :]) * back
+            fin_ref[unit, part, tile] = (value * scale).astype(jnp.bfloat16)
+
+    @pl.when(core == 0)
+    def _():
+        col_ref[0] = column(root[0])
+        col_ref[1] = column(total[0])
+        for unit, i in enumerate((1, 2)):
             for tile in range(2):
-                value = kept_ref[unit, part, tile] + decode(got_ref[unit, part, tile])
-                fin_ref[unit, part, tile] = value.astype(jnp.bfloat16)
+                start = pl.multiple_of(mine * HALF + tile * CR, CR)
+                emit(unit, tile, start, chunk_of_lanes(root[i], j), chunk_of_lanes(total[i], j))
+
+    @pl.when(core == 1)
+    def _():
+        col_ref[0] = column(root[2])
+        col_ref[1] = column(total[2])
+        start = pl.multiple_of(mine * HALF + j * CR, CR)
+        for unit, i in enumerate((1, 0)):
+            for tile in range(2):
+                lanes = slice(tile * HALF, tile * HALF + HALF)
+                emit(unit, tile, start, root[i][:, lanes], total[i][:, lanes])
 
 
 def place_kernel(j, pos_ref, out_in_ref, fin_ref, back_ref, out_ref, sem):
     del out_in_ref
     rows = pl.ds(j * CR, CR)
     pieces = [(unit, part, tile) for unit in range(2) for part in range(2) for tile in range(2)]
-
-    def run(copies):
-        for copy in copies:
-            copy.start()
-        for copy in copies:
-            copy.wait()
 
     @pl.when(pos_ref[0] == 0)
     def _():
@@ -329,11 +383,10 @@
         [(chunk_shape, bf16), token],
         [ANY],
         [pltpu.SemaphoreType.DMA((2,))],
-        out_specs=[ANY, VMEM],
         vmem=52,
     )(own)
     far0 = lax.ppermute(chunk0, "rows", far_route)
-    kept_self, given_self, my_energy = call(
+    kept_self, given_self, message = call(
         "self",
         self_kernel,
         [(half_shape, f32), (half_shape, bf16), ((8, TS), f32)],
@@ -341,36 +394,50 @@
         [pltpu.VMEM((2, 2, HALF, TS), f32), pltpu.VMEM((TS, 128), f32)],
         after=after,
     )(pos, band_tiles, own)
-    other_energy = lax.ppermute(my_energy, "freq", swap)
     got_self = lax.ppermute(given_self, "freq", swap)
-    message, chunk1 = call(
-        "message",
-        message_kernel,
-        [((8, TS), f32), (chunk_shape, bf16)],
-        [VMEM] * 3,
+    near_message = lax.ppermute(message, "rows", pair)
+    far_message = lax.ppermute(near_message, "rows", across_route)
+    chunk1 = call(
+        "second",
+        second_kernel,
+        [(chunk_shape, bf16)],
+        [VMEM],
         [pltpu.SemaphoreType.DMA((2,))],
-        flops=MCOST,
-    )(own, my_energy, other_energy)
+        after=given_self,
+    )(own)
     far1 = lax.ppermute(chunk1, "rows", far_route)
     near = lax.ppermute(own, "rows", pair)
     far = (far0, far1)
-    near_message = lax.ppermute(message, "rows", pair)
-    far_message = lax.ppermute(near_message, "rows", across_route)
 
     unit_shape = (2, 2, 2, CR, HALF)
     after = call("order", order_kernel, [token], [ANY], flops=TCOST)(far0)
-    out, products = None, []
+    products = []
     for j in range(CHUNKS):
         kept, given = call(
             f"pair{j}",
             lambda *refs, j=j: pair_kernel(j, *refs),
-            [(unit_shape, f32), (unit_shape, bf16)],
+            [(unit_shape, f32), (((TILES * CR + (32 if j == 0 else 0)), HALF), bf16)],
             [SMEM] * 4 + [VMEM] * 6,
             [pltpu.VMEM((TS, 128), f32)],
             flops=PCOST,
             after=after,
         )(pos, message, near_message, far_message, own, near, far[j], message, near_message, far_message)
         got = lax.ppermute(given, "freq", swap)
+        if j == 0:
+            after = call(
+                "order1", order_kernel, [token], [ANY], flops=FCOST, after=kept
+            )(got_self)
+        products.append((kept, got))
+    for j, (kept, got) in enumerate(products):
+        fin = call(
+            f"decode{j}",
+            lambda *refs, j=j: pair_finish_kernel(j, *refs),
+            [(unit_shape, bf16)],
+            [SMEM] + [VMEM] * 6,
+            [pltpu.VMEM((2, TS, 128), f32)],
+            after=after,
+        )(pos, kept, got, message, near_message, far_message, products[0][1])
+        back = lax.ppermute(fin, "rows", back_route)
         if j == 0:
             out, after = call(
                 "finish",
@@ -382,15 +449,9 @@
                     pltpu.VMEM((2, TS, 128), f32),
                     pltpu.SemaphoreType.DMA((2,)),
                 ],
-                flops=FCOST,
-                after=kept,
+                after=fin,
                 out_specs=[ANY, VMEM],
-            )(pos, kept_self, got_self, my_energy, other_energy)
-        products.append((kept, got))
-    for j, (kept, got) in enumerate(products):
-        fin = call("decode", pair_finish_kernel, [(unit_shape, bf16)], [VMEM, VMEM], after=after)(kept, got)
-        after = fin
-        back = lax.ppermute(fin, "rows", back_route)
+            )(pos, kept_self, got_self, message, products[0][1])
         out = call(
             f"place{j}",
             lambda *refs, j=j: place_kernel(j, *refs),

time: 108 us -> 76.8 us (0.71)
  the two profiles are of different devices: /device:TPU:391 before, /device:TPU:377 now
where the time goes in v4:
time: 76.8 us; the launch traced here: 76.4 us
  starting transfers between devices  28.1 us (37%)
  waiting for transfers between devices  25.2 us (33%)
  Pallas kernels  22.6 us (29%)
    pallas_call x8, Pallas kernels, call(): return run if after is None else lambda *args: run(after, *args)  17.4 us
    ppermute x2, waiting for transfers between devices, shards(): got = lax.ppermute(given, 'freq', swap)  11.7 us
    ppermute x2, waiting for transfers between devices, shards(): back = lax.ppermute(fin, 'rows', back_route)  9.81 us
    ppermute x1, starting transfers between devices, shards(): far1 = lax.ppermute(chunk1, 'rows', far_route)  6.23 us
    ppermute x2, starting transfers between devices, shards(): got = lax.ppermute(given, 'freq', swap)  5.28 us
    ppermute x2, starting transfers between devices, shards(): back = lax.ppermute(fin, 'rows', back_route)  4.02 us
    ppermute x1, waiting for transfers between devices, shards(): far_message = lax.ppermute(near_message, 'rows', across_route)  3.64 us
    ppermute x1, starting transfers between devices, shards(): got_self = lax.ppermute(given_self, 'freq', swap)  3.11 us
  transfers between devices with their start and end apart: 10, of which 5 were waited for; matrix products, arithmetic and copies ran while one was open for 0% of the time, Pallas kernels for 28%

profile of v4, /device:TPU:377, one launch (start us, length us, event | category | flops | bytes accessed | tf_op | source)
XLA Modules:
  0.0 76.4 jit_solution(2308696508878532886)
XLA Ops:
  0.0 0.0 copy-start
  0.0 0.0 copy-start.1
  0.0 2.7 %collective-permute-start.3 = (bf16[2,4,512,256]{3,2,1,0:T(8,128)(2,1)}, bf16[2,4,512,256]{3,2,1,0:T(8,128)(2,1)}, u32[]{:S(2)}, u32[]{:S(2)}) collective-permute-start(bf16[2,4,512,256]{3,2,1,0:T(8,128)(2,1)} %bitcast.3), channel_id=1, source_target_pairs={{0,4},{4,0},{8,12},{12,8},{16,20},{20,16},{24,28},{28,24},{32,36},... | collective-permute-start | bytes 6291464 | tf_op jit(solution)/shard_map/ppermute | solution.py:409
  2.7 2.2 %pack.1 = (bf16[2,4,2,128,256]{4,3,2,1,0:T(8,128)(2,1)}, f32[8,128]{1,0:T(8,128)S(1)}) custom-call(bf16[2,4,512,256]{3,2,1,0:T(8,128)(2,1)} %bitcast.4), custom_call_target="tpu_custom_call" | custom-call | bytes 2097152 | tf_op jit(solution)/shard_map/pack/pallas_call | solution.py:380
  4.9 2.3 %collective-permute-start = (bf16[2,4,2,128,256]{4,3,2,1,0:T(8,128)(2,1)}, bf16[2,4,2,128,256]{4,3,2,1,0:T(8,128)(2,1)S(1)}, u32[]{:S(2)}, u32[]{:S(2)}) collective-permute-start(bf16[2,4,2,128,256]{4,3,2,1,0:T(8,128)(2,1)} %get-tuple-element.16), channel_id=1, source_target_pairs={{8,0},{16,8},{24,16},{32,24},{40,32},{48,40},{56,48},{64,56},{72,6... | collective-permute-start | bytes 3145736 | tf_op jit(solution)/shard_map/ppermute | solution.py:388
  7.2 0.1 pad_add_fusion.refs_0_
  7.3 0.0 copy-done
  7.3 0.0 copy-done.1
  7.3 3.4 %self.1 = (f32[2,256,512]{2,1,0:T(8,128)S(1)}, bf16[2,256,512]{2,1,0:T(8,128)(2,1)S(1)}, f32[8,512]{1,0:T(8,128)S(1)}) custom-call(f32[8,128]{1,0:T(8,128)S(1)} %get-tuple-element.17._, s32[2]{0:T(128)S(1)} %pad_add_fusion.refs_0_, s32[1,4]{1,0:T(1,128)S(1)} %copy-done.1, bf16[2,4,512,256]{3,2,1,0:T(8,128)(2,1)S(1)} %bitcast.5), custom_call_target="tpu_custom_call" | custom-call | bytes 2097152 | tf_op jit(solution)/shard_map/self/pallas_call | solution.py:361
  10.8 3.1 %collective-permute-start.4 = (bf16[2,256,512]{2,1,0:T(8,128)(2,1)S(1)}, bf16[2,256,512]{2,1,0:T(8,128)(2,1)S(1)}, u32[]{:S(2)}, u32[]{:S(2)}) collective-permute-start(bf16[2,256,512]{2,1,0:T(8,128)(2,1)S(1)} %get-tuple-element.20._), channel_id=1, source_target_pairs={{0,1},{1,0},{2,3},{3,2},{4,5},{5,4},{6,7},{7,6},{8,9},{9,8},{10,11... | collective-permute-start | bytes 1572872 | tf_op jit(solution)/shard_map/ppermute | solution.py:397
  13.9 2.6 %collective-permute-start.1 = (f32[8,512]{1,0:T(8,128)S(1)}, f32[8,512]{1,0:T(8,128)S(1)}, u32[]{:S(2)}, u32[]{:S(2)}) collective-permute-start(f32[8,512]{1,0:T(8,128)S(1)} %get-tuple-element.18.refs_1_.refs_7_.refs_3_), channel_id=1, source_target_pairs={{0,4},{4,0},{8,12},{12,8},{16,20},{20,16},{24,28},{28,24},{32,36},... | collective-permute-start | bytes 49160 | tf_op jit(solution)/shard_map/ppermute | solution.py:398
  16.4 0.1 second.1
  16.6 6.2 %collective-permute-start.7 = (bf16[2,4,2,128,256]{4,3,2,1,0:T(8,128)(2,1)S(1)}, bf16[2,4,2,128,256]{4,3,2,1,0:T(8,128)(2,1)S(1)}, u32[]{:S(2)}, u32[]{:S(2)}) collective-permute-start(bf16[2,4,2,128,256]{4,3,2,1,0:T(8,128)(2,1)S(1)} %second.1), channel_id=1, source_target_pairs={{8,0},{16,8},{24,16},{32,24},{40,32},{48,40},{56,48},{64,56},{72,6... | collective-permute-start | bytes 3145736 | tf_op jit(solution)/shard_map/ppermute | solution.py:408
  22.8 0.0 collective-permute-done.1.refs_2_.refs_8_.refs_4_
  22.8 1.9 %collective-permute-start.2 = (f32[8,512]{1,0:T(8,128)S(1)}, f32[8,512]{1,0:T(8,128)S(1)}, u32[]{:S(2)}, u32[]{:S(2)}) collective-permute-start(f32[8,512]{1,0:T(8,128)S(1)} %collective-permute-done.1.refs_2_.refs_8_.refs_4_), channel_id=1, source_target_pairs={{12,0},{20,8},{28,16},{36,24},{44,32},{52,40},{60,48},{68,56},{76,... | collective-permute-start | bytes 49160 | tf_op jit(solution)/shard_map/ppermute | solution.py:399
  24.7 0.0 collective-permute-done.refs_0_.refs_6_
  24.7 3.6 %collective-permute-done.2.refs_3_.refs_9_.refs_5_ = f32[8,512]{1,0:T(8,128)S(1)} collective-permute-done((f32[8,512]{1,0:T(8,128)S(1)}, f32[8,512]{1,0:T(8,128)S(1)}, u32[]{:S(2)}, u32[]{:S(2)}) %collective-permute-start.2) | collective-permute-done | bytes 16416 | tf_op jit(solution)/shard_map/ppermute | solution.py:399
  28.4 0.0 collective-permute-done.3.refs_5_
  28.4 4.3 %pair0.1 = (f32[2,2,2,128,256]{4,3,2,1,0:T(8,128)S(1)}, bf16[1056,256]{1,0:T(8,128)(2,1)S(1)}) custom-call(f32[8,128]{1,0:T(8,128)S(1)} %order.1._, s32[2]{0:T(128)S(1)} %pad_add_fusion.refs_0_, f32[8,512]{1,0:T(8,128)S(1)} %get-tuple-element.18.refs_1_.refs_7_.refs_3_, f32[8,512]{1,0:T(8,128)S(1)} %collective-permute-done.1.refs_2_.refs_8_.refs_4_, ...), custom_call_target="tpu_custom_call" | custom-call | bytes 2097152 | tf_op jit(solution)/shard_map/pair0/pallas_call | solution.py:361
  32.7 2.2 %collective-permute-start.5 = (bf16[1056,256]{1,0:T(8,128)(2,1)S(1)}, bf16[1056,256]{1,0:T(8,128)(2,1)S(1)}, u32[]{:S(2)}, u32[]{:S(2)}) collective-permute-start(bf16[1056,256]{1,0:T(8,128)(2,1)S(1)} %get-tuple-element.21), channel_id=1, source_target_pairs={{0,1},{1,0},{2,3},{3,2},{4,5},{5,4},{6,7},{7,6},{8,9},{9,8},{10,11... | collective-permute-start | bytes 1622024 | tf_op jit(solution)/shard_map/ppermute | solution.py:425
  34.9 0.0 collective-permute-done.4.refs_0_.refs_2_
  34.9 0.0 collective-permute-done.7.refs_6_
  34.9 4.3 %pair1.1 = (f32[2,2,2,128,256]{4,3,2,1,0:T(8,128)S(1)}, bf16[1024,256]{1,0:T(8,128)(2,1)S(1)}) custom-call(f32[8,128]{1,0:T(8,128)S(1)} %order1.1._, s32[2]{0:T(128)S(1)} %pad_add_fusion.refs_0_, f32[8,512]{1,0:T(8,128)S(1)} %get-tuple-element.18.refs_1_.refs_7_.refs_3_, f32[8,512]{1,0:T(8,128)S(1)} %collective-permute-done.1.refs_2_.refs_8_.refs_4_, ...), custom_call_target="tpu_custom_call" | custom-call | bytes 2097152 | tf_op jit(solution)/shard_map/pair1/pallas_call | solution.py:361
  39.2 3.1 %collective-permute-start.8 = (bf16[1024,256]{1,0:T(8,128)(2,1)S(1)}, bf16[1024,256]{1,0:T(8,128)(2,1)S(1)}, u32[]{:S(2)}, u32[]{:S(2)}) collective-permute-start(bf16[1024,256]{1,0:T(8,128)(2,1)S(1)} %get-tuple-element.26), channel_id=1, source_target_pairs={{0,1},{1,0},{2,3},{3,2},{4,5},{5,4},{6,7},{7,6},{8,9},{9,8},{10,11... | collective-permute-start | bytes 1572872 | tf_op jit(solution)/shard_map/ppermute | solution.py:425
  42.3 6.4 %collective-permute-done.5.refs_2_.refs_6_.refs_4_ = bf16[1056,256]{1,0:T(8,128)(2,1)S(1)} collective-permute-done((bf16[1056,256]{1,0:T(8,128)(2,1)S(1)}, bf16[1056,256]{1,0:T(8,128)(2,1)S(1)}, u32[]{:S(2)}, u32[]{:S(2)}) %collective-permute-start.5) | collective-permute-done | bytes 540704 | tf_op jit(solution)/shard_map/ppermute | solution.py:425
  48.7 1.5 %decode0.1._.refs_2_ = bf16[2,2,2,128,256]{4,3,2,1,0:T(8,128)(2,1)S(1)} custom-call(f32[8,128]{1,0:T(8,128)S(1)} %order1.1._, s32[2]{0:T(128)S(1)} %pad_add_fusion.refs_0_, f32[2,2,2,128,256]{4,3,2,1,0:T(8,128)S(1)} %get-tuple-element.19._.refs_1_, bf16[1056,256]{1,0:T(8,128)(2,1)S(1)} %collective-permute-done.5.refs_2_.refs_6_.refs_4_, ...), custom_call_target="tpu_custom_call" | custom-call | bytes 2097152 | tf_op jit(solution)/shard_map/decode0/pallas_call | solution.py:361
  50.2 2.1 %collective-permute-start.6 = (bf16[2,2,2,128,256]{4,3,2,1,0:T(8,128)(2,1)S(1)}, bf16[2,2,2,128,256]{4,3,2,1,0:T(8,128)(2,1)S(1)}, u32[]{:S(2)}, u32[]{:S(2)}) collective-permute-start(bf16[2,2,2,128,256]{4,3,2,1,0:T(8,128)(2,1)S(1)} %decode0.1._.refs_2_), channel_id=1, source_target_pairs={{12,4},{20,12},{28,20},{36,28},{44,36},{52,44},{60,52},{68,60},{76... | collective-permute-start | bytes 1572872 | tf_op jit(solution)/shard_map/ppermute | solution.py:440
  52.3 2.2 %finish.1 = (bf16[2,1,3,256,512]{4,3,2,1,0:T(8,128)(2,1)}, f32[8,128]{1,0:T(8,128)S(1)}) custom-call(bf16[2,2,2,128,256]{4,3,2,1,0:T(8,128)(2,1)S(1)} %decode0.1._.refs_2_, s32[2]{0:T(128)S(1)} %pad_add_fusion.refs_0_, f32[2,256,512]{2,1,0:T(8,128)S(1)} %get-tuple-element.22.refs_1_, bf16[2,256,512]{2,1,0:T(8,128)(2,1)S(1)} %collective-permute-done.4.refs_0_.refs_2_, ...), custom_call_target="tpu_custom_call" | custom-call | bytes 2097152 | tf_op jit(solution)/shard_map/finish/pallas_call | solution.py:361
  54.6 5.4 %collective-permute-done.8.refs_2_ = bf16[1024,256]{1,0:T(8,128)(2,1)S(1)} collective-permute-done((bf16[1024,256]{1,0:T(8,128)(2,1)S(1)}, bf16[1024,256]{1,0:T(8,128)(2,1)S(1)}, u32[]{:S(2)}, u32[]{:S(2)}) %collective-permute-start.8) | collective-permute-done | bytes 524320 | tf_op jit(solution)/shard_map/ppermute | solution.py:425
  59.9 1.5 %decode1.1.refs_2_ = bf16[2,2,2,128,256]{4,3,2,1,0:T(8,128)(2,1)S(1)} custom-call(f32[8,128]{1,0:T(8,128)S(1)} %get-tuple-element.24._, s32[2]{0:T(128)S(1)} %pad_add_fusion.refs_0_, f32[2,2,2,128,256]{4,3,2,1,0:T(8,128)S(1)} %get-tuple-element.25.refs_1_, bf16[1024,256]{1,0:T(8,128)(2,1)S(1)} %collective-permute-done.8.refs_2_, ...), custom_call_target="tpu_custom_call" | custom-call | bytes 2097152 | tf_op jit(solution)/shard_map/decode1/pallas_call | solution.py:361
  61.4 1.9 %collective-permute-start.9 = (bf16[2,2,2,128,256]{4,3,2,1,0:T(8,128)(2,1)S(1)}, bf16[2,2,2,128,256]{4,3,2,1,0:T(8,128)(2,1)S(1)}, u32[]{:S(2)}, u32[]{:S(2)}) collective-permute-start(bf16[2,2,2,128,256]{4,3,2,1,0:T(8,128)(2,1)S(1)} %decode1.1.refs_2_), channel_id=1, source_target_pairs={{12,4},{20,12},{28,20},{36,28},{44,36},{52,44},{60,52},{68,60},{76... | collective-permute-start | bytes 1572872 | tf_op jit(solution)/shard_map/ppermute | solution.py:440
  63.4 0.1 collective-permute-done.6.refs_3_
  63.5 1.5 %place0.1.refs_1_ = bf16[2,1,3,256,512]{4,3,2,1,0:T(8,128)(2,1)} custom-call(s32[2]{0:T(128)S(1)} %pad_add_fusion.refs_0_, bf16[2,1,3,256,512]{4,3,2,1,0:T(8,128)(2,1)} %get-tuple-element.23.refs_1_, bf16[2,2,2,128,256]{4,3,2,1,0:T(8,128)(2,1)S(1)} %decode0.1._.refs_2_, ...), custom_call_target="tpu_custom_call", output_to_operand_aliasing={{}: (1, {})} | custom-call | bytes 2097152 | tf_op jit(solution)/shard_map/place0/pallas_call | solution.py:455
  65.0 9.7 %collective-permute-done.9.refs_3_ = bf16[2,2,2,128,256]{4,3,2,1,0:T(8,128)(2,1)S(1)} collective-permute-done((bf16[2,2,2,128,256]{4,3,2,1,0:T(8,128)(2,1)S(1)}, bf16[2,2,2,128,256]{4,3,2,1,0:T(8,128)(2,1)S(1)}, u32[]{:S(2)}, u32[]{:S(2)}) %collective-permute-start.9) | collective-permute-done | bytes 524320 | tf_op jit(solution)/shard_map/ppermute | solution.py:440
  74.7 1.5 %place1.1 = bf16[2,1,3,256,512]{4,3,2,1,0:T(8,128)(2,1)} custom-call(s32[2]{0:T(128)S(1)} %pad_add_fusion.refs_0_, bf16[2,1,3,256,512]{4,3,2,1,0:T(8,128)(2,1)} %place0.1.refs_1_, bf16[2,2,2,128,256]{4,3,2,1,0:T(8,128)(2,1)S(1)} %decode1.1.refs_2_, bf16[2,2,2,128,256]{4,3,2,1,0:T(8,128)(2,1)S(1)} %collective-permute-done.9.refs_3_), custom_call_target="tpu_custom_call", output_to_operand_aliasing={{}: (1, {})} | custom-call | bytes 2097152 | tf_op jit(solution)/shard_map/place1/pallas_call | solution.py:455
  (2 shorter events, 0.0 us)
Async XLA Ops:
  0.0 7.3 %copy-start = (bf16[2,1,4,512,256]{4,3,2,1,0:T(8,128)(2,1)S(1)}, bf16[2,1,4,512,256]{4,3,2,1,0:T(8,128)(2,1)}, u32[]{:S(2)}) copy-start(bf16[2,1,4,512,256]{4,3,2,1,0:T(8,128)(2,1)} %param.2) | copy-start | bytes 6291460
  0.0 7.3 %copy-start.1 = (s32[1,4]{1,0:T(1,128)S(1)}, s32[1,4]{1,0:T(1,128)}, u32[]{:S(2)}) copy-start(s32[1,4]{1,0:T(1,128)} %refs_1_.1) | copy-start | bytes 52
  0.0 28.4 %collective-permute-start.3 = (bf16[2,4,512,256]{3,2,1,0:T(8,128)(2,1)}, bf16[2,4,512,256]{3,2,1,0:T(8,128)(2,1)}, u32[]{:S(2)}, u32[]{:S(2)}) collective-permute-start(bf16[2,4,512,256]{3,2,1,0:T(8,128)(2,1)} %bitcast.3), channel_id=1, source_target_pairs={{0,4},{4,0},{8,12},{12,8},{16,20},{20,16},{24,28},{28,24},{32,36},... | collective-permute-start | bytes 6291464 | tf_op jit(solution)/shard_map/ppermute | solution.py:409
  4.9 19.8 %collective-permute-start = (bf16[2,4,2,128,256]{4,3,2,1,0:T(8,128)(2,1)}, bf16[2,4,2,128,256]{4,3,2,1,0:T(8,128)(2,1)S(1)}, u32[]{:S(2)}, u32[]{:S(2)}) collective-permute-start(bf16[2,4,2,128,256]{4,3,2,1,0:T(8,128)(2,1)} %get-tuple-element.16), channel_id=1, source_target_pairs={{8,0},{16,8},{24,16},{32,24},{40,32},{48,40},{56,48},{64,56},{72,6... | collective-permute-start | bytes 3145736 | tf_op jit(solution)/shard_map/ppermute | solution.py:388
  10.8 24.1 %collective-permute-start.4 = (bf16[2,256,512]{2,1,0:T(8,128)(2,1)S(1)}, bf16[2,256,512]{2,1,0:T(8,128)(2,1)S(1)}, u32[]{:S(2)}, u32[]{:S(2)}) collective-permute-start(bf16[2,256,512]{2,1,0:T(8,128)(2,1)S(1)} %get-tuple-element.20._), channel_id=1, source_target_pairs={{0,1},{1,0},{2,3},{3,2},{4,5},{5,4},{6,7},{7,6},{8,9},{9,8},{10,11... | collective-permute-start | bytes 1572872 | tf_op jit(solution)/shard_map/ppermute | solution.py:397
  13.9 8.9 %collective-permute-start.1 = (f32[8,512]{1,0:T(8,128)S(1)}, f32[8,512]{1,0:T(8,128)S(1)}, u32[]{:S(2)}, u32[]{:S(2)}) collective-permute-start(f32[8,512]{1,0:T(8,128)S(1)} %get-tuple-element.18.refs_1_.refs_7_.refs_3_), channel_id=1, source_target_pairs={{0,4},{4,0},{8,12},{12,8},{16,20},{20,16},{24,28},{28,24},{32,36},... | collective-permute-start | bytes 49160 | tf_op jit(solution)/shard_map/ppermute | solution.py:398
  16.6 18.3 %collective-permute-start.7 = (bf16[2,4,2,128,256]{4,3,2,1,0:T(8,128)(2,1)S(1)}, bf16[2,4,2,128,256]{4,3,2,1,0:T(8,128)(2,1)S(1)}, u32[]{:S(2)}, u32[]{:S(2)}) collective-permute-start(bf16[2,4,2,128,256]{4,3,2,1,0:T(8,128)(2,1)S(1)} %second.1), channel_id=1, source_target_pairs={{8,0},{16,8},{24,16},{32,24},{40,32},{48,40},{56,48},{64,56},{72,6... | collective-permute-start | bytes 3145736 | tf_op jit(solution)/shard_map/ppermute | solution.py:408
  22.8 5.6 %collective-permute-start.2 = (f32[8,512]{1,0:T(8,128)S(1)}, f32[8,512]{1,0:T(8,128)S(1)}, u32[]{:S(2)}, u32[]{:S(2)}) collective-permute-start(f32[8,512]{1,0:T(8,128)S(1)} %collective-permute-done.1.refs_2_.refs_8_.refs_4_), channel_id=1, source_target_pairs={{12,0},{20,8},{28,16},{36,24},{44,32},{52,40},{60,48},{68,56},{76,... | collective-permute-start | bytes 49160 | tf_op jit(solution)/shard_map/ppermute | solution.py:399
  32.7 16.0 %collective-permute-start.5 = (bf16[1056,256]{1,0:T(8,128)(2,1)S(1)}, bf16[1056,256]{1,0:T(8,128)(2,1)S(1)}, u32[]{:S(2)}, u32[]{:S(2)}) collective-permute-start(bf16[1056,256]{1,0:T(8,128)(2,1)S(1)} %get-tuple-element.21), channel_id=1, source_target_pairs={{0,1},{1,0},{2,3},{3,2},{4,5},{5,4},{6,7},{7,6},{8,9},{9,8},{10,11... | collective-permute-start | bytes 1622024 | tf_op jit(solution)/shard_map/ppermute | solution.py:425
  39.2 20.7 %collective-permute-start.8 = (bf16[1024,256]{1,0:T(8,128)(2,1)S(1)}, bf16[1024,256]{1,0:T(8,128)(2,1)S(1)}, u32[]{:S(2)}, u32[]{:S(2)}) collective-permute-start(bf16[1024,256]{1,0:T(8,128)(2,1)S(1)} %get-tuple-element.26), channel_id=1, source_target_pairs={{0,1},{1,0},{2,3},{3,2},{4,5},{5,4},{6,7},{7,6},{8,9},{9,8},{10,11... | collective-permute-start | bytes 1572872 | tf_op jit(solution)/shard_map/ppermute | solution.py:425
  50.2 13.2 %collective-permute-start.6 = (bf16[2,2,2,128,256]{4,3,2,1,0:T(8,128)(2,1)S(1)}, bf16[2,2,2,128,256]{4,3,2,1,0:T(8,128)(2,1)S(1)}, u32[]{:S(2)}, u32[]{:S(2)}) collective-permute-start(bf16[2,2,2,128,256]{4,3,2,1,0:T(8,128)(2,1)S(1)} %decode0.1._.refs_2_), channel_id=1, source_target_pairs={{12,4},{20,12},{28,20},{36,28},{44,36},{52,44},{60,52},{68,60},{76... | collective-permute-start | bytes 1572872 | tf_op jit(solution)/shard_map/ppermute | solution.py:440
  61.4 13.2 %collective-permute-start.9 = (bf16[2,2,2,128,256]{4,3,2,1,0:T(8,128)(2,1)S(1)}, bf16[2,2,2,128,256]{4,3,2,1,0:T(8,128)(2,1)S(1)}, u32[]{:S(2)}, u32[]{:S(2)}) collective-permute-start(bf16[2,2,2,128,256]{4,3,2,1,0:T(8,128)(2,1)S(1)} %decode1.1.refs_2_), channel_id=1, source_target_pairs={{12,4},{20,12},{28,20},{36,28},{44,36},{52,44},{60,52},{68,60},{76... | collective-permute-start | bytes 1572872 | tf_op jit(solution)/shard_map/ppermute | solution.py:440

commit v5 on v4

--- a/solution.py
+++ b/solution.py
@@ -11,6 +11,7 @@
 CHUNKS = 2
 CR = HALF // CHUNKS
 TILES = 8
+ROWS = 2 * BAND * 2 * CR
 EPSILON = 1e-06
 TINY = 1e-30
 CODE = 2.0**7.5
@@ -50,7 +51,7 @@
 
 def put_energies(messages, given_ref):
     for i, message in enumerate(messages):
-        rest = message[0:1, :]
+        rest = message
         for level in range(3):
             term = rest.astype(jnp.bfloat16)
             rest = rest - term.astype(jnp.float32)
@@ -86,15 +87,8 @@
     return with_re[:rows] + with_im[rows:], with_re[rows:] - with_im[:rows]
 
 
-def chunk_copies(j, own_ref, chunk_ref, sem):
-    return [
-        pltpu.make_async_copy(
-            own_ref.at[:, :, pl.ds(half * HALF + j * CR, CR), :],
-            chunk_ref.at[:, :, half],
-            sem.at[half],
-        )
-        for half in range(2)
-    ]
+def live_before(band_ref, tile):
+    return sum((band_ref[0, d] < tile).astype(jnp.int32) for d in range(BAND))
 
 
 def run(copies):
@@ -104,9 +98,30 @@
         copy.wait()
 
 
-def pack_kernel(own_ref, chunk0_ref, token_ref, sem):
+def pack_kernel(pos_ref, tiles_ref, own_ref, chunk0_ref, token_ref, shift_ref, band_ref, sem):
+    bands = pltpu.make_async_copy(tiles_ref, band_ref, sem.at[17])
+    bands.start()
+    copies = [
+        pltpu.make_async_copy(
+            own_ref.at[part, d, pl.ds(half * HALF, CR), :],
+            chunk0_ref.at[pl.ds(((part * BAND + d) * 2 + half) * CR, CR), :],
+            sem.at[(part * BAND + d) * 2 + half],
+        )
+        for part in range(2)
+        for d in range(BAND)
+        for half in range(2)
+    ]
+    for copy in copies:
+        copy.start()
     token_ref[...] = jnp.zeros_like(token_ref)
-    run(chunk_copies(0, own_ref, chunk0_ref, sem))
+    shift_ref[...] = jnp.zeros_like(shift_ref)
+    bands.wait()
+    for offset in (1, 2):
+        count = live_before(band_ref, pos_ref[2] + offset).astype(jnp.float32)
+        shift_ref[offset : offset + 1, :] = jnp.full((1, HALF), count).astype(jnp.bfloat16)
+    run([pltpu.make_async_copy(shift_ref, chunk0_ref.at[pl.ds(ROWS, 16), :], sem.at[16])])
+    for copy in copies:
+        copy.wait()
 
 
 def order_kernel(*refs):
@@ -115,14 +130,23 @@
 
 
 def second_kernel(own_ref, chunk1_ref, sem):
-    run(chunk_copies(1, own_ref, chunk1_ref, sem))
-
-
-def self_kernel(pos_ref, band_ref, own_ref, kept_ref, given_ref, msg_ref, product_ref, col_ref):
+    run(
+        [
+            pltpu.make_async_copy(
+                own_ref.at[part, d, pl.ds(half * HALF + CR, CR), :],
+                chunk1_ref.at[pl.ds(((part * BAND + d) * 2 + half) * CR, CR), :],
+                sem.at[(part * BAND + d) * 2 + half],
+            )
+            for part in range(2)
+            for d in range(BAND)
+            for half in range(2)
+        ]
+    )
+
+
+def self_kernel(pos_ref, own_ref, kept_ref, given_ref, msg_ref, product_ref, col_ref):
     mine = pos_ref[1]
     msg_ref[...] = jnp.zeros_like(msg_ref)
-    for d in range(BAND):
-        msg_ref[1 + d : 2 + d, :] = jnp.full((1, TS), band_ref[0, d].astype(jnp.float32))
     right_re = jnp.concatenate([own_ref[0, d] for d in range(BAND)], axis=1)
     right_im = jnp.concatenate([own_ref[1, d] for d in range(BAND)], axis=1)
     diagonal = lax.broadcasted_iota(jnp.int32, (HALF, HALF), 0) == lax.broadcasted_iota(
@@ -156,19 +180,49 @@
         kept_ref[part] = product_ref[mine, part]
 
 
+def row_energies(load, blocks):
+    rows = []
+    for block in range(blocks):
+        total = jnp.zeros((CR, HALF), jnp.float32)
+        for part in range(2):
+            for d in range(BAND):
+                wide = load(part, d, block).astype(jnp.float32)
+                total += wide * wide
+        folded = jnp.transpose(total[:, :128] + total[:, 128:])
+        rows.append(jnp.sum(folded, axis=0, keepdims=True))
+    return jnp.concatenate(rows, axis=1)
+
+
 def pair_kernel(
-    j, pos_ref, own_s, near_s, far_s, own_ref, near_ref, far_ref, own_m, near_m, far_m,
-    kept_ref, given_ref, col_ref,
+    j, pos_ref, band_ref, own_ref, near_ref, far_ref, shift_ref, own_m, *rest
 ):
+    if j == 0:
+        kept_ref, given_ref, pair_m, col_ref = rest
+    else:
+        first_m, kept_ref, given_ref, pair_m, col_ref = rest
     core = pos_ref[0]
     mine = pos_ref[1]
+
+    def far_block(part, k, half):
+        start = pl.multiple_of(((part * BAND + k) * 2 + half) * CR, CR)
+        return far_ref[pl.ds(start, CR), :]
+
+    def far_chunk(part, k):
+        start = pl.multiple_of((part * BAND + k) * 2 * CR, 2 * CR)
+        return far_ref[pl.ds(start, 2 * CR), :]
+
+    pair_m[...] = jnp.zeros_like(pair_m)
     if j == 0:
-        given_ref[TILES * CR :, :] = jnp.zeros((32, HALF), jnp.bfloat16)
-        put_energies((own_m, near_m, far_m), given_ref)
-
-    def shift(left_s, right_s):
-        first = right_s[1, 0]
-        return sum((left_s[1 + d, 0] < first).astype(jnp.int32) for d in range(BAND))
+        pair_m[0:1, :] = row_energies(
+            lambda part, d, block: near_ref[part, d, block * CR : block * CR + CR, :], TS // CR
+        )
+    else:
+        pair_m[0:1, :] = first_m[0:1, :]
+    pair_m[1:2, : 2 * CR] = row_energies(far_block, 2)
+    near_row = pair_m[0:1, :]
+    far_row = pair_m[1:2, : 2 * CR]
+    given_ref[TILES * CR :, :] = jnp.zeros((32, HALF), jnp.bfloat16)
+    put_energies((own_m[0:1, :], near_row, pair_m[1:2, :]), given_ref)
 
     def aligned(load, part, s):
         blocks = []
@@ -202,14 +256,14 @@
     def _():
         col_ref[...] = column(inverse(own_m[0:1, :]))
         units = (
-            (near_s, chunk_of_rows(near_ref), near_m),
-            (far_s, lambda part, k: far_ref[part, k].reshape(2 * CR, HALF), far_m),
-        )
-        for unit, (right_s, load, right_m) in enumerate(units):
-            s = shift(own_s, right_s)
+            (chunk_of_rows(near_ref), chunk_of_lanes(near_row, j)),
+            (far_chunk, far_row),
+        )
+        for unit, (load, energy) in enumerate(units):
+            s = live_before(band_ref, pos_ref[2] + 1 + unit)
             right_re = aligned(load, 0, s)
             right_im = aligned(load, 1, s)
-            row = inverse(chunk_of_lanes(right_m[0:1, :], j))
+            row = inverse(energy)
             for keep in (False, True):
                 start = pl.multiple_of((mine if keep else 1 - mine) * HALF, HALF)
                 left = jnp.concatenate(
@@ -226,25 +280,26 @@
 
     @pl.when(core == 1)
     def _():
-        col_ref[...] = column(inverse(far_m[0:1, :]))
-        units = ((near_s, near_ref, near_m), (own_s, own_ref, own_m))
-        for unit, (right_s, right_ref, right_m) in enumerate(units):
-            s = shift(far_s, right_s)
+        col_ref[: 2 * CR, :] = column(inverse(far_row))
+        shifts = shift_ref[ROWS:, :].astype(jnp.float32)
+        units = ((near_ref, near_row), (own_ref, own_m[0:1, :]))
+        for unit, (right_ref, energy) in enumerate(units):
+            s = jnp.max(shifts[unit + 1 : unit + 2, :]).astype(jnp.int32)
             load = lambda part, k: right_ref[part, k]
             right_re = aligned(load, 0, s)
             right_im = aligned(load, 1, s)
-            row = inverse(right_m[0:1, :])
+            row = inverse(energy)
             for keep in (False, True):
                 half = mine if keep else 1 - mine
                 left = jnp.concatenate(
                     [
-                        jnp.concatenate([far_ref[part, d, half] for d in range(BAND)], axis=1)
+                        jnp.concatenate([far_block(part, d, half) for d in range(BAND)], axis=1)
                         for part in range(2)
                     ],
                     axis=0,
                 )
                 real, imag = complex_product(left, right_re, right_im)
-                start = pl.multiple_of(half * HALF + j * CR, CR)
+                start = pl.multiple_of(half * CR, CR)
                 emit(unit, keep, real, imag, start, CR, row, lambda v, t: v[:, t * HALF : t * HALF + HALF])
 
 
@@ -273,13 +328,11 @@
         copy.wait()
 
 
-def pair_finish_kernel(
-    j, pos_ref, kept_ref, got_ref, own_m, near_m, far_m, first_ref, fin_ref, col_ref
-):
+def pair_finish_kernel(j, pos_ref, kept_ref, got_ref, own_m, pair_m, fin_ref, col_ref):
     core = pos_ref[0]
     mine = pos_ref[1]
-    other = [get_energy(first_ref, i) for i in range(3)]
-    total = [m[0:1, :] + o for m, o in zip((own_m, near_m, far_m), other)]
+    other = [get_energy(got_ref, i) for i in range(3)]
+    total = [m + o for m, o in zip((own_m[0:1, :], pair_m[0:1, :], pair_m[1:2, :]), other)]
     root = [jnp.sqrt(jnp.maximum(o, TINY)) for o in other]
 
     def emit(unit, tile, start, root_row, total_row):
@@ -293,16 +346,16 @@
     def _():
         col_ref[0] = column(root[0])
         col_ref[1] = column(total[0])
-        for unit, i in enumerate((1, 2)):
-            for tile in range(2):
-                start = pl.multiple_of(mine * HALF + tile * CR, CR)
-                emit(unit, tile, start, chunk_of_lanes(root[i], j), chunk_of_lanes(total[i], j))
+        for tile in range(2):
+            start = pl.multiple_of(mine * HALF + tile * CR, CR)
+            emit(0, tile, start, chunk_of_lanes(root[1], j), chunk_of_lanes(total[1], j))
+            emit(1, tile, start, root[2][:, : 2 * CR], total[2][:, : 2 * CR])
 
     @pl.when(core == 1)
     def _():
         col_ref[0] = column(root[2])
         col_ref[1] = column(total[2])
-        start = pl.multiple_of(mine * HALF + j * CR, CR)
+        start = pl.multiple_of(mine * CR, CR)
         for unit, i in enumerate((1, 0)):
             for tile in range(2):
                 lanes = slice(tile * HALF, tile * HALF + HALF)
@@ -366,43 +419,39 @@
     count = lax.axis_size("rows")
     core = lax.axis_index("rows") % 2
     mine = lax.axis_index("freq") % 2
-    pos = jnp.stack([core, mine]).astype(jnp.int32)
+    pos = jnp.stack([core, mine, lax.axis_index("rows")]).astype(jnp.int32)
     own = correlation.reshape(2, BAND, TS, HALF)
     swap = [(i, i ^ 1) for i in range(lax.axis_size("freq"))]
     pair = [(i, i ^ 1) for i in range(count)]
     far_route = [(i + 2, i) for i in range(0, count - 2, 2)] + [(i - 2, i) for i in range(3, count, 2)]
-    across_route = [(i + 3, i) for i in range(0, count - 2, 2)] + [(i - 3, i) for i in range(3, count, 2)]
     back_route = [(i, i - 2) for i in range(3, count, 2)]
 
-    chunk_shape = (2, BAND, 2, CR, HALF)
     half_shape = (2, HALF, TS)
     token = ((8, 128), f32)
     chunk0, after = call(
         "pack",
         pack_kernel,
-        [(chunk_shape, bf16), token],
-        [ANY],
-        [pltpu.SemaphoreType.DMA((2,))],
+        [((ROWS + 16, HALF), bf16), token],
+        [SMEM, ANY, ANY],
+        [pltpu.VMEM((16, HALF), bf16), pltpu.SMEM((1, BAND), jnp.int32), pltpu.SemaphoreType.DMA((18,))],
         vmem=52,
-    )(own)
+    )(pos, band_tiles, own)
     far0 = lax.ppermute(chunk0, "rows", far_route)
     kept_self, given_self, message = call(
         "self",
         self_kernel,
         [(half_shape, f32), (half_shape, bf16), ((8, TS), f32)],
-        [SMEM, SMEM, VMEM],
+        [SMEM, VMEM],
         [pltpu.VMEM((2, 2, HALF, TS), f32), pltpu.VMEM((TS, 128), f32)],
         after=after,
-    )(pos, band_tiles, own)
+    )(pos, own)
     got_self = lax.ppermute(given_self, "freq", swap)
-    near_message = lax.ppermute(message, "rows", pair)
-    far_message = lax.ppermute(near_message, "rows", across_route)
     chunk1 = call(
         "second",
         second_kernel,
-        [(chunk_shape, bf16)],
+        [((ROWS, HALF), bf16)],
         [VMEM],
-        [pltpu.SemaphoreType.DMA((2,))],
+        [pltpu.SemaphoreType.DMA((16,))],
         after=given_self,
     )(own)
     far1 = lax.ppermute(chunk1, "rows", far_route)
@@ -411,17 +460,18 @@
 
     unit_shape = (2, 2, 2, CR, HALF)
     after = call("order", order_kernel, [token], [ANY], flops=TCOST)(far0)
-    products = []
+    products, pairs = [], []
     for j in range(CHUNKS):
-        kept, given = call(
+        kept, given, pair_m = call(
             f"pair{j}",
             lambda *refs, j=j: pair_kernel(j, *refs),
-            [(unit_shape, f32), (((TILES * CR + (32 if j == 0 else 0)), HALF), bf16)],
-            [SMEM] * 4 + [VMEM] * 6,
+            [(unit_shape, f32), ((TILES * CR + 32, HALF), bf16), ((8, TS), f32)],
+            [SMEM, SMEM] + [VMEM] * (5 + j),
             [pltpu.VMEM((TS, 128), f32)],
             flops=PCOST,
             after=after,
-        )(pos, message, near_message, far_message, own, near, far[j], message, near_message, far_message)
+        )(pos, band_tiles, own, near, far[j], far0, message, *pairs)
+        pairs.append(pair_m)
         got = lax.ppermute(given, "freq", swap)
         if j == 0:
             after = call(
@@ -433,10 +483,10 @@
             f"decode{j}",
             lambda *refs, j=j: pair_finish_kernel(j, *refs),
             [(unit_shape, bf16)],
-            [SMEM] + [VMEM] * 6,
+            [SMEM] + [VMEM] * 4,
             [pltpu.VMEM((2, TS, 128), f32)],
             after=after,
-        )(pos, kept, got, message, near_message, far_message, products[0][1])
+        )(pos, kept, got, message, pairs[j])
         back = lax.ppermute(fin, "rows", back_route)
         if j == 0:
             out, after = call(

time: 76.8 us -> 71.1 us (0.926)
  the two profiles are of different devices: /device:TPU:377 before, /device:TPU:1 now
where the time goes in v5:
time: 71.1 us; the launch traced here: 70.7 us
  Pallas kernels  24.9 us (35%)
  waiting for transfers between devices  24.7 us (35%)
  starting transfers between devices  20 us (28%)
    pallas_call x8, Pallas kernels, call(): return run if after is None else lambda *args: run(after, *args)  20 us
    ppermute x2, waiting for transfers between devices, shards(): back = lax.ppermute(fin, 'rows', back_route)  10.4 us
    ppermute x1, starting transfers between devices, shards(): near = lax.ppermute(own, 'rows', pair)  8.91 us
    ppermute x2, waiting for transfers between devices, shards(): got = lax.ppermute(given, 'freq', swap)  6.51 us
    ppermute x1, waiting for transfers between devices, shards(): far1 = lax.ppermute(chunk1, 'rows', far_route)  4.01 us
    ppermute x2, starting transfers between devices, shards(): got = lax.ppermute(given, 'freq', swap)  3.84 us
    ppermute x1, waiting for transfers between devices, shards(): far0 = lax.ppermute(chunk0, 'rows', far_route)  3.48 us
    pallas_call x2, Pallas kernels, shards(): call(f'place{j}', lambda *refs, j=j: place_kernel(j, *refs), [((2, 1, 3,...  3 us
  transfers between devices with their start and end apart: 8, of which 6 were waited for; matrix products, arithmetic and copies ran while one was open for 0% of the time, Pallas kernels for 33%

profile of v5, /device:TPU:1, one launch (start us, length us, event | category | flops | bytes accessed | tf_op | source)
XLA Modules:
  0.0 70.7 jit_solution(15340255503660094511)
XLA Ops:
  0.0 0.0 copy-start
  0.0 8.9 %collective-permute-start.1 = (bf16[2,4,512,256]{3,2,1,0:T(8,128)(2,1)}, bf16[2,4,512,256]{3,2,1,0:T(8,128)(2,1)}, u32[]{:S(2)}, u32[]{:S(2)}) collective-permute-start(bf16[2,4,512,256]{3,2,1,0:T(8,128)(2,1)} %bitcast.4), channel_id=1, source_target_pairs={{0,4},{4,0},{8,12},{12,8},{16,20},{20,16},{24,28},{28,24},{32,36},... | collective-permute-start | bytes 6291464 | tf_op jit(solution)/shard_map/ppermute | solution.py:458
  8.9 0.1 pad_add_fusion.pos_ref.refs_0_
  9.0 0.0 copy-start.1
  9.0 0.7 copy-done.1
  9.7 1.9 %pack.1 = (bf16[2064,256]{1,0:T(8,128)(2,1)S(1)}, f32[8,128]{1,0:T(8,128)S(1)}) custom-call(s32[3]{0:T(128)S(1)} %pad_add_fusion.pos_ref.refs_0_, s32[1,4]{1,0:T(1,128)S(1)} %copy-done.1, bf16[2,4,512,256]{3,2,1,0:T(8,128)(2,1)} %bitcast.5), custom_call_target="tpu_custom_call" | custom-call | bytes 2097152 | tf_op jit(solution)/shard_map/pack/pallas_call | solution.py:431
  11.6 1.4 %collective-permute-start = (bf16[2064,256]{1,0:T(8,128)(2,1)S(1)}, bf16[2064,256]{1,0:T(8,128)(2,1)S(1)}, u32[]{:S(2)}, u32[]{:S(2)}) collective-permute-start(bf16[2064,256]{1,0:T(8,128)(2,1)S(1)} %get-tuple-element.18), channel_id=1, source_target_pairs={{8,0},{16,8},{24,16},{32,24},{40,32},{48,40},{56,48},{64,56},{72,6... | collective-permute-start | bytes 3170312 | tf_op jit(solution)/shard_map/ppermute | solution.py:439
  13.0 0.0 copy-done
  13.0 3.4 %self.1 = (f32[2,256,512]{2,1,0:T(8,128)S(1)}, bf16[2,256,512]{2,1,0:T(8,128)(2,1)S(1)}, f32[8,512]{1,0:T(8,128)S(1)}) custom-call(f32[8,128]{1,0:T(8,128)S(1)} %get-tuple-element.19._, s32[3]{0:T(128)S(1)} %pad_add_fusion.pos_ref.refs_0_, bf16[2,4,512,256]{3,2,1,0:T(8,128)(2,1)S(1)} %bitcast.6), custom_call_target="tpu_custom_call" | custom-call | bytes 2097152 | tf_op jit(solution)/shard_map/self/pallas_call | solution.py:414
  16.4 1.9 %collective-permute-start.2 = (bf16[2,256,512]{2,1,0:T(8,128)(2,1)S(1)}, bf16[2,256,512]{2,1,0:T(8,128)(2,1)S(1)}, u32[]{:S(2)}, u32[]{:S(2)}) collective-permute-start(bf16[2,256,512]{2,1,0:T(8,128)(2,1)S(1)} %get-tuple-element.22._), channel_id=1, source_target_pairs={{0,1},{1,0},{2,3},{3,2},{4,5},{5,4},{6,7},{7,6},{8,9},{9,8},{10,11... | collective-permute-start | bytes 1572872 | tf_op jit(solution)/shard_map/ppermute | solution.py:448
  18.3 1.5 %second.1 = bf16[2048,256]{1,0:T(8,128)(2,1)S(1)} custom-call(bf16[2,256,512]{2,1,0:T(8,128)(2,1)S(1)} %get-tuple-element.22._, bf16[2,4,512,256]{3,2,1,0:T(8,128)(2,1)S(1)} %bitcast.7), custom_call_target="tpu_custom_call" | custom-call | bytes 2097152 | tf_op jit(solution)/shard_map/second/pallas_call | solution.py:414
  19.9 1.4 %collective-permute-start.5 = (bf16[2048,256]{1,0:T(8,128)(2,1)S(1)}, bf16[2048,256]{1,0:T(8,128)(2,1)S(1)}, u32[]{:S(2)}, u32[]{:S(2)}) collective-permute-start(bf16[2048,256]{1,0:T(8,128)(2,1)S(1)} %second.1), channel_id=1, source_target_pairs={{8,0},{16,8},{24,16},{32,24},{40,32},{48,40},{56,48},{64,56},{72,6... | collective-permute-start | bytes 3145736 | tf_op jit(solution)/shard_map/ppermute | solution.py:457
  21.2 3.5 %collective-permute-done.refs_0_.refs_4_.refs_5_ = bf16[2064,256]{1,0:T(8,128)(2,1)S(1)} collective-permute-done((bf16[2064,256]{1,0:T(8,128)(2,1)S(1)}, bf16[2064,256]{1,0:T(8,128)(2,1)S(1)}, u32[]{:S(2)}, u32[]{:S(2)}) %collective-permute-start) | collective-permute-done | bytes 1056800 | tf_op jit(solution)/shard_map/ppermute | solution.py:439
  24.7 0.0 collective-permute-done.1.refs_3_
  24.7 5.0 %pair0.1 = (f32[2,2,2,128,256]{4,3,2,1,0:T(8,128)S(1)}, bf16[1056,256]{1,0:T(8,128)(2,1)S(1)}, f32[8,512]{1,0:T(8,128)S(1)}) custom-call(f32[8,128]{1,0:T(8,128)S(1)} %order.1._, s32[3]{0:T(128)S(1)} %pad_add_fusion.pos_ref.refs_0_, s32[1,4]{1,0:T(1,128)S(1)} %copy-done.1, bf16[2,4,512,256]{3,2,1,0:T(8,128)(2,1)S(1)} %bitcast.8, ...), custom_call_target="tpu_custom_call" | custom-call | bytes 2097152 | tf_op jit(solution)/shard_map/pair0/pallas_call | solution.py:414
  29.7 1.9 %collective-permute-start.3 = (bf16[1056,256]{1,0:T(8,128)(2,1)S(1)}, bf16[1056,256]{1,0:T(8,128)(2,1)S(1)}, u32[]{:S(2)}, u32[]{:S(2)}) collective-permute-start(bf16[1056,256]{1,0:T(8,128)(2,1)S(1)} %get-tuple-element.23), channel_id=1, source_target_pairs={{0,1},{1,0},{2,3},{3,2},{4,5},{5,4},{6,7},{7,6},{8,9},{9,8},{10,11... | collective-permute-start | bytes 1622024 | tf_op jit(solution)/shard_map/ppermute | solution.py:475
  31.6 0.3 collective-permute-done.2.refs_0_.refs_2_
  31.9 4.0 %collective-permute-done.5.refs_4_ = bf16[2048,256]{1,0:T(8,128)(2,1)S(1)} collective-permute-done((bf16[2048,256]{1,0:T(8,128)(2,1)S(1)}, bf16[2048,256]{1,0:T(8,128)(2,1)S(1)}, u32[]{:S(2)}, u32[]{:S(2)}) %collective-permute-start.5) | collective-permute-done | bytes 1048608 | tf_op jit(solution)/shard_map/ppermute | solution.py:457
  36.0 4.6 %pair1.1 = (f32[2,2,2,128,256]{4,3,2,1,0:T(8,128)S(1)}, bf16[1056,256]{1,0:T(8,128)(2,1)S(1)}, f32[8,512]{1,0:T(8,128)S(1)}) custom-call(f32[8,128]{1,0:T(8,128)S(1)} %order1.1._, s32[3]{0:T(128)S(1)} %pad_add_fusion.pos_ref.refs_0_, s32[1,4]{1,0:T(1,128)S(1)} %copy-done.1, bf16[2,4,512,256]{3,2,1,0:T(8,128)(2,1)S(1)} %bitcast.9, ...), custom_call_target="tpu_custom_call" | custom-call | bytes 2097152 | tf_op jit(solution)/shard_map/pair1/pallas_call | solution.py:414
  40.6 1.9 %collective-permute-start.6 = (bf16[1056,256]{1,0:T(8,128)(2,1)S(1)}, bf16[1056,256]{1,0:T(8,128)(2,1)S(1)}, u32[]{:S(2)}, u32[]{:S(2)}) collective-permute-start(bf16[1056,256]{1,0:T(8,128)(2,1)S(1)} %get-tuple-element.29), channel_id=1, source_target_pairs={{0,1},{1,0},{2,3},{3,2},{4,5},{5,4},{6,7},{7,6},{8,9},{9,8},{10,11... | collective-permute-start | bytes 1622024 | tf_op jit(solution)/shard_map/ppermute | solution.py:475
  42.5 0.0 collective-permute-done.3.refs_2_.refs_4_
  42.5 1.7 %decode0.1._.refs_2_ = bf16[2,2,2,128,256]{4,3,2,1,0:T(8,128)(2,1)S(1)} custom-call(f32[8,128]{1,0:T(8,128)S(1)} %order1.1._, s32[3]{0:T(128)S(1)} %pad_add_fusion.pos_ref.refs_0_, f32[2,2,2,128,256]{4,3,2,1,0:T(8,128)S(1)} %get-tuple-element.21._.refs_1_, bf16[1056,256]{1,0:T(8,128)(2,1)S(1)} %collective-permute-done.3.refs_2_.refs_4_, ...), custom_call_target="tpu_custom_call" | custom-call | bytes 2097152 | tf_op jit(solution)/shard_map/decode0/pallas_call | solution.py:414
  44.2 1.3 %collective-permute-start.4 = (bf16[2,2,2,128,256]{4,3,2,1,0:T(8,128)(2,1)S(1)}, bf16[2,2,2,128,256]{4,3,2,1,0:T(8,128)(2,1)S(1)}, u32[]{:S(2)}, u32[]{:S(2)}) collective-permute-start(bf16[2,2,2,128,256]{4,3,2,1,0:T(8,128)(2,1)S(1)} %decode0.1._.refs_2_), channel_id=1, source_target_pairs={{12,4},{20,12},{28,20},{36,28},{44,36},{52,44},{60,52},{68,60},{76... | collective-permute-start | bytes 1572872 | tf_op jit(solution)/shard_map/ppermute | solution.py:490
  45.5 2.2 %finish.1 = (bf16[2,1,3,256,512]{4,3,2,1,0:T(8,128)(2,1)}, f32[8,128]{1,0:T(8,128)S(1)}) custom-call(bf16[2,2,2,128,256]{4,3,2,1,0:T(8,128)(2,1)S(1)} %decode0.1._.refs_2_, s32[3]{0:T(128)S(1)} %pad_add_fusion.pos_ref.refs_0_, f32[2,256,512]{2,1,0:T(8,128)S(1)} %get-tuple-element.25.refs_1_, bf16[2,256,512]{2,1,0:T(8,128)(2,1)S(1)} %collective-permute-done.2.refs_0_.refs_2_, ...), custom_call_target="tpu_custom_call" | custom-call | bytes 2097152 | tf_op jit(solution)/shard_map/finish/pallas_call | solution.py:414
  47.8 6.5 %collective-permute-done.6.refs_2_ = bf16[1056,256]{1,0:T(8,128)(2,1)S(1)} collective-permute-done((bf16[1056,256]{1,0:T(8,128)(2,1)S(1)}, bf16[1056,256]{1,0:T(8,128)(2,1)S(1)}, u32[]{:S(2)}, u32[]{:S(2)}) %collective-permute-start.6) | collective-permute-done | bytes 540704 | tf_op jit(solution)/shard_map/ppermute | solution.py:475
  54.3 1.5 %decode1.1.refs_2_ = bf16[2,2,2,128,256]{4,3,2,1,0:T(8,128)(2,1)S(1)} custom-call(f32[8,128]{1,0:T(8,128)S(1)} %get-tuple-element.27._, s32[3]{0:T(128)S(1)} %pad_add_fusion.pos_ref.refs_0_, f32[2,2,2,128,256]{4,3,2,1,0:T(8,128)S(1)} %get-tuple-element.28.refs_1_, bf16[1056,256]{1,0:T(8,128)(2,1)S(1)} %collective-permute-done.6.refs_2_, ...), custom_call_target="tpu_custom_call" | custom-call | bytes 2097152 | tf_op jit(solution)/shard_map/decode1/pallas_call | solution.py:414
  55.8 1.3 %collective-permute-start.7 = (bf16[2,2,2,128,256]{4,3,2,1,0:T(8,128)(2,1)S(1)}, bf16[2,2,2,128,256]{4,3,2,1,0:T(8,128)(2,1)S(1)}, u32[]{:S(2)}, u32[]{:S(2)}) collective-permute-start(bf16[2,2,2,128,256]{4,3,2,1,0:T(8,128)(2,1)S(1)} %decode1.1.refs_2_), channel_id=1, source_target_pairs={{12,4},{20,12},{28,20},{36,28},{44,36},{52,44},{60,52},{68,60},{76... | collective-permute-start | bytes 1572872 | tf_op jit(solution)/shard_map/ppermute | solution.py:490
  57.1 0.4 collective-permute-done.4.refs_3_
  57.5 1.5 %place0.1.refs_1_ = bf16[2,1,3,256,512]{4,3,2,1,0:T(8,128)(2,1)} custom-call(s32[3]{0:T(128)S(1)} %pad_add_fusion.pos_ref.refs_0_, bf16[2,1,3,256,512]{4,3,2,1,0:T(8,128)(2,1)} %get-tuple-element.26.refs_1_, bf16[2,2,2,128,256]{4,3,2,1,0:T(8,128)(2,1)S(1)} %decode0.1._.refs_2_, ...), custom_call_target="tpu_custom_call", output_to_operand_aliasing={{}: (1, {})} | custom-call | bytes 2097152 | tf_op jit(solution)/shard_map/place0/pallas_call | solution.py:505
  59.0 10.0 %collective-permute-done.7.refs_3_ = bf16[2,2,2,128,256]{4,3,2,1,0:T(8,128)(2,1)S(1)} collective-permute-done((bf16[2,2,2,128,256]{4,3,2,1,0:T(8,128)(2,1)S(1)}, bf16[2,2,2,128,256]{4,3,2,1,0:T(8,128)(2,1)S(1)}, u32[]{:S(2)}, u32[]{:S(2)}) %collective-permute-start.7) | collective-permute-done | bytes 524320 | tf_op jit(solution)/shard_map/ppermute | solution.py:490
  69.0 1.5 %place1.1 = bf16[2,1,3,256,512]{4,3,2,1,0:T(8,128)(2,1)} custom-call(s32[3]{0:T(128)S(1)} %pad_add_fusion.pos_ref.refs_0_, bf16[2,1,3,256,512]{4,3,2,1,0:T(8,128)(2,1)} %place0.1.refs_1_, bf16[2,2,2,128,256]{4,3,2,1,0:T(8,128)(2,1)S(1)} %decode1.1.refs_2_, bf16[2,2,2,128,256]{4,3,2,1,0:T(8,128)(2,1)S(1)} %collective-permute-done.7.refs_3_), custom_call_target="tpu_custom_call", output_to_operand_aliasing={{}: (1, {})} | custom-call | bytes 2097152 | tf_op jit(solution)/shard_map/place1/pallas_call | solution.py:505
  (2 shorter events, 0.0 us)
Async XLA Ops:
  0.0 13.0 %copy-start = (bf16[2,1,4,512,256]{4,3,2,1,0:T(8,128)(2,1)S(1)}, bf16[2,1,4,512,256]{4,3,2,1,0:T(8,128)(2,1)}, u32[]{:S(2)}) copy-start(bf16[2,1,4,512,256]{4,3,2,1,0:T(8,128)(2,1)} %param.2) | copy-start | bytes 6291460
  0.0 24.7 %collective-permute-start.1 = (bf16[2,4,512,256]{3,2,1,0:T(8,128)(2,1)}, bf16[2,4,512,256]{3,2,1,0:T(8,128)(2,1)}, u32[]{:S(2)}, u32[]{:S(2)}) collective-permute-start(bf16[2,4,512,256]{3,2,1,0:T(8,128)(2,1)} %bitcast.4), channel_id=1, source_target_pairs={{0,4},{4,0},{8,12},{12,8},{16,20},{20,16},{24,28},{28,24},{32,36},... | collective-permute-start | bytes 6291464 | tf_op jit(solution)/shard_map/ppermute | solution.py:458
  9.0 0.7 copy-start.1
  11.6 13.1 %collective-permute-start = (bf16[2064,256]{1,0:T(8,128)(2,1)S(1)}, bf16[2064,256]{1,0:T(8,128)(2,1)S(1)}, u32[]{:S(2)}, u32[]{:S(2)}) collective-permute-start(bf16[2064,256]{1,0:T(8,128)(2,1)S(1)} %get-tuple-element.18), channel_id=1, source_target_pairs={{8,0},{16,8},{24,16},{32,24},{40,32},{48,40},{56,48},{64,56},{72,6... | collective-permute-start | bytes 3170312 | tf_op jit(solution)/shard_map/ppermute | solution.py:439
  16.4 15.5 %collective-permute-start.2 = (bf16[2,256,512]{2,1,0:T(8,128)(2,1)S(1)}, bf16[2,256,512]{2,1,0:T(8,128)(2,1)S(1)}, u32[]{:S(2)}, u32[]{:S(2)}) collective-permute-start(bf16[2,256,512]{2,1,0:T(8,128)(2,1)S(1)} %get-tuple-element.22._), channel_id=1, source_target_pairs={{0,1},{1,0},{2,3},{3,2},{4,5},{5,4},{6,7},{7,6},{8,9},{9,8},{10,11... | collective-permute-start | bytes 1572872 | tf_op jit(solution)/shard_map/ppermute | solution.py:448
  19.9 16.1 %collective-permute-start.5 = (bf16[2048,256]{1,0:T(8,128)(2,1)S(1)}, bf16[2048,256]{1,0:T(8,128)(2,1)S(1)}, u32[]{:S(2)}, u32[]{:S(2)}) collective-permute-start(bf16[2048,256]{1,0:T(8,128)(2,1)S(1)} %second.1), channel_id=1, source_target_pairs={{8,0},{16,8},{24,16},{32,24},{40,32},{48,40},{56,48},{64,56},{72,6... | collective-permute-start | bytes 3145736 | tf_op jit(solution)/shard_map/ppermute | solution.py:457
  29.7 12.8 %collective-permute-start.3 = (bf16[1056,256]{1,0:T(8,128)(2,1)S(1)}, bf16[1056,256]{1,0:T(8,128)(2,1)S(1)}, u32[]{:S(2)}, u32[]{:S(2)}) collective-permute-start(bf16[1056,256]{1,0:T(8,128)(2,1)S(1)} %get-tuple-element.23), channel_id=1, source_target_pairs={{0,1},{1,0},{2,3},{3,2},{4,5},{5,4},{6,7},{7,6},{8,9},{9,8},{10,11... | collective-permute-start | bytes 1622024 | tf_op jit(solution)/shard_map/ppermute | solution.py:475
  40.6 13.7 %collective-permute-start.6 = (bf16[1056,256]{1,0:T(8,128)(2,1)S(1)}, bf16[1056,256]{1,0:T(8,128)(2,1)S(1)}, u32[]{:S(2)}, u32[]{:S(2)}) collective-permute-start(bf16[1056,256]{1,0:T(8,128)(2,1)S(1)} %get-tuple-element.29), channel_id=1, source_target_pairs={{0,1},{1,0},{2,3},{3,2},{4,5},{5,4},{6,7},{7,6},{8,9},{9,8},{10,11... | collective-permute-start | bytes 1622024 | tf_op jit(solution)/shard_map/ppermute | solution.py:475
  44.2 13.3 %collective-permute-start.4 = (bf16[2,2,2,128,256]{4,3,2,1,0:T(8,128)(2,1)S(1)}, bf16[2,2,2,128,256]{4,3,2,1,0:T(8,128)(2,1)S(1)}, u32[]{:S(2)}, u32[]{:S(2)}) collective-permute-start(bf16[2,2,2,128,256]{4,3,2,1,0:T(8,128)(2,1)S(1)} %decode0.1._.refs_2_), channel_id=1, source_target_pairs={{12,4},{20,12},{28,20},{36,28},{44,36},{52,44},{60,52},{68,60},{76... | collective-permute-start | bytes 1572872 | tf_op jit(solution)/shard_map/ppermute | solution.py:490
  55.8 13.2 %collective-permute-start.7 = (bf16[2,2,2,128,256]{4,3,2,1,0:T(8,128)(2,1)S(1)}, bf16[2,2,2,128,256]{4,3,2,1,0:T(8,128)(2,1)S(1)}, u32[]{:S(2)}, u32[]{:S(2)}) collective-permute-start(bf16[2,2,2,128,256]{4,3,2,1,0:T(8,128)(2,1)S(1)} %decode1.1.refs_2_), channel_id=1, source_target_pairs={{12,4},{20,12},{28,20},{36,28},{44,36},{52,44},{60,52},{68,60},{76... | collective-permute-start | bytes 1572872 | tf_op jit(solution)/shard_map/ppermute | solution.py:490

commit v6 on v5

v6 whole, which is shorter than its diff:
```python
import jax
import jax.numpy as jnp
from jax import lax
from jax.experimental import pallas as pl
from jax.experimental.pallas import tpu as pltpu
from jax.sharding import PartitionSpec as P

TS = 512
HALF = 256
BAND = 4
CHUNKS = 2
CR = HALF // CHUNKS
TILES = 4
ROWS = 2 * BAND * 2 * CR
EPSILON = 1e-06
TINY = 1e-30
CODE = 2.0**7.5
VMEM = pl.BlockSpec(memory_space=pltpu.VMEM)
ANY = pl.BlockSpec(memory_space=pl.ANY)
SMEM = pl.BlockSpec(memory_space=pltpu.SMEM)
MIB = 1024 * 1024
PCOST = 0
TCOST = 2**32
FCOST = 2**35


def encode(x):
    u = x * CODE
    y = u * u
    y = y * y
    y = y * y
    y = y * y
    return jnp.where(u < 0, -y, y).astype(jnp.bfloat16)


def decode(y):
    y = y.astype(jnp.float32)
    r = lax.rsqrt(lax.rsqrt(lax.rsqrt(lax.rsqrt(jnp.abs(y))))) * (1.0 / CODE)
    return jnp.where(y < 0, -r, r)


def column(row):
    width = row.shape[1]
    return jnp.transpose(jnp.broadcast_to(row, (128, width)))


def tile_rows(part, tile):
    return pl.ds((part * 2 + tile) * CR, CR)


def put_energies(messages, given_ref):
    for i, message in enumerate(messages):
        rest = message
        for level in range(3):
            term = rest.astype(jnp.bfloat16)
            rest = rest - term.astype(jnp.float32)
            for h in range(2):
                row = TILES * CR + (i * 3 + level) * 2 + h
                given_ref[row : row + 1, :] = term[:, h * HALF : h * HALF + HALF]


def get_energy(got_ref, i):
    tail = got_ref[TILES * CR :, :].astype(jnp.float32)
    halves = []
    for h in range(2):
        rows = [tail[(i * 3 + level) * 2 + h :][:1] for level in range(3)]
        halves.append(rows[0] + (rows[1] + rows[2]))
    return jnp.concatenate(halves, axis=1)


def inverse(energy):
    return lax.rsqrt(jnp.maximum(energy, TINY))


def chunk_of_lanes(row, j):
    return jnp.concatenate(
        [row[:, h * HALF + j * CR : h * HALF + j * CR + CR] for h in range(2)], axis=1
    )


def complex_product(left, right_re, right_im):
    dims = (((1,), (1,)), ((), ()))
    with_re = lax.dot_general(left, right_re, dims, preferred_element_type=jnp.float32)
    with_im = lax.dot_general(left, right_im, dims, preferred_element_type=jnp.float32)
    rows = left.shape[0] // 2
    return with_re[:rows] + with_im[rows:], with_re[rows:] - with_im[:rows]


def live_before(band_ref, tile):
    return sum((band_ref[0, d] < tile).astype(jnp.int32) for d in range(BAND))


def run(copies):
    for copy in copies:
        copy.start()
    for copy in copies:
        copy.wait()


def pack_kernel(pos_ref, tiles_ref, own_ref, chunk0_ref, token_ref, shift_ref, band_ref, sem):
    bands = pltpu.make_async_copy(tiles_ref, band_ref, sem.at[17])
    bands.start()
    copies = [
        pltpu.make_async_copy(
            own_ref.at[part, d, pl.ds(half * HALF, CR), :],
            chunk0_ref.at[pl.ds(((part * BAND + d) * 2 + half) * CR, CR), :],
            sem.at[(part * BAND + d) * 2 + half],
        )
        for part in range(2)
        for d in range(BAND)
        for half in range(2)
    ]
    for copy in copies:
        copy.start()
    token_ref[...] = jnp.zeros_like(token_ref)
    shift_ref[...] = jnp.zeros_like(shift_ref)
    bands.wait()
    for offset in (1, 2):
        count = live_before(band_ref, pos_ref[2] + offset).astype(jnp.float32)
        shift_ref[offset : offset + 1, :] = jnp.full((1, HALF), count).astype(jnp.bfloat16)
    run([pltpu.make_async_copy(shift_ref, chunk0_ref.at[pl.ds(ROWS, 16), :], sem.at[16])])
    for copy in copies:
        copy.wait()


def order_kernel(*refs):
    token_ref = refs[-1]
    token_ref[...] = jnp.zeros_like(token_ref)


def second_kernel(own_ref, chunk1_ref, sem):
    run(
        [
            pltpu.make_async_copy(
                own_ref.at[part, d, pl.ds(half * HALF + CR, CR), :],
                chunk1_ref.at[pl.ds(((part * BAND + d) * 2 + half) * CR, CR), :],
                sem.at[(part * BAND + d) * 2 + half],
            )
            for part in range(2)
            for d in range(BAND)
            for half in range(2)
        ]
    )


def self_kernel(
    pos_ref, own_ref, kept_ref, given_ref, msg_ref, again_ref, product_ref, col_ref, sem
):
    mine = pos_ref[1]
    again = pltpu.make_async_copy(own_ref, again_ref, sem)
    again.start()
    msg_ref[...] = jnp.zeros_like(msg_ref)
    right_re = jnp.concatenate([own_ref[0, d] for d in range(BAND)], axis=1)
    right_im = jnp.concatenate([own_ref[1, d] for d in range(BAND)], axis=1)
    diagonal = lax.broadcasted_iota(jnp.int32, (HALF, HALF), 0) == lax.broadcasted_iota(
        jnp.int32, (HALF, HALF), 1
    )
    for half in range(2):
        start = half * HALF
        left = jnp.concatenate(
            [
                jnp.concatenate(
                    [own_ref[part, d, start : start + HALF, :] for d in range(BAND)], axis=1
                )
                for part in range(2)
            ],
            axis=0,
        )
        real, imag = complex_product(left, right_re, right_im)
        product_ref[half, 0] = real
        product_ref[half, 1] = imag
        energies = jnp.where(diagonal, real[:, start : start + HALF], 0.0)
        msg_ref[0:1, start : start + HALF] = jnp.sum(energies, axis=0, keepdims=True)
        col_ref[start : start + HALF, :] = jnp.broadcast_to(
            jnp.sum(energies, axis=1, keepdims=True), (HALF, 128)
        )
    other = pl.multiple_of((1 - mine) * HALF, HALF)
    scale = lax.rsqrt(jnp.maximum(col_ref[pl.ds(other, HALF), 0:1], TINY)) * lax.rsqrt(
        jnp.maximum(msg_ref[0:1, :], TINY)
    )
    for part in range(2):
        given_ref[part] = encode(product_ref[1 - mine, part] * scale)
        kept_ref[part] = product_ref[mine, part]
    again.wait()


def row_energies(load, blocks):
    rows = []
    for block in range(blocks):
        total = jnp.zeros((CR, HALF), jnp.float32)
        for part in range(2):
            for d in range(BAND):
                wide = load(part, d, block).astype(jnp.float32)
                total += wide * wide
        folded = jnp.transpose(total[:, :128] + total[:, 128:])
        rows.append(jnp.sum(folded, axis=0, keepdims=True))
    return jnp.concatenate(rows, axis=1)


def pair_kernel(j, unit, pos_ref, band_ref, own_ref, far_ref, shift_ref, own_m, *rest):
    if (j, unit) == (0, 0):
        kept_ref, given_ref, pair_m, col_ref = rest
        pair_m[...] = jnp.zeros_like(pair_m)
    else:
        before_m, *rest = rest
        if unit == 1:
            near_ref, *rest = rest
        kept_ref, given_ref, pair_m, col_ref = rest
        pair_m[...] = before_m[...]
    core = pos_ref[0]
    mine = pos_ref[1]

    def far_block(part, k, half):
        start = pl.multiple_of(((part * BAND + k) * 2 + half) * CR, CR)
        return far_ref[pl.ds(start, CR), :]

    def far_chunk(part, k):
        start = pl.multiple_of((part * BAND + k) * 2 * CR, 2 * CR)
        return far_ref[pl.ds(start, 2 * CR), :]

    if unit == 0:
        pair_m[1:2, : 2 * CR] = row_energies(far_block, 2)
    elif j == 0:
        pair_m[0:1, :] = row_energies(
            lambda part, d, block: near_ref[part, d, block * CR : block * CR + CR, :], TS // CR
        )
    own_row = own_m[0:1, :]
    near_row = pair_m[0:1, :]
    far_row = pair_m[1:2, : 2 * CR]
    given_ref[TILES * CR :, :] = jnp.zeros((32, HALF), jnp.bfloat16)
    put_energies((own_row, near_row, pair_m[1:2, :]), given_ref)

    def aligned(load, part, s):
        blocks = []
        for d in range(BAND):
            block = load(part, jnp.maximum(d - s, 0))
            if d < 2:
                block = jnp.where(d >= s, block, jnp.zeros_like(block))
            blocks.append(block)
        return jnp.concatenate(blocks, axis=1)

    def chunk_of_rows(ref):
        def load(part, k):
            return jnp.concatenate(
                [ref[part, k, h * HALF + j * CR : h * HALF + j * CR + CR, :] for h in range(2)],
                axis=0,
            )
        return load

    def emit(keep, real, imag, start, rows, row, split):
        for part, value in enumerate((real, imag)):
            if not keep:
                value = encode(value * (col_ref[pl.ds(start, rows), 0:1] * row))
            for tile in range(2):
                if keep:
                    kept_ref[part, tile] = split(value, tile)
                else:
                    given_ref[tile_rows(part, tile), :] = split(value, tile)

    @pl.when(core == 0)
    def _():
        col_ref[...] = column(inverse(own_row))
        if unit == 0:
            load, energy = far_chunk, far_row
        else:
            load, energy = chunk_of_rows(near_ref), chunk_of_lanes(near_row, j)
        s = live_before(band_ref, pos_ref[2] + 2 - unit)
        right_re = aligned(load, 0, s)
        right_im = aligned(load, 1, s)
        row = inverse(energy)
        for keep in (False, True):
            start = pl.multiple_of((mine if keep else 1 - mine) * HALF, HALF)
            left = jnp.concatenate(
                [
                    jnp.concatenate(
                        [own_ref[part, d, pl.ds(start, HALF), :] for d in range(BAND)], axis=1
                    )
                    for part in range(2)
                ],
                axis=0,
            )
            real, imag = complex_product(left, right_re, right_im)
            emit(keep, real, imag, start, HALF, row, lambda v, t: v[t * CR : t * CR + CR])

    @pl.when(core == 1)
    def _():
        col_ref[: 2 * CR, :] = column(inverse(far_row))
        shifts = shift_ref[ROWS:, :].astype(jnp.float32)
        right_ref, energy = (own_ref, own_row) if unit == 0 else (near_ref, near_row)
        s = jnp.max(shifts[2 - unit : 3 - unit, :]).astype(jnp.int32)
        load = lambda part, k: right_ref[part, k]
        right_re = aligned(load, 0, s)
        right_im = aligned(load, 1, s)
        row = inverse(energy)
        for keep in (False, True):
            half = mine if keep else 1 - mine
            left = jnp.concatenate(
                [
                    jnp.concatenate([far_block(part, d, half) for d in range(BAND)], axis=1)
                    for part in range(2)
                ],
                axis=0,
            )
            real, imag = complex_product(left, right_re, right_im)
            start = pl.multiple_of(half * CR, CR)
            emit(keep, real, imag, start, CR, row, lambda v, t: v[:, t * HALF : t * HALF + HALF])


def decode_kernel(j, units, pos_ref, own_m, pair_m, *rest):
    kepts = rest[: len(units)]
    gots = rest[len(units) : 2 * len(units)]
    fin_ref, col_ref = rest[2 * len(units) :]
    core = pos_ref[0]
    mine = pos_ref[1]
    for n, (unit, kept_ref, got_ref) in enumerate(zip(units, kepts, gots)):
        other = [get_energy(got_ref, i) for i in range(3)]
        total = [m + o for m, o in zip((own_m[0:1, :], pair_m[0:1, :], pair_m[1:2, :]), other)]
        root = [jnp.sqrt(jnp.maximum(o, TINY)) for o in other]

        def emit(tile, start, root_row, total_row):
            back = col_ref[0, pl.ds(start, CR), 0:1] * root_row
            scale = lax.rsqrt(col_ref[1, pl.ds(start, CR), 0:1] * total_row + EPSILON)
            for part in range(2):
                value = kept_ref[part, tile] + decode(got_ref[tile_rows(part, tile), :]) * back
                fin_ref[n, part, tile] = (value * scale).astype(jnp.bfloat16)

        @pl.when(core == 0)
        def _():
            col_ref[0] = column(root[0])
            col_ref[1] = column(total[0])
            for tile in range(2):
                start = pl.multiple_of(mine * HALF + tile * CR, CR)
                if unit == 0:
                    emit(tile, start, root[2][:, : 2 * CR], total[2][:, : 2 * CR])
                else:
                    emit(tile, start, chunk_of_lanes(root[1], j), chunk_of_lanes(total[1], j))

        @pl.when(core == 1)
        def _():
            col_ref[0] = column(root[2])
            col_ref[1] = column(total[2])
            start = pl.multiple_of(mine * CR, CR)
            i = 0 if unit == 0 else 1
            for tile in range(2):
                lanes = slice(tile * HALF, tile * HALF + HALF)
                emit(tile, start, root[i][:, lanes], total[i][:, lanes])


def place_copies(core, j, unit, source_ref, out_ref, sem):
    copies = []
    for part in range(2):
        for tile in range(2):
            at = out_ref.at[part, 0, 2 - unit]
            piece = source_ref.at[part, tile]
            n = part * 2 + tile
            if core == 1:
                target = at.at[pl.ds(j * CR, CR), pl.ds(tile * HALF, HALF)]
                copies.append(pltpu.make_async_copy(piece, target, sem.at[n]))
            else:
                for h in range(2):
                    target = at.at[pl.ds(tile * CR, CR), pl.ds(h * HALF + j * CR, CR)]
                    source = piece.at[:, pl.ds(h * CR, CR)]
                    copies.append(pltpu.make_async_copy(source, target, sem.at[2 * n + h]))
    return copies


def finish_kernel(
    pos_ref, kept_ref, got_ref, mine_ref, first_ref, fin0, fin1, back0, back1,
    out_ref, fin_ref, col_ref, sem, place_sem,
):
    places = ((0, 0, 0, 0), (0, 1, 0, 1), (1, 0, 1, 0))
    for wait in (False, True):
        for core, sources in enumerate(((fin0, fin1), (back0, back1))):
            @pl.when(pos_ref[0] == core)
            def _():
                for n, (j, unit, source, slot) in enumerate(places):
                    for copy in place_copies(
                        core, j, unit, sources[source].at[slot], out_ref, place_sem.at[n]
                    ):
                        if wait:
                            copy.wait()
                        else:
                            copy.start()
        if wait:
            break
        start = pl.multiple_of(pos_ref[1] * HALF, HALF)
        energy = get_energy(first_ref, 0)
        other = jnp.sqrt(jnp.maximum(energy, TINY))
        total = mine_ref[0:1, :] + energy
        col_ref[0] = column(other)
        col_ref[1] = column(total)
        scale = lax.rsqrt(col_ref[1, pl.ds(start, HALF), 0:1] * total + EPSILON)
        back = col_ref[0, pl.ds(start, HALF), 0:1] * other
        for part in range(2):
            value = (kept_ref[part] + decode(got_ref[part]) * back) * scale
            fin_ref[part] = value.astype(jnp.bfloat16)
        run(
            [
                pltpu.make_async_copy(fin_ref.at[part], out_ref.at[part, 0, 0], sem.at[part])
                for part in range(2)
            ]
        )


def place_kernel(pos_ref, out_in_ref, fin_ref, back_ref, out_ref, sem):
    del out_in_ref
    for core, source in enumerate((fin_ref, back_ref)):
        @pl.when(pos_ref[0] == core)
        def _():
            run(place_copies(core, 1, 1, source.at[0], out_ref, sem))


def call(name, kernel, outs, specs, scratch=(), flops=0, after=None, out_specs=None, aliases=None, vmem=40):
    shapes = [jax.ShapeDtypeStruct(shape, dtype) for shape, dtype in outs]
    body = kernel if after is None else lambda _, *refs: kernel(*refs)
    run = pl.pallas_call(
        body,
        name=name,
        out_shape=shapes if len(shapes) > 1 else shapes[0],
        in_specs=specs if after is None else [ANY, *specs],
        out_specs=out_specs or ([VMEM] * len(shapes) if len(shapes) > 1 else VMEM),
        scratch_shapes=list(scratch),
        compiler_params=pltpu.CompilerParams(vmem_limit_bytes=vmem * MIB),
        input_output_aliases=aliases or {},
        cost_estimate=pl.CostEstimate(flops=flops, bytes_accessed=2**21, transcendentals=0),
    )
    return run if after is None else lambda *args: run(after, *args)


def shards(correlation, band_tiles):
    bf16, f32 = jnp.bfloat16, jnp.float32
    count = lax.axis_size("rows")
    core = lax.axis_index("rows") % 2
    mine = lax.axis_index("freq") % 2
    pos = jnp.stack([core, mine, lax.axis_index("rows")]).astype(jnp.int32)
    own = correlation.reshape(2, BAND, TS, HALF)
    swap = [(i, i ^ 1) for i in range(lax.axis_size("freq"))]
    pair = [(i, i ^ 1) for i in range(count)]
    far_route = [(i + 2, i) for i in range(0, count - 2, 2)] + [(i - 2, i) for i in range(3, count, 2)]
    back_route = [(i, i - 2) for i in range(3, count, 2)]

    half_shape = (2, HALF, TS)
    token = ((8, 128), f32)
    chunk0, after = call(
        "pack",
        pack_kernel,
        [((ROWS + 16, HALF), bf16), token],
        [SMEM, ANY, ANY],
        [pltpu.VMEM((16, HALF), bf16), pltpu.SMEM((1, BAND), jnp.int32), pltpu.SemaphoreType.DMA((18,))],
        vmem=52,
    )(pos, band_tiles, own)
    far0 = lax.ppermute(chunk0, "rows", far_route)
    kept_self, given_self, message, again = call(
        "self",
        self_kernel,
        [(half_shape, f32), (half_shape, bf16), ((8, TS), f32), (own.shape, bf16)],
        [SMEM, VMEM],
        [
            pltpu.VMEM((2, 2, HALF, TS), f32),
            pltpu.VMEM((TS, 128), f32),
            pltpu.SemaphoreType.DMA(()),
        ],
        after=after,
    )(pos, own)
    got_self = lax.ppermute(given_self, "freq", swap)
    chunk1 = call(
        "second",
        second_kernel,
        [((ROWS, HALF), bf16)],
        [VMEM],
        [pltpu.SemaphoreType.DMA((16,))],
        after=given_self,
    )(own)
    far1 = lax.ppermute(chunk1, "rows", far_route)
    near = lax.ppermute(again, "rows", pair)
    far = (far0, far1)

    unit_shape = (2, 2, CR, HALF)
    after = call("order", order_kernel, [token], [ANY], flops=TCOST)(far0)
    units = {}
    pair_m = None
    for j in range(CHUNKS):
        for unit in range(2):
            extra = [] if pair_m is None else [pair_m] + [near] * unit
            kept, given, pair_m = call(
                f"pair{j}{unit}",
                lambda *refs, j=j, unit=unit: pair_kernel(j, unit, *refs),
                [(unit_shape, f32), ((TILES * CR + 32, HALF), bf16), ((8, TS), f32)],
                [SMEM, SMEM] + [VMEM] * (4 + len(extra)),
                [pltpu.VMEM((TS, 128), f32)],
                flops=PCOST,
                after=after,
            )(pos, band_tiles, own, far[j], far0, message, *extra)
            units[j, unit] = kept, lax.ppermute(given, "freq", swap), pair_m
            after = kept
            if (j, unit) == (0, 0):
                after = call("order1", order_kernel, [token], [ANY], flops=FCOST, after=kept)(got_self)

    def finished(name, j, which, after):
        kepts = [units[j, unit][0] for unit in which]
        gots = [units[j, unit][1] for unit in which]
        fin = call(
            name,
            lambda *refs: decode_kernel(j, which, *refs),
            [((len(which), *unit_shape), bf16)],
            [SMEM] + [VMEM] * (2 + 2 * len(which)),
            [pltpu.VMEM((2, TS, 128), f32)],
            after=after,
        )(pos, message, units[j, which[-1]][2], *kepts, *gots)
        return fin, lax.ppermute(fin, "rows", back_route)

    fin0, back0 = finished("decode0", 0, (0, 1), after)
    fin1, back1 = finished("decode1", 1, (0,), fin0)
    fin2, back2 = finished("decode2", 1, (1,), fin1)
    out_shape = ((2, 1, 3, HALF, TS), bf16)
    out = call(
        "finish",
        finish_kernel,
        [out_shape],
        [SMEM] + [VMEM] * 8,
        [
            pltpu.VMEM((2, HALF, TS), bf16),
            pltpu.VMEM((2, TS, 128), f32),
            pltpu.SemaphoreType.DMA((2,)),
            pltpu.SemaphoreType.DMA((3, 8)),
        ],
        after=fin2,
        out_specs=ANY,
    )(pos, kept_self, got_self, message, units[0, 0][1], fin0, fin1, back0, back1)
    return call(
        "place",
        place_kernel,
        [out_shape],
        [SMEM, ANY, VMEM, VMEM],
        [pltpu.SemaphoreType.DMA((8,))],
        out_specs=ANY,
        aliases={1: 0},
    )(pos, out, fin2, back2)


def solution(mesh):
    return jax.shard_map(
        shards,
        mesh=mesh,
        in_specs=(P(None, "rows", None, None, "freq"), P("rows", None)),
        out_specs=P(None, "rows", None, "freq", None),
        check_vma=False,
    )
```

time: 71.1 us -> 64.1 us (0.902)
  the two profiles are of different devices: /device:TPU:1 before, /device:TPU:249 now
where the time goes in v6:
time: 64.1 us; the launch traced here: 63.7 us
  starting transfers between devices  30.4 us (47%)
  Pallas kernels  24.2 us (38%)
  waiting for transfers between devices  7.82 us (12%)
  local copies, waits for them, and re-layouts  0.79 us (1%)
    pallas_call x11, Pallas kernels, call(): return run if after is None else lambda *args: run(after, *args)  21 us
    ppermute x4, starting transfers between devices, shards(): units[j, unit] = (kept, lax.ppermute(given, 'freq', swap), pair_m)  10.6 us
    ppermute x3, starting transfers between devices, finished(): return (fin, lax.ppermute(fin, 'rows', back_route))  7.17 us
    ppermute x3, waiting for transfers between devices, finished(): return (fin, lax.ppermute(fin, 'rows', back_route))  5.86 us
    ppermute x1, starting transfers between devices, shards(): far0 = lax.ppermute(chunk0, 'rows', far_route)  4.42 us
    ppermute x1, starting transfers between devices, shards(): far1 = lax.ppermute(chunk1, 'rows', far_route)  3.21 us
    ppermute x1, starting transfers between devices, shards(): got_self = lax.ppermute(given_self, 'freq', swap)  3.12 us
    pallas_call x1, Pallas kernels, shards(): call('pack', pack_kernel, [((ROWS + 16, HALF), bf16), token], [SMEM, ANY,...  1.93 us
  transfers between devices with their start and end apart: 11, of which 4 were waited for; matrix products, arithmetic and copies ran while one was open for 0% of the time, Pallas kernels for 33%

profile of v6, /device:TPU:249, one launch (start us, length us, event | category | flops | bytes accessed | tf_op | source)
XLA Modules:
  0.0 63.7 jit_solution(6974046642542161454)
XLA Ops:
  0.0 0.0 copy-start
  0.0 0.1 pad_add_fusion.pos_ref.refs_0_
  0.1 0.0 copy-start.1
  0.1 0.8 %copy-done.1 = s32[1,4]{1,0:T(1,128)S(1)} copy-done((s32[1,4]{1,0:T(1,128)S(1)}, s32[1,4]{1,0:T(1,128)}, u32[]{:S(2)}) %copy-start.1) | copy-done | bytes 40
  0.9 1.9 %pack.1 = (bf16[2064,256]{1,0:T(8,128)(2,1)S(1)}, f32[8,128]{1,0:T(8,128)S(1)}) custom-call(s32[3]{0:T(128)S(1)} %pad_add_fusion.pos_ref.refs_0_, s32[1,4]{1,0:T(1,128)S(1)} %copy-done.1, bf16[2,4,512,256]{3,2,1,0:T(8,128)(2,1)} %bitcast.4), custom_call_target="tpu_custom_call" | custom-call | bytes 2097152 | tf_op jit(solution)/shard_map/pack/pallas_call | solution.py:444
  2.8 4.4 %collective-permute-start = (bf16[2064,256]{1,0:T(8,128)(2,1)S(1)}, bf16[2064,256]{1,0:T(8,128)(2,1)S(1)}, u32[]{:S(2)}, u32[]{:S(2)}) collective-permute-start(bf16[2064,256]{1,0:T(8,128)(2,1)S(1)} %get-tuple-element.23), channel_id=1, source_target_pairs={{8,0},{16,8},{24,16},{32,24},{40,32},{48,40},{56,48},{64,56},{72,6... | collective-permute-start | bytes 3170312 | tf_op jit(solution)/shard_map/ppermute | solution.py:452
  7.2 0.0 copy-done
  7.2 3.6 %self.1 = (f32[2,256,512]{2,1,0:T(8,128)S(1)}, bf16[2,256,512]{2,1,0:T(8,128)(2,1)S(1)}, f32[8,512]{1,0:T(8,128)S(1)}, bf16[2,4,512,256]{3,2,1,0:T(8,128)(2,1)S(1)}) custom-call(f32[8,128]{1,0:T(8,128)S(1)} %get-tuple-element.24._, s32[3]{0:T(128)S(1)} %pad_add_fusion.pos_ref.refs_0_, bf16[2,4,512,256]{3,2,1,0:T(8,128)(2,1)S(1)} %bitcast.5), custom_call_target="tpu_custom_call" | custom-call | bytes 2097152 | tf_op jit(solution)/shard_map/self/pallas_call | solution.py:427
  10.8 3.1 %collective-permute-start.1 = (bf16[2,256,512]{2,1,0:T(8,128)(2,1)S(1)}, bf16[2,256,512]{2,1,0:T(8,128)(2,1)S(1)}, u32[]{:S(2)}, u32[]{:S(2)}) collective-permute-start(bf16[2,256,512]{2,1,0:T(8,128)(2,1)S(1)} %get-tuple-element.27._), channel_id=1, source_target_pairs={{0,1},{1,0},{2,3},{3,2},{4,5},{5,4},{6,7},{7,6},{8,9},{9,8},{10,11... | collective-permute-start | bytes 1572872 | tf_op jit(solution)/shard_map/ppermute | solution.py:465
  14.0 1.5 %second.1 = bf16[2048,256]{1,0:T(8,128)(2,1)S(1)} custom-call(bf16[2,256,512]{2,1,0:T(8,128)(2,1)S(1)} %get-tuple-element.27._, bf16[2,4,512,256]{3,2,1,0:T(8,128)(2,1)S(1)} %bitcast.6), custom_call_target="tpu_custom_call" | custom-call | bytes 2097152 | tf_op jit(solution)/shard_map/second/pallas_call | solution.py:427
  15.5 3.2 %collective-permute-start.3 = (bf16[2048,256]{1,0:T(8,128)(2,1)S(1)}, bf16[2048,256]{1,0:T(8,128)(2,1)S(1)}, u32[]{:S(2)}, u32[]{:S(2)}) collective-permute-start(bf16[2048,256]{1,0:T(8,128)(2,1)S(1)} %second.1), channel_id=1, source_target_pairs={{8,0},{16,8},{24,16},{32,24},{40,32},{48,40},{56,48},{64,56},{72,6... | collective-permute-start | bytes 3145736 | tf_op jit(solution)/shard_map/ppermute | solution.py:474
  18.7 1.9 %collective-permute-start.2 = (bf16[2,4,512,256]{3,2,1,0:T(8,128)(2,1)S(1)}, bf16[2,4,512,256]{3,2,1,0:T(8,128)(2,1)S(1)}, u32[]{:S(2)}, u32[]{:S(2)}) collective-permute-start(bf16[2,4,512,256]{3,2,1,0:T(8,128)(2,1)S(1)} %get-tuple-element.29), channel_id=1, source_target_pairs={{0,4},{4,0},{8,12},{12,8},{16,20},{20,16},{24,28},{28,24},{32,36},... | collective-permute-start | bytes 6291464 | tf_op jit(solution)/shard_map/ppermute | solution.py:475
  20.6 0.0 collective-permute-done.refs_0_.refs_3_.refs_4_
  20.7 2.3 %pair00.1 = (f32[2,2,128,256]{3,2,1,0:T(8,128)S(1)}, bf16[544,256]{1,0:T(8,128)(2,1)S(1)}, f32[8,512]{1,0:T(8,128)S(1)}) custom-call(f32[8,128]{1,0:T(8,128)S(1)} %order.1._, s32[3]{0:T(128)S(1)} %pad_add_fusion.pos_ref.refs_0_, s32[1,4]{1,0:T(1,128)S(1)} %copy-done.1, bf16[2,4,512,256]{3,2,1,0:T(8,128)(2,1)S(1)} %bitcast.7, ...), custom_call_target="tpu_custom_call" | custom-call | bytes 2097152 | tf_op jit(solution)/shard_map/pair00/pallas_call | solution.py:427
  23.0 2.2 %collective-permute-start.4 = (bf16[544,256]{1,0:T(8,128)(2,1)S(1)}, bf16[544,256]{1,0:T(8,128)(2,1)S(1)}, u32[]{:S(2)}, u32[]{:S(2)}) collective-permute-start(bf16[544,256]{1,0:T(8,128)(2,1)S(1)} %get-tuple-element.35), channel_id=1, source_target_pairs={{0,1},{1,0},{2,3},{3,2},{4,5},{5,4},{6,7},{7,6},{8,9},{9,8},{10,11... | collective-permute-start | bytes 835592 | tf_op jit(solution)/shard_map/ppermute | solution.py:494
  25.1 0.9 %collective-permute-done.1.refs_0_.refs_2_ = bf16[2,256,512]{2,1,0:T(8,128)(2,1)S(1)} collective-permute-done((bf16[2,256,512]{2,1,0:T(8,128)(2,1)S(1)}, bf16[2,256,512]{2,1,0:T(8,128)(2,1)S(1)}, u32[]{:S(2)}, u32[]{:S(2)}) %collective-permute-start.1) | collective-permute-done | bytes 524320 | tf_op jit(solution)/shard_map/ppermute | solution.py:465
  26.0 0.0 collective-permute-done.2.refs_7_
  26.0 2.5 %pair01.1 = (f32[2,2,128,256]{3,2,1,0:T(8,128)S(1)}, bf16[544,256]{1,0:T(8,128)(2,1)S(1)}, f32[8,512]{1,0:T(8,128)S(1)}) custom-call(f32[8,128]{1,0:T(8,128)S(1)} %order1.1._, s32[3]{0:T(128)S(1)} %pad_add_fusion.pos_ref.refs_0_, s32[1,4]{1,0:T(1,128)S(1)} %copy-done.1, bf16[2,4,512,256]{3,2,1,0:T(8,128)(2,1)S(1)} %bitcast.8, ...), custom_call_target="tpu_custom_call" | custom-call | bytes 2097152 | tf_op jit(solution)/shard_map/pair01/pallas_call | solution.py:427
  28.5 3.1 %collective-permute-start.5 = (bf16[544,256]{1,0:T(8,128)(2,1)S(1)}, bf16[544,256]{1,0:T(8,128)(2,1)S(1)}, u32[]{:S(2)}, u32[]{:S(2)}) collective-permute-start(bf16[544,256]{1,0:T(8,128)(2,1)S(1)} %get-tuple-element.36), channel_id=1, source_target_pairs={{0,1},{1,0},{2,3},{3,2},{4,5},{5,4},{6,7},{7,6},{8,9},{9,8},{10,11... | collective-permute-start | bytes 835592 | tf_op jit(solution)/shard_map/ppermute | solution.py:494
  31.7 0.0 collective-permute-done.3.refs_3_
  31.7 2.3 %pair10.1 = (f32[2,2,128,256]{3,2,1,0:T(8,128)S(1)}, bf16[544,256]{1,0:T(8,128)(2,1)S(1)}, f32[8,512]{1,0:T(8,128)S(1)}) custom-call(f32[2,2,128,256]{3,2,1,0:T(8,128)S(1)} %get-tuple-element.30._.refs_4_, s32[3]{0:T(128)S(1)} %pad_add_fusion.pos_ref.refs_0_, s32[1,4]{1,0:T(1,128)S(1)} %copy-done.1, bf16[2,4,512,256]{3,2,1,0:T(8,128)(2,1)S(1)} %bitcast.9, ...), custom_call_target="tpu_custom_call" | custom-call | bytes 2097152 | tf_op jit(solution)/shard_map/pair10/pallas_call | solution.py:427
  34.0 2.2 %collective-permute-start.6 = (bf16[544,256]{1,0:T(8,128)(2,1)S(1)}, bf16[544,256]{1,0:T(8,128)(2,1)S(1)}, u32[]{:S(2)}, u32[]{:S(2)}) collective-permute-start(bf16[544,256]{1,0:T(8,128)(2,1)S(1)} %get-tuple-element.37), channel_id=1, source_target_pairs={{0,1},{1,0},{2,3},{3,2},{4,5},{5,4},{6,7},{7,6},{8,9},{9,8},{10,11... | collective-permute-start | bytes 835592 | tf_op jit(solution)/shard_map/ppermute | solution.py:494
  36.2 2.3 %pair11.1 = (f32[2,2,128,256]{3,2,1,0:T(8,128)S(1)}, bf16[544,256]{1,0:T(8,128)(2,1)S(1)}, f32[8,512]{1,0:T(8,128)S(1)}) custom-call(f32[2,2,128,256]{3,2,1,0:T(8,128)S(1)} %get-tuple-element.32._.refs_3_, s32[3]{0:T(128)S(1)} %pad_add_fusion.pos_ref.refs_0_, s32[1,4]{1,0:T(1,128)S(1)} %copy-done.1, bf16[2,4,512,256]{3,2,1,0:T(8,128)(2,1)S(1)} %bitcast.10, ...), custom_call_target="tpu_custom_call" | custom-call | bytes 2097152 | tf_op jit(solution)/shard_map/pair11/pallas_call | solution.py:427
  38.5 3.1 %collective-permute-start.7 = (bf16[544,256]{1,0:T(8,128)(2,1)S(1)}, bf16[544,256]{1,0:T(8,128)(2,1)S(1)}, u32[]{:S(2)}, u32[]{:S(2)}) collective-permute-start(bf16[544,256]{1,0:T(8,128)(2,1)S(1)} %get-tuple-element.39), channel_id=1, source_target_pairs={{0,1},{1,0},{2,3},{3,2},{4,5},{5,4},{6,7},{7,6},{8,9},{9,8},{10,11... | collective-permute-start | bytes 835592 | tf_op jit(solution)/shard_map/ppermute | solution.py:494
  41.6 0.0 collective-permute-done.4.refs_5_.refs_4_
  41.6 0.0 collective-permute-done.5.refs_6_
  41.6 1.7 %decode0.1._.refs_5_ = bf16[2,2,2,128,256]{4,3,2,1,0:T(8,128)(2,1)S(1)} custom-call(f32[2,2,128,256]{3,2,1,0:T(8,128)S(1)} %get-tuple-element.34._.refs_3_, s32[3]{0:T(128)S(1)} %pad_add_fusion.pos_ref.refs_0_, f32[8,512]{1,0:T(8,128)S(1)} %get-tuple-element.25.refs_5_.refs_1_.refs_3_, f32[8,512]{1,0:T(8,128)S(1)} %get-tuple-element.31.refs_6_.refs_2_, ...), custom_call_target="tpu_custom_call" | custom-call | bytes 2097152 | tf_op jit(solution)/shard_map/decode0/pallas_call | solution.py:427
  43.3 1.9 %collective-permute-start.8 = (bf16[2,2,2,128,256]{4,3,2,1,0:T(8,128)(2,1)S(1)}, bf16[2,2,2,128,256]{4,3,2,1,0:T(8,128)(2,1)S(1)}, u32[]{:S(2)}, u32[]{:S(2)}) collective-permute-start(bf16[2,2,2,128,256]{4,3,2,1,0:T(8,128)(2,1)S(1)} %decode0.1._.refs_5_), channel_id=1, source_target_pairs={{12,4},{20,12},{28,20},{36,28},{44,36},{52,44},{60,52},{68,60},{76... | collective-permute-start | bytes 1572872 | tf_op jit(solution)/shard_map/ppermute | solution.py:510
  45.3 0.0 collective-permute-done.6.refs_4_
  45.3 1.1 %decode1.1._.refs_6_ = bf16[1,2,2,128,256]{4,3,2,1,0:T(8,128)(2,1)S(1)} custom-call(bf16[2,2,2,128,256]{4,3,2,1,0:T(8,128)(2,1)S(1)} %decode0.1._.refs_5_, s32[3]{0:T(128)S(1)} %pad_add_fusion.pos_ref.refs_0_, f32[8,512]{1,0:T(8,128)S(1)} %get-tuple-element.25.refs_5_.refs_1_.refs_3_, f32[8,512]{1,0:T(8,128)S(1)} %get-tuple-element.33.refs_6_.refs_2_, ...), custom_call_target="tpu_custom_call" | custom-call | bytes 2097152 | tf_op jit(solution)/shard_map/decode1/pallas_call | solution.py:427
  46.4 1.9 %collective-permute-start.9 = (bf16[1,2,2,128,256]{4,3,2,1,0:T(8,128)(2,1)S(1)}, bf16[1,2,2,128,256]{4,3,2,1,0:T(8,128)(2,1)S(1)}, u32[]{:S(2)}, u32[]{:S(2)}) collective-permute-start(bf16[1,2,2,128,256]{4,3,2,1,0:T(8,128)(2,1)S(1)} %decode1.1._.refs_6_), channel_id=1, source_target_pairs={{12,4},{20,12},{28,20},{36,28},{44,36},{52,44},{60,52},{68,60},{76... | collective-permute-start | bytes 786440 | tf_op jit(solution)/shard_map/ppermute | solution.py:510
  48.3 1.0 %collective-permute-done.7.refs_4_ = bf16[544,256]{1,0:T(8,128)(2,1)S(1)} collective-permute-done((bf16[544,256]{1,0:T(8,128)(2,1)S(1)}, bf16[544,256]{1,0:T(8,128)(2,1)S(1)}, u32[]{:S(2)}, u32[]{:S(2)}) %collective-permute-start.7) | collective-permute-done | bytes 278560 | tf_op jit(solution)/shard_map/ppermute | solution.py:494
  49.4 1.1 %decode2.1._.fin_ref = bf16[1,2,2,128,256]{4,3,2,1,0:T(8,128)(2,1)S(1)} custom-call(bf16[1,2,2,128,256]{4,3,2,1,0:T(8,128)(2,1)S(1)} %decode1.1._.refs_6_, s32[3]{0:T(128)S(1)} %pad_add_fusion.pos_ref.refs_0_, f32[8,512]{1,0:T(8,128)S(1)} %get-tuple-element.25.refs_5_.refs_1_.refs_3_, f32[8,512]{1,0:T(8,128)S(1)} %get-tuple-element.38.refs_2_, ...), custom_call_target="tpu_custom_call" | custom-call | bytes 2097152 | tf_op jit(solution)/shard_map/decode2/pallas_call | solution.py:427
  50.5 3.3 %collective-permute-start.10 = (bf16[1,2,2,128,256]{4,3,2,1,0:T(8,128)(2,1)S(1)}, bf16[1,2,2,128,256]{4,3,2,1,0:T(8,128)(2,1)S(1)}, u32[]{:S(2)}, u32[]{:S(2)}) collective-permute-start(bf16[1,2,2,128,256]{4,3,2,1,0:T(8,128)(2,1)S(1)} %decode2.1._.fin_ref), channel_id=1, source_target_pairs={{12,4},{20,12},{28,20},{36,28},{44,36},{52,44},{60,52},{68,60},{76... | collective-permute-start | bytes 786440 | tf_op jit(solution)/shard_map/ppermute | solution.py:510
  53.9 5.5 %collective-permute-done.9.refs_8_ = bf16[1,2,2,128,256]{4,3,2,1,0:T(8,128)(2,1)S(1)} collective-permute-done((bf16[1,2,2,128,256]{4,3,2,1,0:T(8,128)(2,1)S(1)}, bf16[1,2,2,128,256]{4,3,2,1,0:T(8,128)(2,1)S(1)}, u32[]{:S(2)}, u32[]{:S(2)}) %collective-permute-start.9) | collective-permute-done | bytes 262176 | tf_op jit(solution)/shard_map/ppermute | solution.py:510
  59.4 0.0 collective-permute-done.8.refs_7_
  59.4 2.5 %finish.1.out_in_ref = bf16[2,1,3,256,512]{4,3,2,1,0:T(8,128)(2,1)} custom-call(bf16[1,2,2,128,256]{4,3,2,1,0:T(8,128)(2,1)S(1)} %decode2.1._.fin_ref, s32[3]{0:T(128)S(1)} %pad_add_fusion.pos_ref.refs_0_, f32[2,256,512]{2,1,0:T(8,128)S(1)} %get-tuple-element.40.refs_1_, bf16[2,256,512]{2,1,0:T(8,128)(2,1)S(1)} %collective-permute-done.1.refs_0_.refs_2_, ...), custom_call_target="tpu_custom_call" | custom-call | bytes 2097152 | tf_op jit(solution)/shard_map/finish/pallas_call | solution.py:427
  61.9 0.3 collective-permute-done.10.back_ref
  62.2 1.3 %place.1 = bf16[2,1,3,256,512]{4,3,2,1,0:T(8,128)(2,1)} custom-call(s32[3]{0:T(128)S(1)} %pad_add_fusion.pos_ref.refs_0_, bf16[2,1,3,256,512]{4,3,2,1,0:T(8,128)(2,1)} %finish.1.out_in_ref, bf16[1,2,2,128,256]{4,3,2,1,0:T(8,128)(2,1)S(1)} %decode2.1._.fin_ref, ...), custom_call_target="tpu_custom_call", output_to_operand_aliasing={{}: (1, {})} | custom-call | bytes 2097152 | tf_op jit(solution)/shard_map/place/pallas_call | solution.py:530
  (2 shorter events, 0.0 us)
Async XLA Ops:
  0.0 7.2 %copy-start = (bf16[2,1,4,512,256]{4,3,2,1,0:T(8,128)(2,1)S(1)}, bf16[2,1,4,512,256]{4,3,2,1,0:T(8,128)(2,1)}, u32[]{:S(2)}) copy-start(bf16[2,1,4,512,256]{4,3,2,1,0:T(8,128)(2,1)} %param.2) | copy-start | bytes 6291460
  0.1 0.8 %copy-start.1 = (s32[1,4]{1,0:T(1,128)S(1)}, s32[1,4]{1,0:T(1,128)}, u32[]{:S(2)}) copy-start(s32[1,4]{1,0:T(1,128)} %refs_1_.7) | copy-start | bytes 52
  2.8 17.8 %collective-permute-start = (bf16[2064,256]{1,0:T(8,128)(2,1)S(1)}, bf16[2064,256]{1,0:T(8,128)(2,1)S(1)}, u32[]{:S(2)}, u32[]{:S(2)}) collective-permute-start(bf16[2064,256]{1,0:T(8,128)(2,1)S(1)} %get-tuple-element.23), channel_id=1, source_target_pairs={{8,0},{16,8},{24,16},{32,24},{40,32},{48,40},{56,48},{64,56},{72,6... | collective-permute-start | bytes 3170312 | tf_op jit(solution)/shard_map/ppermute | solution.py:452
  10.8 15.2 %collective-permute-start.1 = (bf16[2,256,512]{2,1,0:T(8,128)(2,1)S(1)}, bf16[2,256,512]{2,1,0:T(8,128)(2,1)S(1)}, u32[]{:S(2)}, u32[]{:S(2)}) collective-permute-start(bf16[2,256,512]{2,1,0:T(8,128)(2,1)S(1)} %get-tuple-element.27._), channel_id=1, source_target_pairs={{0,1},{1,0},{2,3},{3,2},{4,5},{5,4},{6,7},{7,6},{8,9},{9,8},{10,11... | collective-permute-start | bytes 1572872 | tf_op jit(solution)/shard_map/ppermute | solution.py:465
  15.5 16.2 %collective-permute-start.3 = (bf16[2048,256]{1,0:T(8,128)(2,1)S(1)}, bf16[2048,256]{1,0:T(8,128)(2,1)S(1)}, u32[]{:S(2)}, u32[]{:S(2)}) collective-permute-start(bf16[2048,256]{1,0:T(8,128)(2,1)S(1)} %second.1), channel_id=1, source_target_pairs={{8,0},{16,8},{24,16},{32,24},{40,32},{48,40},{56,48},{64,56},{72,6... | collective-permute-start | bytes 3145736 | tf_op jit(solution)/shard_map/ppermute | solution.py:474
  18.7 7.3 %collective-permute-start.2 = (bf16[2,4,512,256]{3,2,1,0:T(8,128)(2,1)S(1)}, bf16[2,4,512,256]{3,2,1,0:T(8,128)(2,1)S(1)}, u32[]{:S(2)}, u32[]{:S(2)}) collective-permute-start(bf16[2,4,512,256]{3,2,1,0:T(8,128)(2,1)S(1)} %get-tuple-element.29), channel_id=1, source_target_pairs={{0,4},{4,0},{8,12},{12,8},{16,20},{20,16},{24,28},{28,24},{32,36},... | collective-permute-start | bytes 6291464 | tf_op jit(solution)/shard_map/ppermute | solution.py:475
  23.0 18.6 %collective-permute-start.4 = (bf16[544,256]{1,0:T(8,128)(2,1)S(1)}, bf16[544,256]{1,0:T(8,128)(2,1)S(1)}, u32[]{:S(2)}, u32[]{:S(2)}) collective-permute-start(bf16[544,256]{1,0:T(8,128)(2,1)S(1)} %get-tuple-element.35), channel_id=1, source_target_pairs={{0,1},{1,0},{2,3},{3,2},{4,5},{5,4},{6,7},{7,6},{8,9},{9,8},{10,11... | collective-permute-start | bytes 835592 | tf_op jit(solution)/shard_map/ppermute | solution.py:494
  28.5 13.0 %collective-permute-start.5 = (bf16[544,256]{1,0:T(8,128)(2,1)S(1)}, bf16[544,256]{1,0:T(8,128)(2,1)S(1)}, u32[]{:S(2)}, u32[]{:S(2)}) collective-permute-start(bf16[544,256]{1,0:T(8,128)(2,1)S(1)} %get-tuple-element.36), channel_id=1, source_target_pairs={{0,1},{1,0},{2,3},{3,2},{4,5},{5,4},{6,7},{7,6},{8,9},{9,8},{10,11... | collective-permute-start | bytes 835592 | tf_op jit(solution)/shard_map/ppermute | solution.py:494
  34.0 11.3 %collective-permute-start.6 = (bf16[544,256]{1,0:T(8,128)(2,1)S(1)}, bf16[544,256]{1,0:T(8,128)(2,1)S(1)}, u32[]{:S(2)}, u32[]{:S(2)}) collective-permute-start(bf16[544,256]{1,0:T(8,128)(2,1)S(1)} %get-tuple-element.37), channel_id=1, source_target_pairs={{0,1},{1,0},{2,3},{3,2},{4,5},{5,4},{6,7},{7,6},{8,9},{9,8},{10,11... | collective-permute-start | bytes 835592 | tf_op jit(solution)/shard_map/ppermute | solution.py:494
  38.5 10.9 %collective-permute-start.7 = (bf16[544,256]{1,0:T(8,128)(2,1)S(1)}, bf16[544,256]{1,0:T(8,128)(2,1)S(1)}, u32[]{:S(2)}, u32[]{:S(2)}) collective-permute-start(bf16[544,256]{1,0:T(8,128)(2,1)S(1)} %get-tuple-element.39), channel_id=1, source_target_pairs={{0,1},{1,0},{2,3},{3,2},{4,5},{5,4},{6,7},{7,6},{8,9},{9,8},{10,11... | collective-permute-start | bytes 835592 | tf_op jit(solution)/shard_map/ppermute | solution.py:494
  43.3 16.1 %collective-permute-start.8 = (bf16[2,2,2,128,256]{4,3,2,1,0:T(8,128)(2,1)S(1)}, bf16[2,2,2,128,256]{4,3,2,1,0:T(8,128)(2,1)S(1)}, u32[]{:S(2)}, u32[]{:S(2)}) collective-permute-start(bf16[2,2,2,128,256]{4,3,2,1,0:T(8,128)(2,1)S(1)} %decode0.1._.refs_5_), channel_id=1, source_target_pairs={{12,4},{20,12},{28,20},{36,28},{44,36},{52,44},{60,52},{68,60},{76... | collective-permute-start | bytes 1572872 | tf_op jit(solution)/shard_map/ppermute | solution.py:510
  46.4 13.0 %collective-permute-start.9 = (bf16[1,2,2,128,256]{4,3,2,1,0:T(8,128)(2,1)S(1)}, bf16[1,2,2,128,256]{4,3,2,1,0:T(8,128)(2,1)S(1)}, u32[]{:S(2)}, u32[]{:S(2)}) collective-permute-start(bf16[1,2,2,128,256]{4,3,2,1,0:T(8,128)(2,1)S(1)} %decode1.1._.refs_6_), channel_id=1, source_target_pairs={{12,4},{20,12},{28,20},{36,28},{44,36},{52,44},{60,52},{68,60},{76... | collective-permute-start | bytes 786440 | tf_op jit(solution)/shard_map/ppermute | solution.py:510
  50.5 11.7 %collective-permute-start.10 = (bf16[1,2,2,128,256]{4,3,2,1,0:T(8,128)(2,1)S(1)}, bf16[1,2,2,128,256]{4,3,2,1,0:T(8,128)(2,1)S(1)}, u32[]{:S(2)}, u32[]{:S(2)}) collective-permute-start(bf16[1,2,2,128,256]{4,3,2,1,0:T(8,128)(2,1)S(1)} %decode2.1._.fin_ref), channel_id=1, source_target_pairs={{12,4},{20,12},{28,20},{36,28},{44,36},{52,44},{60,52},{68,60},{76... | collective-permute-start | bytes 786440 | tf_op jit(solution)/shard_map/ppermute | solution.py:510

commit v7 on v6

--- a/solution.py
+++ b/solution.py
@@ -128,27 +128,23 @@
     token_ref[...] = jnp.zeros_like(token_ref)
 
 
-def second_kernel(own_ref, chunk1_ref, sem):
-    run(
-        [
-            pltpu.make_async_copy(
-                own_ref.at[part, d, pl.ds(half * HALF + CR, CR), :],
-                chunk1_ref.at[pl.ds(((part * BAND + d) * 2 + half) * CR, CR), :],
-                sem.at[(part * BAND + d) * 2 + half],
-            )
-            for part in range(2)
-            for d in range(BAND)
-            for half in range(2)
-        ]
-    )
-
-
 def self_kernel(
-    pos_ref, own_ref, kept_ref, given_ref, msg_ref, again_ref, product_ref, col_ref, sem
+    pos_ref, own_ref, kept_ref, given_ref, msg_ref, again_ref, chunk1_ref, product_ref, col_ref, sem
 ):
     mine = pos_ref[1]
-    again = pltpu.make_async_copy(own_ref, again_ref, sem)
-    again.start()
+    copies = [pltpu.make_async_copy(own_ref, again_ref, sem.at[16])]
+    copies += [
+        pltpu.make_async_copy(
+            own_ref.at[part, d, pl.ds(half * HALF + CR, CR), :],
+            chunk1_ref.at[pl.ds(((part * BAND + d) * 2 + half) * CR, CR), :],
+            sem.at[(part * BAND + d) * 2 + half],
+        )
+        for part in range(2)
+        for d in range(BAND)
+        for half in range(2)
+    ]
+    for copy in copies:
+        copy.start()
     msg_ref[...] = jnp.zeros_like(msg_ref)
     right_re = jnp.concatenate([own_ref[0, d] for d in range(BAND)], axis=1)
     right_im = jnp.concatenate([own_ref[1, d] for d in range(BAND)], axis=1)
@@ -181,7 +177,8 @@
     for part in range(2):
         given_ref[part] = encode(product_ref[1 - mine, part] * scale)
         kept_ref[part] = product_ref[mine, part]
-    again.wait()
+    for copy in copies:
+        copy.wait()
 
 
 def row_energies(load, blocks):
@@ -306,7 +303,7 @@
             emit(keep, real, imag, start, CR, row, lambda v, t: v[:, t * HALF : t * HALF + HALF])
 
 
-def decode_kernel(j, units, pos_ref, own_m, pair_m, *rest):
+def decode_kernel(j, units, pos_ref, own_m, pair_m, *rest, first=0):
     kepts = rest[: len(units)]
     gots = rest[len(units) : 2 * len(units)]
     fin_ref, col_ref = rest[2 * len(units) :]
@@ -322,7 +319,7 @@
             scale = lax.rsqrt(col_ref[1, pl.ds(start, CR), 0:1] * total_row + EPSILON)
             for part in range(2):
                 value = kept_ref[part, tile] + decode(got_ref[tile_rows(part, tile), :]) * back
-                fin_ref[n, part, tile] = (value * scale).astype(jnp.bfloat16)
+                fin_ref[first + n, part, tile] = (value * scale).astype(jnp.bfloat16)
 
         @pl.when(core == 0)
         def _():
@@ -344,6 +341,13 @@
             for tile in range(2):
                 lanes = slice(tile * HALF, tile * HALF + HALF)
                 emit(tile, start, root[i][:, lanes], total[i][:, lanes])
+
+
+def last_decode_kernel(pos_ref, own_m, pair_m, kept_ref, got_ref, done_ref, fin_ref, col_ref, sem):
+    copy = pltpu.make_async_copy(done_ref.at[0], fin_ref.at[0], sem)
+    copy.start()
+    decode_kernel(1, (1,), pos_ref, own_m, pair_m, kept_ref, got_ref, fin_ref, col_ref, first=1)
+    copy.wait()
 
 
 def place_copies(core, j, unit, source_ref, out_ref, sem):
@@ -365,17 +369,15 @@
 
 
 def finish_kernel(
-    pos_ref, kept_ref, got_ref, mine_ref, first_ref, fin0, fin1, back0, back1,
-    out_ref, fin_ref, col_ref, sem, place_sem,
+    pos_ref, kept_ref, got_ref, mine_ref, first_ref, fin0, back0, out_ref, fin_ref, col_ref, sem, place_sem
 ):
-    places = ((0, 0, 0, 0), (0, 1, 0, 1), (1, 0, 1, 0))
     for wait in (False, True):
-        for core, sources in enumerate(((fin0, fin1), (back0, back1))):
+        for core, source in enumerate((fin0, back0)):
             @pl.when(pos_ref[0] == core)
             def _():
-                for n, (j, unit, source, slot) in enumerate(places):
+                for unit in range(2):
                     for copy in place_copies(
-                        core, j, unit, sources[source].at[slot], out_ref, place_sem.at[n]
+                        core, 0, unit, source.at[unit], out_ref, place_sem.at[unit]
                     ):
                         if wait:
                             copy.wait()
@@ -407,7 +409,13 @@
     for core, source in enumerate((fin_ref, back_ref)):
         @pl.when(pos_ref[0] == core)
         def _():
-            run(place_copies(core, 1, 1, source.at[0], out_ref, sem))
+            run(
+                [
+                    copy
+                    for unit in range(2)
+                    for copy in place_copies(core, 1, unit, source.at[unit], out_ref, sem.at[unit])
+                ]
+            )
 
 
 def call(name, kernel, outs, specs, scratch=(), flops=0, after=None, out_specs=None, aliases=None, vmem=40):
@@ -450,27 +458,19 @@
         vmem=52,
     )(pos, band_tiles, own)
     far0 = lax.ppermute(chunk0, "rows", far_route)
-    kept_self, given_self, message, again = call(
+    kept_self, given_self, message, again, chunk1 = call(
         "self",
         self_kernel,
-        [(half_shape, f32), (half_shape, bf16), ((8, TS), f32), (own.shape, bf16)],
+        [(half_shape, f32), (half_shape, bf16), ((8, TS), f32), (own.shape, bf16), ((ROWS, HALF), bf16)],
         [SMEM, VMEM],
         [
             pltpu.VMEM((2, 2, HALF, TS), f32),
             pltpu.VMEM((TS, 128), f32),
-            pltpu.SemaphoreType.DMA(()),
+            pltpu.SemaphoreType.DMA((17,)),
         ],
         after=after,
     )(pos, own)
     got_self = lax.ppermute(given_self, "freq", swap)
-    chunk1 = call(
-        "second",
-        second_kernel,
-        [((ROWS, HALF), bf16)],
-        [VMEM],
-        [pltpu.SemaphoreType.DMA((16,))],
-        after=given_self,
-    )(own)
     far1 = lax.ppermute(chunk1, "rows", far_route)
     near = lax.ppermute(again, "rows", pair)
     far = (far0, far1)
@@ -496,43 +496,54 @@
             if (j, unit) == (0, 0):
                 after = call("order1", order_kernel, [token], [ANY], flops=FCOST, after=kept)(got_self)
 
-    def finished(name, j, which, after):
-        kepts = [units[j, unit][0] for unit in which]
-        gots = [units[j, unit][1] for unit in which]
-        fin = call(
+    def decoded(name, j, which, after):
+        return call(
             name,
             lambda *refs: decode_kernel(j, which, *refs),
             [((len(which), *unit_shape), bf16)],
             [SMEM] + [VMEM] * (2 + 2 * len(which)),
             [pltpu.VMEM((2, TS, 128), f32)],
             after=after,
-        )(pos, message, units[j, which[-1]][2], *kepts, *gots)
-        return fin, lax.ppermute(fin, "rows", back_route)
-
-    fin0, back0 = finished("decode0", 0, (0, 1), after)
-    fin1, back1 = finished("decode1", 1, (0,), fin0)
-    fin2, back2 = finished("decode2", 1, (1,), fin1)
+        )(
+            pos,
+            message,
+            units[j, which[-1]][2],
+            *[units[j, unit][0] for unit in which],
+            *[units[j, unit][1] for unit in which],
+        )
+
+    fin0 = decoded("decode0", 0, (0, 1), after)
+    back0 = lax.ppermute(fin0, "rows", back_route)
+    fin1 = decoded("decode1", 1, (0,), fin0)
+    fin2 = call(
+        "decode2",
+        last_decode_kernel,
+        [((2, *unit_shape), bf16)],
+        [SMEM] + [VMEM] * 5,
+        [pltpu.VMEM((2, TS, 128), f32), pltpu.SemaphoreType.DMA(())],
+    )(pos, message, units[1, 1][2], *units[1, 1][:2], fin1)
+    back2 = lax.ppermute(fin2, "rows", back_route)
     out_shape = ((2, 1, 3, HALF, TS), bf16)
     out = call(
         "finish",
         finish_kernel,
         [out_shape],
-        [SMEM] + [VMEM] * 8,
+        [SMEM] + [VMEM] * 6,
         [
             pltpu.VMEM((2, HALF, TS), bf16),
             pltpu.VMEM((2, TS, 128), f32),
             pltpu.SemaphoreType.DMA((2,)),
-            pltpu.SemaphoreType.DMA((3, 8)),
+            pltpu.SemaphoreType.DMA((2, 8)),
         ],
         after=fin2,
         out_specs=ANY,
-    )(pos, kept_self, got_self, message, units[0, 0][1], fin0, fin1, back0, back1)
+    )(pos, kept_self, got_self, message, units[0, 0][1], fin0, back0)
     return call(
         "place",
         place_kernel,
         [out_shape],
         [SMEM, ANY, VMEM, VMEM],
-        [pltpu.SemaphoreType.DMA((8,))],
+        [pltpu.SemaphoreType.DMA((2, 8))],
         out_specs=ANY,
         aliases={1: 0},
     )(pos, out, fin2, back2)

time: 64.1 us -> 67.6 us (1.055)
  the two profiles are of different devices: /device:TPU:249 before, /device:TPU:125 now
where the time goes in v7:
time: 67.6 us; the launch traced here: 67.2 us
  starting transfers between devices  26.8 us (40%)
  Pallas kernels  24.4 us (36%)
  waiting for transfers between devices  14.8 us (22%)
  local copies, waits for them, and re-layouts  0.79 us (1%)
    pallas_call x9, Pallas kernels, call(): return run if after is None else lambda *args: run(after, *args)  19.8 us
    ppermute x4, starting transfers between devices, shards(): units[j, unit] = (kept, lax.ppermute(given, 'freq', swap), pair_m)  10.6 us
    ppermute x1, waiting for transfers between devices, shards(): back2 = lax.ppermute(fin2, 'rows', back_route)  5.29 us
    ppermute x1, starting transfers between devices, shards(): far0 = lax.ppermute(chunk0, 'rows', far_route)  4.42 us
    ppermute x1, waiting for transfers between devices, shards(): back0 = lax.ppermute(fin0, 'rows', back_route)  3.62 us
    ppermute x4, waiting for transfers between devices, shards(): units[j, unit] = (kept, lax.ppermute(given, 'freq', swap), pair_m)  3.46 us
    ppermute x1, starting transfers between devices, shards(): far1 = lax.ppermute(chunk1, 'rows', far_route)  3.2 us
    ppermute x1, starting transfers between devices, shards(): got_self = lax.ppermute(given_self, 'freq', swap)  2.82 us
  transfers between devices with their start and end apart: 10, of which 4 were waited for; matrix products, arithmetic and copies ran while one was open for 0% of the time, Pallas kernels for 31%

profile of v7, /device:TPU:125, one launch (start us, length us, event | category | flops | bytes accessed | tf_op | source)
XLA Modules:
  0.0 67.2 jit_solution(10786644460110289610)
XLA Ops:
  0.0 0.0 copy-start
  0.0 0.1 pad_add_fusion.pos_ref.refs_0_
  0.1 0.0 copy-start.1
  0.1 0.8 %copy-done.1 = s32[1,4]{1,0:T(1,128)S(1)} copy-done((s32[1,4]{1,0:T(1,128)S(1)}, s32[1,4]{1,0:T(1,128)}, u32[]{:S(2)}) %copy-start.1) | copy-done | bytes 40
  0.9 1.9 %pack.1 = (bf16[2064,256]{1,0:T(8,128)(2,1)S(1)}, f32[8,128]{1,0:T(8,128)S(1)}) custom-call(s32[3]{0:T(128)S(1)} %pad_add_fusion.pos_ref.refs_0_, s32[1,4]{1,0:T(1,128)S(1)} %copy-done.1, bf16[2,4,512,256]{3,2,1,0:T(8,128)(2,1)} %bitcast.4), custom_call_target="tpu_custom_call" | custom-call | bytes 2097152 | tf_op jit(solution)/shard_map/pack/pallas_call | solution.py:452
  2.8 4.4 %collective-permute-start = (bf16[2064,256]{1,0:T(8,128)(2,1)S(1)}, bf16[2064,256]{1,0:T(8,128)(2,1)S(1)}, u32[]{:S(2)}, u32[]{:S(2)}) collective-permute-start(bf16[2064,256]{1,0:T(8,128)(2,1)S(1)} %get-tuple-element.26), channel_id=1, source_target_pairs={{8,0},{16,8},{24,16},{32,24},{40,32},{48,40},{56,48},{64,56},{72,6... | collective-permute-start | bytes 3170312 | tf_op jit(solution)/shard_map/ppermute | solution.py:460
  7.2 0.0 copy-done
  7.2 5.1 %self.1 = (f32[2,256,512]{2,1,0:T(8,128)S(1)}, bf16[2,256,512]{2,1,0:T(8,128)(2,1)S(1)}, f32[8,512]{1,0:T(8,128)S(1)}, bf16[2,4,512,256]{3,2,1,0:T(8,128)(2,1)S(1)}, bf16[2048,256]{1,0:T(8,128)(2,1)S(1)}) custom-call(f32[8,128]{1,0:T(8,128)S(1)} %get-tuple-element.24._, s32[3]{0:T(128)S(1)} %pad_add_fusion.pos_ref.refs_0_, bf16[2,4,512,256]{3,2,1,0:T(8,128)(2,1)S(1)} %bitcast.5), custom_call_target="tpu_custom_call" | custom-call | bytes 2097152 | tf_op jit(solution)/shard_map/self/pallas_call | solution.py:435
  12.4 2.8 %collective-permute-start.1 = (bf16[2,256,512]{2,1,0:T(8,128)(2,1)S(1)}, bf16[2,256,512]{2,1,0:T(8,128)(2,1)S(1)}, u32[]{:S(2)}, u32[]{:S(2)}) collective-permute-start(bf16[2,256,512]{2,1,0:T(8,128)(2,1)S(1)} %get-tuple-element.28), channel_id=1, source_target_pairs={{0,1},{1,0},{2,3},{3,2},{4,5},{5,4},{6,7},{7,6},{8,9},{9,8},{10,11... | collective-permute-start | bytes 1572872 | tf_op jit(solution)/shard_map/ppermute | solution.py:473
  15.2 3.2 %collective-permute-start.3 = (bf16[2048,256]{1,0:T(8,128)(2,1)S(1)}, bf16[2048,256]{1,0:T(8,128)(2,1)S(1)}, u32[]{:S(2)}, u32[]{:S(2)}) collective-permute-start(bf16[2048,256]{1,0:T(8,128)(2,1)S(1)} %get-tuple-element.32), channel_id=1, source_target_pairs={{8,0},{16,8},{24,16},{32,24},{40,32},{48,40},{56,48},{64,56},{72,6... | collective-permute-start | bytes 3145736 | tf_op jit(solution)/shard_map/ppermute | solution.py:474
  18.4 1.9 %collective-permute-start.2 = (bf16[2,4,512,256]{3,2,1,0:T(8,128)(2,1)S(1)}, bf16[2,4,512,256]{3,2,1,0:T(8,128)(2,1)S(1)}, u32[]{:S(2)}, u32[]{:S(2)}) collective-permute-start(bf16[2,4,512,256]{3,2,1,0:T(8,128)(2,1)S(1)} %get-tuple-element.30), channel_id=1, source_target_pairs={{0,4},{4,0},{8,12},{12,8},{16,20},{20,16},{24,28},{28,24},{32,36},... | collective-permute-start | bytes 6291464 | tf_op jit(solution)/shard_map/ppermute | solution.py:475
  20.3 0.0 collective-permute-done.refs_0_.refs_3_.refs_4_
  20.3 2.3 %pair00.1 = (f32[2,2,128,256]{3,2,1,0:T(8,128)S(1)}, bf16[544,256]{1,0:T(8,128)(2,1)S(1)}, f32[8,512]{1,0:T(8,128)S(1)}) custom-call(f32[8,128]{1,0:T(8,128)S(1)} %order.1._, s32[3]{0:T(128)S(1)} %pad_add_fusion.pos_ref.refs_0_, s32[1,4]{1,0:T(1,128)S(1)} %copy-done.1, bf16[2,4,512,256]{3,2,1,0:T(8,128)(2,1)S(1)} %bitcast.6, ...), custom_call_target="tpu_custom_call" | custom-call | bytes 2097152 | tf_op jit(solution)/shard_map/pair00/pallas_call | solution.py:435
  22.7 2.5 %collective-permute-start.5 = (bf16[544,256]{1,0:T(8,128)(2,1)S(1)}, bf16[544,256]{1,0:T(8,128)(2,1)S(1)}, u32[]{:S(2)}, u32[]{:S(2)}) collective-permute-start(bf16[544,256]{1,0:T(8,128)(2,1)S(1)} %get-tuple-element.39), channel_id=1, source_target_pairs={{0,1},{1,0},{2,3},{3,2},{4,5},{5,4},{6,7},{7,6},{8,9},{9,8},{10,11... | collective-permute-start | bytes 835592 | tf_op jit(solution)/shard_map/ppermute | solution.py:494
  25.1 2.4 %collective-permute-done.1.refs_0_.refs_2_ = bf16[2,256,512]{2,1,0:T(8,128)(2,1)S(1)} collective-permute-done((bf16[2,256,512]{2,1,0:T(8,128)(2,1)S(1)}, bf16[2,256,512]{2,1,0:T(8,128)(2,1)S(1)}, u32[]{:S(2)}, u32[]{:S(2)}) %collective-permute-start.1) | collective-permute-done | bytes 524320 | tf_op jit(solution)/shard_map/ppermute | solution.py:473
  27.6 0.0 collective-permute-done.2.refs_7_
  27.6 2.5 %pair01.1 = (f32[2,2,128,256]{3,2,1,0:T(8,128)S(1)}, bf16[544,256]{1,0:T(8,128)(2,1)S(1)}, f32[8,512]{1,0:T(8,128)S(1)}) custom-call(f32[8,128]{1,0:T(8,128)S(1)} %order1.1._, s32[3]{0:T(128)S(1)} %pad_add_fusion.pos_ref.refs_0_, s32[1,4]{1,0:T(1,128)S(1)} %copy-done.1, bf16[2,4,512,256]{3,2,1,0:T(8,128)(2,1)S(1)} %bitcast.7, ...), custom_call_target="tpu_custom_call" | custom-call | bytes 2097152 | tf_op jit(solution)/shard_map/pair01/pallas_call | solution.py:435
  30.1 2.8 %collective-permute-start.6 = (bf16[544,256]{1,0:T(8,128)(2,1)S(1)}, bf16[544,256]{1,0:T(8,128)(2,1)S(1)}, u32[]{:S(2)}, u32[]{:S(2)}) collective-permute-start(bf16[544,256]{1,0:T(8,128)(2,1)S(1)} %get-tuple-element.40), channel_id=1, source_target_pairs={{0,1},{1,0},{2,3},{3,2},{4,5},{5,4},{6,7},{7,6},{8,9},{9,8},{10,11... | collective-permute-start | bytes 835592 | tf_op jit(solution)/shard_map/ppermute | solution.py:494
  32.9 0.0 collective-permute-done.3.refs_3_
  32.9 2.3 %pair10.1 = (f32[2,2,128,256]{3,2,1,0:T(8,128)S(1)}, bf16[544,256]{1,0:T(8,128)(2,1)S(1)}, f32[8,512]{1,0:T(8,128)S(1)}) custom-call(f32[2,2,128,256]{3,2,1,0:T(8,128)S(1)} %get-tuple-element.31._.refs_4_, s32[3]{0:T(128)S(1)} %pad_add_fusion.pos_ref.refs_0_, s32[1,4]{1,0:T(1,128)S(1)} %copy-done.1, bf16[2,4,512,256]{3,2,1,0:T(8,128)(2,1)S(1)} %bitcast.8, ...), custom_call_target="tpu_custom_call" | custom-call | bytes 2097152 | tf_op jit(solution)/shard_map/pair10/pallas_call | solution.py:435
  35.2 2.5 %collective-permute-start.7 = (bf16[544,256]{1,0:T(8,128)(2,1)S(1)}, bf16[544,256]{1,0:T(8,128)(2,1)S(1)}, u32[]{:S(2)}, u32[]{:S(2)}) collective-permute-start(bf16[544,256]{1,0:T(8,128)(2,1)S(1)} %get-tuple-element.41), channel_id=1, source_target_pairs={{0,1},{1,0},{2,3},{3,2},{4,5},{5,4},{6,7},{7,6},{8,9},{9,8},{10,11... | collective-permute-start | bytes 835592 | tf_op jit(solution)/shard_map/ppermute | solution.py:494
  37.7 2.3 %pair11.1 = (f32[2,2,128,256]{3,2,1,0:T(8,128)S(1)}, bf16[544,256]{1,0:T(8,128)(2,1)S(1)}, f32[8,512]{1,0:T(8,128)S(1)}) custom-call(f32[2,2,128,256]{3,2,1,0:T(8,128)S(1)} %get-tuple-element.34._.refs_3_, s32[3]{0:T(128)S(1)} %pad_add_fusion.pos_ref.refs_0_, s32[1,4]{1,0:T(1,128)S(1)} %copy-done.1, bf16[2,4,512,256]{3,2,1,0:T(8,128)(2,1)S(1)} %bitcast.9, ...), custom_call_target="tpu_custom_call" | custom-call | bytes 2097152 | tf_op jit(solution)/shard_map/pair11/pallas_call | solution.py:435
  40.0 2.8 %collective-permute-start.4 = (bf16[544,256]{1,0:T(8,128)(2,1)S(1)}, bf16[544,256]{1,0:T(8,128)(2,1)S(1)}, u32[]{:S(2)}, u32[]{:S(2)}) collective-permute-start(bf16[544,256]{1,0:T(8,128)(2,1)S(1)} %get-tuple-element.38), channel_id=1, source_target_pairs={{0,1},{1,0},{2,3},{3,2},{4,5},{5,4},{6,7},{7,6},{8,9},{9,8},{10,11... | collective-permute-start | bytes 835592 | tf_op jit(solution)/shard_map/ppermute | solution.py:494
  42.8 0.0 collective-permute-done.5.refs_5_.refs_4_
  42.8 0.0 collective-permute-done.6.refs_6_
  42.8 1.7 %decode0.1._.refs_5_ = bf16[2,2,2,128,256]{4,3,2,1,0:T(8,128)(2,1)S(1)} custom-call(f32[2,2,128,256]{3,2,1,0:T(8,128)S(1)} %get-tuple-element.37._.kept_ref, s32[3]{0:T(128)S(1)} %pad_add_fusion.pos_ref.refs_0_, f32[8,512]{1,0:T(8,128)S(1)} %get-tuple-element.25.refs_5_.refs_1_.own_m.refs_3_, f32[8,512]{1,0:T(8,128)S(1)} %get-tuple-element.33.refs_6_.refs_2_, ...), custom_call_target="tpu_custom_call" | custom-call | bytes 2097152 | tf_op jit(solution)/shard_map/decode0/pallas_call | solution.py:435
  44.6 1.9 %collective-permute-start.8 = (bf16[2,2,2,128,256]{4,3,2,1,0:T(8,128)(2,1)S(1)}, bf16[2,2,2,128,256]{4,3,2,1,0:T(8,128)(2,1)S(1)}, u32[]{:S(2)}, u32[]{:S(2)}) collective-permute-start(bf16[2,2,2,128,256]{4,3,2,1,0:T(8,128)(2,1)S(1)} %decode0.1._.refs_5_), channel_id=1, source_target_pairs={{12,4},{20,12},{28,20},{36,28},{44,36},{52,44},{60,52},{68,60},{76... | collective-permute-start | bytes 1572872 | tf_op jit(solution)/shard_map/ppermute | solution.py:516
  46.5 0.0 collective-permute-done.7.refs_4_
  46.5 1.1 %decode1.1.done_ref = bf16[1,2,2,128,256]{4,3,2,1,0:T(8,128)(2,1)S(1)} custom-call(bf16[2,2,2,128,256]{4,3,2,1,0:T(8,128)(2,1)S(1)} %decode0.1._.refs_5_, s32[3]{0:T(128)S(1)} %pad_add_fusion.pos_ref.refs_0_, f32[8,512]{1,0:T(8,128)S(1)} %get-tuple-element.25.refs_5_.refs_1_.own_m.refs_3_, f32[8,512]{1,0:T(8,128)S(1)} %get-tuple-element.35.refs_6_.refs_2_, ...), custom_call_target="tpu_custom_call" | custom-call | bytes 2097152 | tf_op jit(solution)/shard_map/decode1/pallas_call | solution.py:435
  47.6 3.5 %collective-permute-done.4.got_ref = bf16[544,256]{1,0:T(8,128)(2,1)S(1)} collective-permute-done((bf16[544,256]{1,0:T(8,128)(2,1)S(1)}, bf16[544,256]{1,0:T(8,128)(2,1)S(1)}, u32[]{:S(2)}, u32[]{:S(2)}) %collective-permute-start.4) | collective-permute-done | bytes 278560 | tf_op jit(solution)/shard_map/ppermute | solution.py:494
  51.1 1.2 %decode2.1._.fin_ref = bf16[2,2,2,128,256]{4,3,2,1,0:T(8,128)(2,1)S(1)} custom-call(s32[3]{0:T(128)S(1)} %pad_add_fusion.pos_ref.refs_0_, f32[8,512]{1,0:T(8,128)S(1)} %get-tuple-element.25.refs_5_.refs_1_.own_m.refs_3_, f32[8,512]{1,0:T(8,128)S(1)} %get-tuple-element.36.pair_m, f32[2,2,128,256]{3,2,1,0:T(8,128)S(1)} %get-tuple-element.37._.kept_ref, ...), custom_call_target="tpu_custom_call" | custom-call | bytes 2097152 | tf_op jit(solution)/shard_map/decode2/pallas_call | solution.py:518
  52.3 1.9 %collective-permute-start.9 = (bf16[2,2,2,128,256]{4,3,2,1,0:T(8,128)(2,1)S(1)}, bf16[2,2,2,128,256]{4,3,2,1,0:T(8,128)(2,1)S(1)}, u32[]{:S(2)}, u32[]{:S(2)}) collective-permute-start(bf16[2,2,2,128,256]{4,3,2,1,0:T(8,128)(2,1)S(1)} %decode2.1._.fin_ref), channel_id=1, source_target_pairs={{12,4},{20,12},{28,20},{36,28},{44,36},{52,44},{60,52},{68,60},{76... | collective-permute-start | bytes 1572872 | tf_op jit(solution)/shard_map/ppermute | solution.py:525
  54.2 3.6 %collective-permute-done.8.refs_6_ = bf16[2,2,2,128,256]{4,3,2,1,0:T(8,128)(2,1)S(1)} collective-permute-done((bf16[2,2,2,128,256]{4,3,2,1,0:T(8,128)(2,1)S(1)}, bf16[2,2,2,128,256]{4,3,2,1,0:T(8,128)(2,1)S(1)}, u32[]{:S(2)}, u32[]{:S(2)}) %collective-permute-start.8) | collective-permute-done | bytes 524320 | tf_op jit(solution)/shard_map/ppermute | solution.py:516
  57.8 2.4 %finish.1.out_in_ref = bf16[2,1,3,256,512]{4,3,2,1,0:T(8,128)(2,1)} custom-call(bf16[2,2,2,128,256]{4,3,2,1,0:T(8,128)(2,1)S(1)} %decode2.1._.fin_ref, s32[3]{0:T(128)S(1)} %pad_add_fusion.pos_ref.refs_0_, f32[2,256,512]{2,1,0:T(8,128)S(1)} %get-tuple-element.42.refs_1_, bf16[2,256,512]{2,1,0:T(8,128)(2,1)S(1)} %collective-permute-done.1.refs_0_.refs_2_, ...), custom_call_target="tpu_custom_call" | custom-call | bytes 2097152 | tf_op jit(solution)/shard_map/finish/pallas_call | solution.py:435
  60.2 5.3 %collective-permute-done.9.back_ref = bf16[2,2,2,128,256]{4,3,2,1,0:T(8,128)(2,1)S(1)} collective-permute-done((bf16[2,2,2,128,256]{4,3,2,1,0:T(8,128)(2,1)S(1)}, bf16[2,2,2,128,256]{4,3,2,1,0:T(8,128)(2,1)S(1)}, u32[]{:S(2)}, u32[]{:S(2)}) %collective-permute-start.9) | collective-permute-done | bytes 524320 | tf_op jit(solution)/shard_map/ppermute | solution.py:525
  65.5 1.5 %place.1 = bf16[2,1,3,256,512]{4,3,2,1,0:T(8,128)(2,1)} custom-call(s32[3]{0:T(128)S(1)} %pad_add_fusion.pos_ref.refs_0_, bf16[2,1,3,256,512]{4,3,2,1,0:T(8,128)(2,1)} %finish.1.out_in_ref, bf16[2,2,2,128,256]{4,3,2,1,0:T(8,128)(2,1)S(1)} %decode2.1._.fin_ref, ...), custom_call_target="tpu_custom_call", output_to_operand_aliasing={{}: (1, {})} | custom-call | bytes 2097152 | tf_op jit(solution)/shard_map/place/pallas_call | solution.py:541
  (2 shorter events, 0.0 us)
Async XLA Ops:
  0.0 7.2 %copy-start = (bf16[2,1,4,512,256]{4,3,2,1,0:T(8,128)(2,1)S(1)}, bf16[2,1,4,512,256]{4,3,2,1,0:T(8,128)(2,1)}, u32[]{:S(2)}) copy-start(bf16[2,1,4,512,256]{4,3,2,1,0:T(8,128)(2,1)} %param.2) | copy-start | bytes 6291460
  0.1 0.8 %copy-start.1 = (s32[1,4]{1,0:T(1,128)S(1)}, s32[1,4]{1,0:T(1,128)}, u32[]{:S(2)}) copy-start(s32[1,4]{1,0:T(1,128)} %refs_1_.7) | copy-start | bytes 52
  2.8 17.5 %collective-permute-start = (bf16[2064,256]{1,0:T(8,128)(2,1)S(1)}, bf16[2064,256]{1,0:T(8,128)(2,1)S(1)}, u32[]{:S(2)}, u32[]{:S(2)}) collective-permute-start(bf16[2064,256]{1,0:T(8,128)(2,1)S(1)} %get-tuple-element.26), channel_id=1, source_target_pairs={{8,0},{16,8},{24,16},{32,24},{40,32},{48,40},{56,48},{64,56},{72,6... | collective-permute-start | bytes 3170312 | tf_op jit(solution)/shard_map/ppermute | solution.py:460
  12.4 15.2 %collective-permute-start.1 = (bf16[2,256,512]{2,1,0:T(8,128)(2,1)S(1)}, bf16[2,256,512]{2,1,0:T(8,128)(2,1)S(1)}, u32[]{:S(2)}, u32[]{:S(2)}) collective-permute-start(bf16[2,256,512]{2,1,0:T(8,128)(2,1)S(1)} %get-tuple-element.28), channel_id=1, source_target_pairs={{0,1},{1,0},{2,3},{3,2},{4,5},{5,4},{6,7},{7,6},{8,9},{9,8},{10,11... | collective-permute-start | bytes 1572872 | tf_op jit(solution)/shard_map/ppermute | solution.py:473
  15.2 17.7 %collective-permute-start.3 = (bf16[2048,256]{1,0:T(8,128)(2,1)S(1)}, bf16[2048,256]{1,0:T(8,128)(2,1)S(1)}, u32[]{:S(2)}, u32[]{:S(2)}) collective-permute-start(bf16[2048,256]{1,0:T(8,128)(2,1)S(1)} %get-tuple-element.32), channel_id=1, source_target_pairs={{8,0},{16,8},{24,16},{32,24},{40,32},{48,40},{56,48},{64,56},{72,6... | collective-permute-start | bytes 3145736 | tf_op jit(solution)/shard_map/ppermute | solution.py:474
  18.4 9.2 %collective-permute-start.2 = (bf16[2,4,512,256]{3,2,1,0:T(8,128)(2,1)S(1)}, bf16[2,4,512,256]{3,2,1,0:T(8,128)(2,1)S(1)}, u32[]{:S(2)}, u32[]{:S(2)}) collective-permute-start(bf16[2,4,512,256]{3,2,1,0:T(8,128)(2,1)S(1)} %get-tuple-element.30), channel_id=1, source_target_pairs={{0,4},{4,0},{8,12},{12,8},{16,20},{20,16},{24,28},{28,24},{32,36},... | collective-permute-start | bytes 6291464 | tf_op jit(solution)/shard_map/ppermute | solution.py:475
  22.7 20.2 %collective-permute-start.5 = (bf16[544,256]{1,0:T(8,128)(2,1)S(1)}, bf16[544,256]{1,0:T(8,128)(2,1)S(1)}, u32[]{:S(2)}, u32[]{:S(2)}) collective-permute-start(bf16[544,256]{1,0:T(8,128)(2,1)S(1)} %get-tuple-element.39), channel_id=1, source_target_pairs={{0,1},{1,0},{2,3},{3,2},{4,5},{5,4},{6,7},{7,6},{8,9},{9,8},{10,11... | collective-permute-start | bytes 835592 | tf_op jit(solution)/shard_map/ppermute | solution.py:494
  30.1 12.7 %collective-permute-start.6 = (bf16[544,256]{1,0:T(8,128)(2,1)S(1)}, bf16[544,256]{1,0:T(8,128)(2,1)S(1)}, u32[]{:S(2)}, u32[]{:S(2)}) collective-permute-start(bf16[544,256]{1,0:T(8,128)(2,1)S(1)} %get-tuple-element.40), channel_id=1, source_target_pairs={{0,1},{1,0},{2,3},{3,2},{4,5},{5,4},{6,7},{7,6},{8,9},{9,8},{10,11... | collective-permute-start | bytes 835592 | tf_op jit(solution)/shard_map/ppermute | solution.py:494
  35.2 11.3 %collective-permute-start.7 = (bf16[544,256]{1,0:T(8,128)(2,1)S(1)}, bf16[544,256]{1,0:T(8,128)(2,1)S(1)}, u32[]{:S(2)}, u32[]{:S(2)}) collective-permute-start(bf16[544,256]{1,0:T(8,128)(2,1)S(1)} %get-tuple-element.41), channel_id=1, source_target_pairs={{0,1},{1,0},{2,3},{3,2},{4,5},{5,4},{6,7},{7,6},{8,9},{9,8},{10,11... | collective-permute-start | bytes 835592 | tf_op jit(solution)/shard_map/ppermute | solution.py:494
  40.0 11.1 %collective-permute-start.4 = (bf16[544,256]{1,0:T(8,128)(2,1)S(1)}, bf16[544,256]{1,0:T(8,128)(2,1)S(1)}, u32[]{:S(2)}, u32[]{:S(2)}) collective-permute-start(bf16[544,256]{1,0:T(8,128)(2,1)S(1)} %get-tuple-element.38), channel_id=1, source_target_pairs={{0,1},{1,0},{2,3},{3,2},{4,5},{5,4},{6,7},{7,6},{8,9},{9,8},{10,11... | collective-permute-start | bytes 835592 | tf_op jit(solution)/shard_map/ppermute | solution.py:494
  44.6 13.2 %collective-permute-start.8 = (bf16[2,2,2,128,256]{4,3,2,1,0:T(8,128)(2,1)S(1)}, bf16[2,2,2,128,256]{4,3,2,1,0:T(8,128)(2,1)S(1)}, u32[]{:S(2)}, u32[]{:S(2)}) collective-permute-start(bf16[2,2,2,128,256]{4,3,2,1,0:T(8,128)(2,1)S(1)} %decode0.1._.refs_5_), channel_id=1, source_target_pairs={{12,4},{20,12},{28,20},{36,28},{44,36},{52,44},{60,52},{68,60},{76... | collective-permute-start | bytes 1572872 | tf_op jit(solution)/shard_map/ppermute | solution.py:516
  52.3 13.2 %collective-permute-start.9 = (bf16[2,2,2,128,256]{4,3,2,1,0:T(8,128)(2,1)S(1)}, bf16[2,2,2,128,256]{4,3,2,1,0:T(8,128)(2,1)S(1)}, u32[]{:S(2)}, u32[]{:S(2)}) collective-permute-start(bf16[2,2,2,128,256]{4,3,2,1,0:T(8,128)(2,1)S(1)} %decode2.1._.fin_ref), channel_id=1, source_target_pairs={{12,4},{20,12},{28,20},{36,28},{44,36},{52,44},{60,52},{68,60},{76... | collective-permute-start | bytes 1572872 | tf_op jit(solution)/shard_map/ppermute | solution.py:525

commit v8 on v6

--- a/solution.py
+++ b/solution.py
@@ -79,11 +79,16 @@
 
 
 def complex_product(left, right_re, right_im):
-    dims = (((1,), (1,)), ((), ()))
-    with_re = lax.dot_general(left, right_re, dims, preferred_element_type=jnp.float32)
-    with_im = lax.dot_general(left, right_im, dims, preferred_element_type=jnp.float32)
     rows = left.shape[0] // 2
-    return with_re[:rows] + with_im[rows:], with_re[rows:] - with_im[:rows]
+    real, imag = left[:rows], left[rows:]
+    both = jnp.concatenate(
+        [jnp.concatenate([real, imag], axis=1), jnp.concatenate([imag, -real], axis=1)], axis=0
+    )
+    right = jnp.concatenate([right_re, right_im], axis=1)
+    product = lax.dot_general(
+        both, right, (((1,), (1,)), ((), ())), preferred_element_type=jnp.float32
+    )
+    return product[:rows], product[rows:]
 
 
 def live_before(band_ref, tile):
@@ -128,19 +133,13 @@
     token_ref[...] = jnp.zeros_like(token_ref)
 
 
-def second_kernel(own_ref, chunk1_ref, sem):
-    run(
-        [
-            pltpu.make_async_copy(
-                own_ref.at[part, d, pl.ds(half * HALF + CR, CR), :],
-                chunk1_ref.at[pl.ds(((part * BAND + d) * 2 + half) * CR, CR), :],
-                sem.at[(part * BAND + d) * 2 + half],
-            )
-            for part in range(2)
-            for d in range(BAND)
-            for half in range(2)
-        ]
-    )
+def second_kernel(own_ref, chunk1_ref):
+    for part in range(2):
+        for d in range(BAND):
+            for half in range(2):
+                row = ((part * BAND + d) * 2 + half) * CR
+                start = half * HALF + CR
+                chunk1_ref[row : row + CR, :] = own_ref[part, d, start : start + CR, :]
 
 
 def self_kernel(
@@ -468,7 +467,6 @@
         second_kernel,
         [((ROWS, HALF), bf16)],
         [VMEM],
-        [pltpu.SemaphoreType.DMA((16,))],
         after=given_self,
     )(own)
     far1 = lax.ppermute(chunk1, "rows", far_route)

time: 64.1 us -> 64 us (level)
  waiting for transfers between devices: 7.82 us -> 9.86 us
  Pallas kernels: 24.2 us -> 22.6 us
    pallas_call x11, Pallas kernels: 21 us -> 19.4 us  [call(): return run if after is None else lambda *args: run(after, *args)]
    ppermute x3, starting transfers between devices: 7.17 us -> 5.76 us  [finished(): return (fin, lax.ppermute(fin, 'rows', back_route))]
    ppermute x3, waiting for transfers between devices: 5.86 us -> 7.2 us  [finished(): return (fin, lax.ppermute(fin, 'rows', back_route))]
    ppermute x4, starting transfers between devices: 10.6 us -> 11.4 us  [shards(): units[j, unit] = (kept, lax.ppermute(given, 'freq', swap), pair_m)]
  transfers between devices with their start and end apart: 11 -> 11, of which waited for: 4 -> 4; matrix products, arithmetic and copies ran while one was open for 0% -> 0% of each run, Pallas kernels for 33% -> 30%
where the time goes in v8:
time: 64 us; the launch traced here: 63.6 us
  starting transfers between devices  29.8 us (47%)
  Pallas kernels  22.6 us (35%)
  waiting for transfers between devices  9.86 us (15%)
  local copies, waits for them, and re-layouts  0.79 us (1%)
    pallas_call x11, Pallas kernels, call(): return run if after is None else lambda *args: run(after, *args)  19.4 us
    ppermute x4, starting transfers between devices, shards(): units[j, unit] = (kept, lax.ppermute(given, 'freq', swap), pair_m)  11.4 us
    ppermute x3, waiting for transfers between devices, finished(): return (fin, lax.ppermute(fin, 'rows', back_route))  7.2 us
    ppermute x3, starting transfers between devices, finished(): return (fin, lax.ppermute(fin, 'rows', back_route))  5.76 us
    ppermute x1, starting transfers between devices, shards(): far0 = lax.ppermute(chunk0, 'rows', far_route)  4.42 us
    ppermute x1, starting transfers between devices, shards(): far1 = lax.ppermute(chunk1, 'rows', far_route)  3.21 us
    ppermute x1, starting transfers between devices, shards(): got_self = lax.ppermute(given_self, 'freq', swap)  3.12 us
    pallas_call x1, Pallas kernels, shards(): call('pack', pack_kernel, [((ROWS + 16, HALF), bf16), token], [SMEM, ANY,...  1.93 us
  transfers between devices with their start and end apart: 11, of which 4 were waited for; matrix products, arithmetic and copies ran while one was open for 0% of the time, Pallas kernels for 30%

profile of v8, /device:TPU:249, one launch (start us, length us, event | category | flops | bytes accessed | tf_op | source)
XLA Modules:
  0.0 63.6 jit_solution(9642438439460450447)
XLA Ops:
  0.0 0.0 copy-start
  0.0 0.1 pad_add_fusion.pos_ref.refs_0_
  0.1 0.0 copy-start.1
  0.1 0.8 %copy-done.1 = s32[1,4]{1,0:T(1,128)S(1)} copy-done((s32[1,4]{1,0:T(1,128)S(1)}, s32[1,4]{1,0:T(1,128)}, u32[]{:S(2)}) %copy-start.1) | copy-done | bytes 40
  0.9 1.9 %pack.1 = (bf16[2064,256]{1,0:T(8,128)(2,1)S(1)}, f32[8,128]{1,0:T(8,128)S(1)}) custom-call(s32[3]{0:T(128)S(1)} %pad_add_fusion.pos_ref.refs_0_, s32[1,4]{1,0:T(1,128)S(1)} %copy-done.1, bf16[2,4,512,256]{3,2,1,0:T(8,128)(2,1)} %bitcast.4), custom_call_target="tpu_custom_call" | custom-call | bytes 2097152 | tf_op jit(solution)/shard_map/pack/pallas_call | solution.py:443
  2.8 4.4 %collective-permute-start = (bf16[2064,256]{1,0:T(8,128)(2,1)S(1)}, bf16[2064,256]{1,0:T(8,128)(2,1)S(1)}, u32[]{:S(2)}, u32[]{:S(2)}) collective-permute-start(bf16[2064,256]{1,0:T(8,128)(2,1)S(1)} %get-tuple-element.23), channel_id=1, source_target_pairs={{8,0},{16,8},{24,16},{32,24},{40,32},{48,40},{56,48},{64,56},{72,6... | collective-permute-start | bytes 3170312 | tf_op jit(solution)/shard_map/ppermute | solution.py:451
  7.2 0.0 copy-done
  7.2 3.5 %self.1 = (f32[2,256,512]{2,1,0:T(8,128)S(1)}, bf16[2,256,512]{2,1,0:T(8,128)(2,1)S(1)}, f32[8,512]{1,0:T(8,128)S(1)}, bf16[2,4,512,256]{3,2,1,0:T(8,128)(2,1)S(1)}) custom-call(f32[8,128]{1,0:T(8,128)S(1)} %get-tuple-element.24._, s32[3]{0:T(128)S(1)} %pad_add_fusion.pos_ref.refs_0_, bf16[2,4,512,256]{3,2,1,0:T(8,128)(2,1)S(1)} %bitcast.5), custom_call_target="tpu_custom_call" | custom-call | bytes 2097152 | tf_op jit(solution)/shard_map/self/pallas_call | solution.py:426
  10.8 3.1 %collective-permute-start.1 = (bf16[2,256,512]{2,1,0:T(8,128)(2,1)S(1)}, bf16[2,256,512]{2,1,0:T(8,128)(2,1)S(1)}, u32[]{:S(2)}, u32[]{:S(2)}) collective-permute-start(bf16[2,256,512]{2,1,0:T(8,128)(2,1)S(1)} %get-tuple-element.27._), channel_id=1, source_target_pairs={{0,1},{1,0},{2,3},{3,2},{4,5},{5,4},{6,7},{7,6},{8,9},{9,8},{10,11... | collective-permute-start | bytes 1572872 | tf_op jit(solution)/shard_map/ppermute | solution.py:464
  13.9 0.1 second.1
  14.0 3.2 %collective-permute-start.3 = (bf16[2048,256]{1,0:T(8,128)(2,1)S(1)}, bf16[2048,256]{1,0:T(8,128)(2,1)S(1)}, u32[]{:S(2)}, u32[]{:S(2)}) collective-permute-start(bf16[2048,256]{1,0:T(8,128)(2,1)S(1)} %second.1), channel_id=1, source_target_pairs={{8,0},{16,8},{24,16},{32,24},{40,32},{48,40},{56,48},{64,56},{72,6... | collective-permute-start | bytes 3145736 | tf_op jit(solution)/shard_map/ppermute | solution.py:472
  17.2 1.9 %collective-permute-start.2 = (bf16[2,4,512,256]{3,2,1,0:T(8,128)(2,1)S(1)}, bf16[2,4,512,256]{3,2,1,0:T(8,128)(2,1)S(1)}, u32[]{:S(2)}, u32[]{:S(2)}) collective-permute-start(bf16[2,4,512,256]{3,2,1,0:T(8,128)(2,1)S(1)} %get-tuple-element.29), channel_id=1, source_target_pairs={{0,4},{4,0},{8,12},{12,8},{16,20},{20,16},{24,28},{28,24},{32,36},... | collective-permute-start | bytes 6291464 | tf_op jit(solution)/shard_map/ppermute | solution.py:473
  19.1 0.0 collective-permute-done.refs_0_.refs_3_.refs_4_
  19.2 2.3 %pair00.1 = (f32[2,2,128,256]{3,2,1,0:T(8,128)S(1)}, bf16[544,256]{1,0:T(8,128)(2,1)S(1)}, f32[8,512]{1,0:T(8,128)S(1)}) custom-call(f32[8,128]{1,0:T(8,128)S(1)} %order.1._, s32[3]{0:T(128)S(1)} %pad_add_fusion.pos_ref.refs_0_, s32[1,4]{1,0:T(1,128)S(1)} %copy-done.1, bf16[2,4,512,256]{3,2,1,0:T(8,128)(2,1)S(1)} %bitcast.7, ...), custom_call_target="tpu_custom_call" | custom-call | bytes 2097152 | tf_op jit(solution)/shard_map/pair00/pallas_call | solution.py:426
  21.4 3.0 %collective-permute-start.4 = (bf16[544,256]{1,0:T(8,128)(2,1)S(1)}, bf16[544,256]{1,0:T(8,128)(2,1)S(1)}, u32[]{:S(2)}, u32[]{:S(2)}) collective-permute-start(bf16[544,256]{1,0:T(8,128)(2,1)S(1)} %get-tuple-element.35), channel_id=1, source_target_pairs={{0,1},{1,0},{2,3},{3,2},{4,5},{5,4},{6,7},{7,6},{8,9},{9,8},{10,11... | collective-permute-start | bytes 835592 | tf_op jit(solution)/shard_map/ppermute | solution.py:492
  24.5 1.5 %collective-permute-done.1.refs_0_.refs_2_ = bf16[2,256,512]{2,1,0:T(8,128)(2,1)S(1)} collective-permute-done((bf16[2,256,512]{2,1,0:T(8,128)(2,1)S(1)}, bf16[2,256,512]{2,1,0:T(8,128)(2,1)S(1)}, u32[]{:S(2)}, u32[]{:S(2)}) %collective-permute-start.1) | collective-permute-done | bytes 524320 | tf_op jit(solution)/shard_map/ppermute | solution.py:464
  26.0 0.0 collective-permute-done.2.refs_7_
  26.0 2.5 %pair01.1 = (f32[2,2,128,256]{3,2,1,0:T(8,128)S(1)}, bf16[544,256]{1,0:T(8,128)(2,1)S(1)}, f32[8,512]{1,0:T(8,128)S(1)}) custom-call(f32[8,128]{1,0:T(8,128)S(1)} %order1.1._, s32[3]{0:T(128)S(1)} %pad_add_fusion.pos_ref.refs_0_, s32[1,4]{1,0:T(1,128)S(1)} %copy-done.1, bf16[2,4,512,256]{3,2,1,0:T(8,128)(2,1)S(1)} %bitcast.8, ...), custom_call_target="tpu_custom_call" | custom-call | bytes 2097152 | tf_op jit(solution)/shard_map/pair01/pallas_call | solution.py:426
  28.5 3.1 %collective-permute-start.5 = (bf16[544,256]{1,0:T(8,128)(2,1)S(1)}, bf16[544,256]{1,0:T(8,128)(2,1)S(1)}, u32[]{:S(2)}, u32[]{:S(2)}) collective-permute-start(bf16[544,256]{1,0:T(8,128)(2,1)S(1)} %get-tuple-element.36), channel_id=1, source_target_pairs={{0,1},{1,0},{2,3},{3,2},{4,5},{5,4},{6,7},{7,6},{8,9},{9,8},{10,11... | collective-permute-start | bytes 835592 | tf_op jit(solution)/shard_map/ppermute | solution.py:492
  31.6 0.0 collective-permute-done.3.refs_3_
  31.6 2.3 %pair10.1 = (f32[2,2,128,256]{3,2,1,0:T(8,128)S(1)}, bf16[544,256]{1,0:T(8,128)(2,1)S(1)}, f32[8,512]{1,0:T(8,128)S(1)}) custom-call(f32[2,2,128,256]{3,2,1,0:T(8,128)S(1)} %get-tuple-element.30._.refs_4_, s32[3]{0:T(128)S(1)} %pad_add_fusion.pos_ref.refs_0_, s32[1,4]{1,0:T(1,128)S(1)} %copy-done.1, bf16[2,4,512,256]{3,2,1,0:T(8,128)(2,1)S(1)} %bitcast.9, ...), custom_call_target="tpu_custom_call" | custom-call | bytes 2097152 | tf_op jit(solution)/shard_map/pair10/pallas_call | solution.py:426
  33.9 2.2 %collective-permute-start.6 = (bf16[544,256]{1,0:T(8,128)(2,1)S(1)}, bf16[544,256]{1,0:T(8,128)(2,1)S(1)}, u32[]{:S(2)}, u32[]{:S(2)}) collective-permute-start(bf16[544,256]{1,0:T(8,128)(2,1)S(1)} %get-tuple-element.37), channel_id=1, source_target_pairs={{0,1},{1,0},{2,3},{3,2},{4,5},{5,4},{6,7},{7,6},{8,9},{9,8},{10,11... | collective-permute-start | bytes 835592 | tf_op jit(solution)/shard_map/ppermute | solution.py:492
  36.1 2.1 %pair11.1 = (f32[2,2,128,256]{3,2,1,0:T(8,128)S(1)}, bf16[544,256]{1,0:T(8,128)(2,1)S(1)}, f32[8,512]{1,0:T(8,128)S(1)}) custom-call(f32[2,2,128,256]{3,2,1,0:T(8,128)S(1)} %get-tuple-element.32._.refs_3_, s32[3]{0:T(128)S(1)} %pad_add_fusion.pos_ref.refs_0_, s32[1,4]{1,0:T(1,128)S(1)} %copy-done.1, bf16[2,4,512,256]{3,2,1,0:T(8,128)(2,1)S(1)} %bitcast.10, ...), custom_call_target="tpu_custom_call" | custom-call | bytes 2097152 | tf_op jit(solution)/shard_map/pair11/pallas_call | solution.py:426
  38.2 3.1 %collective-permute-start.7 = (bf16[544,256]{1,0:T(8,128)(2,1)S(1)}, bf16[544,256]{1,0:T(8,128)(2,1)S(1)}, u32[]{:S(2)}, u32[]{:S(2)}) collective-permute-start(bf16[544,256]{1,0:T(8,128)(2,1)S(1)} %get-tuple-element.39), channel_id=1, source_target_pairs={{0,1},{1,0},{2,3},{3,2},{4,5},{5,4},{6,7},{7,6},{8,9},{9,8},{10,11... | collective-permute-start | bytes 835592 | tf_op jit(solution)/shard_map/ppermute | solution.py:492
  41.3 0.0 collective-permute-done.4.refs_5_.refs_4_
  41.3 0.0 collective-permute-done.5.refs_6_
  41.3 1.9 %decode0.1._.refs_5_ = bf16[2,2,2,128,256]{4,3,2,1,0:T(8,128)(2,1)S(1)} custom-call(f32[2,2,128,256]{3,2,1,0:T(8,128)S(1)} %get-tuple-element.34._.refs_3_, s32[3]{0:T(128)S(1)} %pad_add_fusion.pos_ref.refs_0_, f32[8,512]{1,0:T(8,128)S(1)} %get-tuple-element.25.refs_5_.refs_1_.refs_3_, f32[8,512]{1,0:T(8,128)S(1)} %get-tuple-element.31.refs_6_.refs_2_, ...), custom_call_target="tpu_custom_call" | custom-call | bytes 2097152 | tf_op jit(solution)/shard_map/decode0/pallas_call | solution.py:426
  43.2 1.9 %collective-permute-start.8 = (bf16[2,2,2,128,256]{4,3,2,1,0:T(8,128)(2,1)S(1)}, bf16[2,2,2,128,256]{4,3,2,1,0:T(8,128)(2,1)S(1)}, u32[]{:S(2)}, u32[]{:S(2)}) collective-permute-start(bf16[2,2,2,128,256]{4,3,2,1,0:T(8,128)(2,1)S(1)} %decode0.1._.refs_5_), channel_id=1, source_target_pairs={{12,4},{20,12},{28,20},{36,28},{44,36},{52,44},{60,52},{68,60},{76... | collective-permute-start | bytes 1572872 | tf_op jit(solution)/shard_map/ppermute | solution.py:508
  45.2 0.0 collective-permute-done.6.refs_4_
  45.2 1.1 %decode1.1._.refs_6_ = bf16[1,2,2,128,256]{4,3,2,1,0:T(8,128)(2,1)S(1)} custom-call(bf16[2,2,2,128,256]{4,3,2,1,0:T(8,128)(2,1)S(1)} %decode0.1._.refs_5_, s32[3]{0:T(128)S(1)} %pad_add_fusion.pos_ref.refs_0_, f32[8,512]{1,0:T(8,128)S(1)} %get-tuple-element.25.refs_5_.refs_1_.refs_3_, f32[8,512]{1,0:T(8,128)S(1)} %get-tuple-element.33.refs_6_.refs_2_, ...), custom_call_target="tpu_custom_call" | custom-call | bytes 2097152 | tf_op jit(solution)/shard_map/decode1/pallas_call | solution.py:426
  46.3 1.9 %collective-permute-start.9 = (bf16[1,2,2,128,256]{4,3,2,1,0:T(8,128)(2,1)S(1)}, bf16[1,2,2,128,256]{4,3,2,1,0:T(8,128)(2,1)S(1)}, u32[]{:S(2)}, u32[]{:S(2)}) collective-permute-start(bf16[1,2,2,128,256]{4,3,2,1,0:T(8,128)(2,1)S(1)} %decode1.1._.refs_6_), channel_id=1, source_target_pairs={{12,4},{20,12},{28,20},{36,28},{44,36},{52,44},{60,52},{68,60},{76... | collective-permute-start | bytes 786440 | tf_op jit(solution)/shard_map/ppermute | solution.py:508
  48.3 1.1 %collective-permute-done.7.refs_4_ = bf16[544,256]{1,0:T(8,128)(2,1)S(1)} collective-permute-done((bf16[544,256]{1,0:T(8,128)(2,1)S(1)}, bf16[544,256]{1,0:T(8,128)(2,1)S(1)}, u32[]{:S(2)}, u32[]{:S(2)}) %collective-permute-start.7) | collective-permute-done | bytes 278560 | tf_op jit(solution)/shard_map/ppermute | solution.py:492
  49.4 1.1 %decode2.1._.fin_ref = bf16[1,2,2,128,256]{4,3,2,1,0:T(8,128)(2,1)S(1)} custom-call(bf16[1,2,2,128,256]{4,3,2,1,0:T(8,128)(2,1)S(1)} %decode1.1._.refs_6_, s32[3]{0:T(128)S(1)} %pad_add_fusion.pos_ref.refs_0_, f32[8,512]{1,0:T(8,128)S(1)} %get-tuple-element.25.refs_5_.refs_1_.refs_3_, f32[8,512]{1,0:T(8,128)S(1)} %get-tuple-element.38.refs_2_, ...), custom_call_target="tpu_custom_call" | custom-call | bytes 2097152 | tf_op jit(solution)/shard_map/decode2/pallas_call | solution.py:426
  50.5 1.9 %collective-permute-start.10 = (bf16[1,2,2,128,256]{4,3,2,1,0:T(8,128)(2,1)S(1)}, bf16[1,2,2,128,256]{4,3,2,1,0:T(8,128)(2,1)S(1)}, u32[]{:S(2)}, u32[]{:S(2)}) collective-permute-start(bf16[1,2,2,128,256]{4,3,2,1,0:T(8,128)(2,1)S(1)} %decode2.1._.fin_ref), channel_id=1, source_target_pairs={{12,4},{20,12},{28,20},{36,28},{44,36},{52,44},{60,52},{68,60},{76... | collective-permute-start | bytes 786440 | tf_op jit(solution)/shard_map/ppermute | solution.py:508
  52.4 6.9 %collective-permute-done.9.refs_8_ = bf16[1,2,2,128,256]{4,3,2,1,0:T(8,128)(2,1)S(1)} collective-permute-done((bf16[1,2,2,128,256]{4,3,2,1,0:T(8,128)(2,1)S(1)}, bf16[1,2,2,128,256]{4,3,2,1,0:T(8,128)(2,1)S(1)}, u32[]{:S(2)}, u32[]{:S(2)}) %collective-permute-start.9) | collective-permute-done | bytes 262176 | tf_op jit(solution)/shard_map/ppermute | solution.py:508
  59.3 0.0 collective-permute-done.8.refs_7_
  59.3 2.5 %finish.1.out_in_ref = bf16[2,1,3,256,512]{4,3,2,1,0:T(8,128)(2,1)} custom-call(bf16[1,2,2,128,256]{4,3,2,1,0:T(8,128)(2,1)S(1)} %decode2.1._.fin_ref, s32[3]{0:T(128)S(1)} %pad_add_fusion.pos_ref.refs_0_, f32[2,256,512]{2,1,0:T(8,128)S(1)} %get-tuple-element.40.refs_1_, bf16[2,256,512]{2,1,0:T(8,128)(2,1)S(1)} %collective-permute-done.1.refs_0_.refs_2_, ...), custom_call_target="tpu_custom_call" | custom-call | bytes 2097152 | tf_op jit(solution)/shard_map/finish/pallas_call | solution.py:426
  61.8 0.3 collective-permute-done.10.back_ref
  62.1 1.3 %place.1 = bf16[2,1,3,256,512]{4,3,2,1,0:T(8,128)(2,1)} custom-call(s32[3]{0:T(128)S(1)} %pad_add_fusion.pos_ref.refs_0_, bf16[2,1,3,256,512]{4,3,2,1,0:T(8,128)(2,1)} %finish.1.out_in_ref, bf16[1,2,2,128,256]{4,3,2,1,0:T(8,128)(2,1)S(1)} %decode2.1._.fin_ref, ...), custom_call_target="tpu_custom_call", output_to_operand_aliasing={{}: (1, {})} | custom-call | bytes 2097152 | tf_op jit(solution)/shard_map/place/pallas_call | solution.py:528
  (2 shorter events, 0.0 us)
Async XLA Ops:
  0.0 7.2 %copy-start = (bf16[2,1,4,512,256]{4,3,2,1,0:T(8,128)(2,1)S(1)}, bf16[2,1,4,512,256]{4,3,2,1,0:T(8,128)(2,1)}, u32[]{:S(2)}) copy-start(bf16[2,1,4,512,256]{4,3,2,1,0:T(8,128)(2,1)} %param.2) | copy-start | bytes 6291460
  0.1 0.8 %copy-start.1 = (s32[1,4]{1,0:T(1,128)S(1)}, s32[1,4]{1,0:T(1,128)}, u32[]{:S(2)}) copy-start(s32[1,4]{1,0:T(1,128)} %refs_1_.7) | copy-start | bytes 52
  2.8 16.3 %collective-permute-start = (bf16[2064,256]{1,0:T(8,128)(2,1)S(1)}, bf16[2064,256]{1,0:T(8,128)(2,1)S(1)}, u32[]{:S(2)}, u32[]{:S(2)}) collective-permute-start(bf16[2064,256]{1,0:T(8,128)(2,1)S(1)} %get-tuple-element.23), channel_id=1, source_target_pairs={{8,0},{16,8},{24,16},{32,24},{40,32},{48,40},{56,48},{64,56},{72,6... | collective-permute-start | bytes 3170312 | tf_op jit(solution)/shard_map/ppermute | solution.py:451
  10.8 15.2 %collective-permute-start.1 = (bf16[2,256,512]{2,1,0:T(8,128)(2,1)S(1)}, bf16[2,256,512]{2,1,0:T(8,128)(2,1)S(1)}, u32[]{:S(2)}, u32[]{:S(2)}) collective-permute-start(bf16[2,256,512]{2,1,0:T(8,128)(2,1)S(1)} %get-tuple-element.27._), channel_id=1, source_target_pairs={{0,1},{1,0},{2,3},{3,2},{4,5},{5,4},{6,7},{7,6},{8,9},{9,8},{10,11... | collective-permute-start | bytes 1572872 | tf_op jit(solution)/shard_map/ppermute | solution.py:464
  14.0 17.6 %collective-permute-start.3 = (bf16[2048,256]{1,0:T(8,128)(2,1)S(1)}, bf16[2048,256]{1,0:T(8,128)(2,1)S(1)}, u32[]{:S(2)}, u32[]{:S(2)}) collective-permute-start(bf16[2048,256]{1,0:T(8,128)(2,1)S(1)} %second.1), channel_id=1, source_target_pairs={{8,0},{16,8},{24,16},{32,24},{40,32},{48,40},{56,48},{64,56},{72,6... | collective-permute-start | bytes 3145736 | tf_op jit(solution)/shard_map/ppermute | solution.py:472
  17.2 8.8 %collective-permute-start.2 = (bf16[2,4,512,256]{3,2,1,0:T(8,128)(2,1)S(1)}, bf16[2,4,512,256]{3,2,1,0:T(8,128)(2,1)S(1)}, u32[]{:S(2)}, u32[]{:S(2)}) collective-permute-start(bf16[2,4,512,256]{3,2,1,0:T(8,128)(2,1)S(1)} %get-tuple-element.29), channel_id=1, source_target_pairs={{0,4},{4,0},{8,12},{12,8},{16,20},{20,16},{24,28},{28,24},{32,36},... | collective-permute-start | bytes 6291464 | tf_op jit(solution)/shard_map/ppermute | solution.py:473
  21.4 19.9 %collective-permute-start.4 = (bf16[544,256]{1,0:T(8,128)(2,1)S(1)}, bf16[544,256]{1,0:T(8,128)(2,1)S(1)}, u32[]{:S(2)}, u32[]{:S(2)}) collective-permute-start(bf16[544,256]{1,0:T(8,128)(2,1)S(1)} %get-tuple-element.35), channel_id=1, source_target_pairs={{0,1},{1,0},{2,3},{3,2},{4,5},{5,4},{6,7},{7,6},{8,9},{9,8},{10,11... | collective-permute-start | bytes 835592 | tf_op jit(solution)/shard_map/ppermute | solution.py:492
  28.5 12.8 %collective-permute-start.5 = (bf16[544,256]{1,0:T(8,128)(2,1)S(1)}, bf16[544,256]{1,0:T(8,128)(2,1)S(1)}, u32[]{:S(2)}, u32[]{:S(2)}) collective-permute-start(bf16[544,256]{1,0:T(8,128)(2,1)S(1)} %get-tuple-element.36), channel_id=1, source_target_pairs={{0,1},{1,0},{2,3},{3,2},{4,5},{5,4},{6,7},{7,6},{8,9},{9,8},{10,11... | collective-permute-start | bytes 835592 | tf_op jit(solution)/shard_map/ppermute | solution.py:492
  33.9 11.2 %collective-permute-start.6 = (bf16[544,256]{1,0:T(8,128)(2,1)S(1)}, bf16[544,256]{1,0:T(8,128)(2,1)S(1)}, u32[]{:S(2)}, u32[]{:S(2)}) collective-permute-start(bf16[544,256]{1,0:T(8,128)(2,1)S(1)} %get-tuple-element.37), channel_id=1, source_target_pairs={{0,1},{1,0},{2,3},{3,2},{4,5},{5,4},{6,7},{7,6},{8,9},{9,8},{10,11... | collective-permute-start | bytes 835592 | tf_op jit(solution)/shard_map/ppermute | solution.py:492
  38.2 11.2 %collective-permute-start.7 = (bf16[544,256]{1,0:T(8,128)(2,1)S(1)}, bf16[544,256]{1,0:T(8,128)(2,1)S(1)}, u32[]{:S(2)}, u32[]{:S(2)}) collective-permute-start(bf16[544,256]{1,0:T(8,128)(2,1)S(1)} %get-tuple-element.39), channel_id=1, source_target_pairs={{0,1},{1,0},{2,3},{3,2},{4,5},{5,4},{6,7},{7,6},{8,9},{9,8},{10,11... | collective-permute-start | bytes 835592 | tf_op jit(solution)/shard_map/ppermute | solution.py:492
  43.2 16.1 %collective-permute-start.8 = (bf16[2,2,2,128,256]{4,3,2,1,0:T(8,128)(2,1)S(1)}, bf16[2,2,2,128,256]{4,3,2,1,0:T(8,128)(2,1)S(1)}, u32[]{:S(2)}, u32[]{:S(2)}) collective-permute-start(bf16[2,2,2,128,256]{4,3,2,1,0:T(8,128)(2,1)S(1)} %decode0.1._.refs_5_), channel_id=1, source_target_pairs={{12,4},{20,12},{28,20},{36,28},{44,36},{52,44},{60,52},{68,60},{76... | collective-permute-start | bytes 1572872 | tf_op jit(solution)/shard_map/ppermute | solution.py:508
  46.3 13.0 %collective-permute-start.9 = (bf16[1,2,2,128,256]{4,3,2,1,0:T(8,128)(2,1)S(1)}, bf16[1,2,2,128,256]{4,3,2,1,0:T(8,128)(2,1)S(1)}, u32[]{:S(2)}, u32[]{:S(2)}) collective-permute-start(bf16[1,2,2,128,256]{4,3,2,1,0:T(8,128)(2,1)S(1)} %decode1.1._.refs_6_), channel_id=1, source_target_pairs={{12,4},{20,12},{28,20},{36,28},{44,36},{52,44},{60,52},{68,60},{76... | collective-permute-start | bytes 786440 | tf_op jit(solution)/shard_map/ppermute | solution.py:508
  50.5 11.6 %collective-permute-start.10 = (bf16[1,2,2,128,256]{4,3,2,1,0:T(8,128)(2,1)S(1)}, bf16[1,2,2,128,256]{4,3,2,1,0:T(8,128)(2,1)S(1)}, u32[]{:S(2)}, u32[]{:S(2)}) collective-permute-start(bf16[1,2,2,128,256]{4,3,2,1,0:T(8,128)(2,1)S(1)} %decode2.1._.fin_ref), channel_id=1, source_target_pairs={{12,4},{20,12},{28,20},{36,28},{44,36},{52,44},{60,52},{68,60},{76... | collective-permute-start | bytes 786440 | tf_op jit(solution)/shard_map/ppermute | solution.py:508

commit v9 on v8

--- a/solution.py
+++ b/solution.py
@@ -477,8 +477,24 @@
     after = call("order", order_kernel, [token], [ANY], flops=TCOST)(far0)
     units = {}
     pair_m = None
+    def finished(name, j, which, after):
+        kepts = [units[j, unit][0] for unit in which]
+        gots = [units[j, unit][1] for unit in which]
+        fin = call(
+            name,
+            lambda *refs: decode_kernel(j, which, *refs),
+            [((len(which), *unit_shape), bf16)],
+            [SMEM] + [VMEM] * (2 + 2 * len(which)),
+            [pltpu.VMEM((2, TS, 128), f32)],
+            after=after,
+        )(pos, message, units[j, which[-1]][2], *kepts, *gots)
+        return fin, lax.ppermute(fin, "rows", back_route)
+
     for j in range(CHUNKS):
         for unit in range(2):
+            if (j, unit) == (1, 1):
+                fin0, back0 = finished("decode0", 0, (0, 1), after)
+                after = fin0
             extra = [] if pair_m is None else [pair_m] + [near] * unit
             kept, given, pair_m = call(
                 f"pair{j}{unit}",
@@ -494,21 +510,7 @@
             if (j, unit) == (0, 0):
                 after = call("order1", order_kernel, [token], [ANY], flops=FCOST, after=kept)(got_self)
 
-    def finished(name, j, which, after):
-        kepts = [units[j, unit][0] for unit in which]
-        gots = [units[j, unit][1] for unit in which]
-        fin = call(
-            name,
-            lambda *refs: decode_kernel(j, which, *refs),
-            [((len(which), *unit_shape), bf16)],
-            [SMEM] + [VMEM] * (2 + 2 * len(which)),
-            [pltpu.VMEM((2, TS, 128), f32)],
-            after=after,
-        )(pos, message, units[j, which[-1]][2], *kepts, *gots)
-        return fin, lax.ppermute(fin, "rows", back_route)
-
-    fin0, back0 = finished("decode0", 0, (0, 1), after)
-    fin1, back1 = finished("decode1", 1, (0,), fin0)
+    fin1, back1 = finished("decode1", 1, (0,), after)
     fin2, back2 = finished("decode2", 1, (1,), fin1)
     out_shape = ((2, 1, 3, HALF, TS), bf16)
     out = call(

time: 64 us -> 65.7 us (1.027)
  the two profiles are of different devices: /device:TPU:249 before, /device:TPU:25 now
where the time goes in v9:
time: 65.7 us; the launch traced here: 64.6 us
  starting transfers between devices  34.8 us (53%)
  Pallas kernels  22.6 us (34%)
  waiting for transfers between devices  5.97 us (9%)
  local copies, waits for them, and re-layouts  0.8 us (1%)
    pallas_call x11, Pallas kernels, call(): return run if after is None else lambda *args: run(after, *args)  19.3 us
    ppermute x4, starting transfers between devices, shards(): units[j, unit] = (kept, lax.ppermute(given, 'freq', swap), pair_m)  12.9 us
    ppermute x3, starting transfers between devices, finished(): return (fin, lax.ppermute(fin, 'rows', back_route))  10.4 us
    ppermute x3, waiting for transfers between devices, finished(): return (fin, lax.ppermute(fin, 'rows', back_route))  4.16 us
    ppermute x1, starting transfers between devices, shards(): far0 = lax.ppermute(chunk0, 'rows', far_route)  3.2 us
    ppermute x1, starting transfers between devices, shards(): far1 = lax.ppermute(chunk1, 'rows', far_route)  3.2 us
    ppermute x1, starting transfers between devices, shards(): got_self = lax.ppermute(given_self, 'freq', swap)  3.12 us
    pallas_call x1, Pallas kernels, shards(): call('pack', pack_kernel, [((ROWS + 16, HALF), bf16), token], [SMEM, ANY,...  1.93 us
  transfers between devices with their start and end apart: 11, of which 5 were waited for; matrix products, arithmetic and copies ran while one was open for 0% of the time, Pallas kernels for 30%

profile of v9, /device:TPU:25, one launch (start us, length us, event | category | flops | bytes accessed | tf_op | source)
XLA Modules:
  0.0 64.6 jit_solution(115593510473226357)
XLA Ops:
  0.0 0.0 copy-start
  0.0 0.1 pad_add_fusion.pos_ref.refs_0_
  0.1 0.0 copy-start.1
  0.1 0.8 %copy-done.1 = s32[1,4]{1,0:T(1,128)S(1)} copy-done((s32[1,4]{1,0:T(1,128)S(1)}, s32[1,4]{1,0:T(1,128)}, u32[]{:S(2)}) %copy-start.1) | copy-done | bytes 40
  0.9 1.9 %pack.1 = (bf16[2064,256]{1,0:T(8,128)(2,1)S(1)}, f32[8,128]{1,0:T(8,128)S(1)}) custom-call(s32[3]{0:T(128)S(1)} %pad_add_fusion.pos_ref.refs_0_, s32[1,4]{1,0:T(1,128)S(1)} %copy-done.1, bf16[2,4,512,256]{3,2,1,0:T(8,128)(2,1)} %bitcast.4), custom_call_target="tpu_custom_call" | custom-call | bytes 2097152 | tf_op jit(solution)/shard_map/pack/pallas_call | solution.py:443
  2.8 3.2 %collective-permute-start = (bf16[2064,256]{1,0:T(8,128)(2,1)S(1)}, bf16[2064,256]{1,0:T(8,128)(2,1)S(1)}, u32[]{:S(2)}, u32[]{:S(2)}) collective-permute-start(bf16[2064,256]{1,0:T(8,128)(2,1)S(1)} %get-tuple-element.23), channel_id=1, source_target_pairs={{8,0},{16,8},{24,16},{32,24},{40,32},{48,40},{56,48},{64,56},{72,6... | collective-permute-start | bytes 3170312 | tf_op jit(solution)/shard_map/ppermute | solution.py:451
  6.0 0.0 copy-done
  6.0 3.5 %self.1 = (f32[2,256,512]{2,1,0:T(8,128)S(1)}, bf16[2,256,512]{2,1,0:T(8,128)(2,1)S(1)}, f32[8,512]{1,0:T(8,128)S(1)}, bf16[2,4,512,256]{3,2,1,0:T(8,128)(2,1)S(1)}) custom-call(f32[8,128]{1,0:T(8,128)S(1)} %get-tuple-element.24._, s32[3]{0:T(128)S(1)} %pad_add_fusion.pos_ref.refs_0_, bf16[2,4,512,256]{3,2,1,0:T(8,128)(2,1)S(1)} %bitcast.5), custom_call_target="tpu_custom_call" | custom-call | bytes 2097152 | tf_op jit(solution)/shard_map/self/pallas_call | solution.py:426
  9.6 3.1 %collective-permute-start.1 = (bf16[2,256,512]{2,1,0:T(8,128)(2,1)S(1)}, bf16[2,256,512]{2,1,0:T(8,128)(2,1)S(1)}, u32[]{:S(2)}, u32[]{:S(2)}) collective-permute-start(bf16[2,256,512]{2,1,0:T(8,128)(2,1)S(1)} %get-tuple-element.27._), channel_id=1, source_target_pairs={{0,1},{1,0},{2,3},{3,2},{4,5},{5,4},{6,7},{7,6},{8,9},{9,8},{10,11... | collective-permute-start | bytes 1572872 | tf_op jit(solution)/shard_map/ppermute | solution.py:464
  12.7 0.1 second.1
  12.8 3.2 %collective-permute-start.3 = (bf16[2048,256]{1,0:T(8,128)(2,1)S(1)}, bf16[2048,256]{1,0:T(8,128)(2,1)S(1)}, u32[]{:S(2)}, u32[]{:S(2)}) collective-permute-start(bf16[2048,256]{1,0:T(8,128)(2,1)S(1)} %second.1), channel_id=1, source_target_pairs={{8,0},{16,8},{24,16},{32,24},{40,32},{48,40},{56,48},{64,56},{72,6... | collective-permute-start | bytes 3145736 | tf_op jit(solution)/shard_map/ppermute | solution.py:472
  16.0 0.0 copy-start.2
  16.0 1.9 %collective-permute-start.2 = (bf16[2,4,512,256]{3,2,1,0:T(8,128)(2,1)S(1)}, bf16[2,4,512,256]{3,2,1,0:T(8,128)(2,1)S(1)}, u32[]{:S(2)}, u32[]{:S(2)}) collective-permute-start(bf16[2,4,512,256]{3,2,1,0:T(8,128)(2,1)S(1)} %get-tuple-element.29), channel_id=1, source_target_pairs={{0,4},{4,0},{8,12},{12,8},{16,20},{20,16},{24,28},{28,24},{32,36},... | collective-permute-start | bytes 6291464 | tf_op jit(solution)/shard_map/ppermute | solution.py:473
  17.9 0.8 %collective-permute-done.refs_0_.refs_3_.refs_4_ = bf16[2064,256]{1,0:T(8,128)(2,1)S(1)} collective-permute-done((bf16[2064,256]{1,0:T(8,128)(2,1)S(1)}, bf16[2064,256]{1,0:T(8,128)(2,1)S(1)}, u32[]{:S(2)}, u32[]{:S(2)}) %collective-permute-start) | collective-permute-done | bytes 1056800 | tf_op jit(solution)/shard_map/ppermute | solution.py:451
  18.7 0.0 copy-done.2
  18.7 2.3 %pair00.1 = (f32[2,2,128,256]{3,2,1,0:T(8,128)S(1)}, bf16[544,256]{1,0:T(8,128)(2,1)S(1)}, f32[8,512]{1,0:T(8,128)S(1)}) custom-call(f32[8,128]{1,0:T(8,128)S(1)} %order.1._, s32[3]{0:T(128)S(1)} %pad_add_fusion.pos_ref.refs_0_, s32[1,4]{1,0:T(1,128)S(1)} %copy-done.2, bf16[2,4,512,256]{3,2,1,0:T(8,128)(2,1)S(1)} %bitcast.7, ...), custom_call_target="tpu_custom_call" | custom-call | bytes 2097152 | tf_op jit(solution)/shard_map/pair00/pallas_call | solution.py:426
  21.0 3.1 %collective-permute-start.4 = (bf16[544,256]{1,0:T(8,128)(2,1)S(1)}, bf16[544,256]{1,0:T(8,128)(2,1)S(1)}, u32[]{:S(2)}, u32[]{:S(2)}) collective-permute-start(bf16[544,256]{1,0:T(8,128)(2,1)S(1)} %get-tuple-element.33), channel_id=1, source_target_pairs={{0,1},{1,0},{2,3},{3,2},{4,5},{5,4},{6,7},{7,6},{8,9},{9,8},{10,11... | collective-permute-start | bytes 835592 | tf_op jit(solution)/shard_map/ppermute | solution.py:508
  24.2 0.7 %collective-permute-done.1.refs_0_.refs_2_ = bf16[2,256,512]{2,1,0:T(8,128)(2,1)S(1)} collective-permute-done((bf16[2,256,512]{2,1,0:T(8,128)(2,1)S(1)}, bf16[2,256,512]{2,1,0:T(8,128)(2,1)S(1)}, u32[]{:S(2)}, u32[]{:S(2)}) %collective-permute-start.1) | collective-permute-done | bytes 524320 | tf_op jit(solution)/shard_map/ppermute | solution.py:464
  24.9 0.0 collective-permute-done.2.refs_7_
  24.9 2.5 %pair01.1 = (f32[2,2,128,256]{3,2,1,0:T(8,128)S(1)}, bf16[544,256]{1,0:T(8,128)(2,1)S(1)}, f32[8,512]{1,0:T(8,128)S(1)}) custom-call(f32[8,128]{1,0:T(8,128)S(1)} %order1.1._, s32[3]{0:T(128)S(1)} %pad_add_fusion.pos_ref.refs_0_, s32[1,4]{1,0:T(1,128)S(1)} %copy-done.2, bf16[2,4,512,256]{3,2,1,0:T(8,128)(2,1)S(1)} %bitcast.8, ...), custom_call_target="tpu_custom_call" | custom-call | bytes 2097152 | tf_op jit(solution)/shard_map/pair01/pallas_call | solution.py:426
  27.3 3.1 %collective-permute-start.5 = (bf16[544,256]{1,0:T(8,128)(2,1)S(1)}, bf16[544,256]{1,0:T(8,128)(2,1)S(1)}, u32[]{:S(2)}, u32[]{:S(2)}) collective-permute-start(bf16[544,256]{1,0:T(8,128)(2,1)S(1)} %get-tuple-element.34), channel_id=1, source_target_pairs={{0,1},{1,0},{2,3},{3,2},{4,5},{5,4},{6,7},{7,6},{8,9},{9,8},{10,11... | collective-permute-start | bytes 835592 | tf_op jit(solution)/shard_map/ppermute | solution.py:508
  30.5 0.0 collective-permute-done.3.refs_3_
  30.5 2.3 %pair10.1 = (f32[2,2,128,256]{3,2,1,0:T(8,128)S(1)}, bf16[544,256]{1,0:T(8,128)(2,1)S(1)}, f32[8,512]{1,0:T(8,128)S(1)}) custom-call(f32[2,2,128,256]{3,2,1,0:T(8,128)S(1)} %get-tuple-element.30._.refs_4_, s32[3]{0:T(128)S(1)} %pad_add_fusion.pos_ref.refs_0_, s32[1,4]{1,0:T(1,128)S(1)} %copy-done.2, bf16[2,4,512,256]{3,2,1,0:T(8,128)(2,1)S(1)} %bitcast.9, ...), custom_call_target="tpu_custom_call" | custom-call | bytes 2097152 | tf_op jit(solution)/shard_map/pair10/pallas_call | solution.py:426
  32.8 2.6 %collective-permute-start.6 = (bf16[544,256]{1,0:T(8,128)(2,1)S(1)}, bf16[544,256]{1,0:T(8,128)(2,1)S(1)}, u32[]{:S(2)}, u32[]{:S(2)}) collective-permute-start(bf16[544,256]{1,0:T(8,128)(2,1)S(1)} %get-tuple-element.37), channel_id=1, source_target_pairs={{0,1},{1,0},{2,3},{3,2},{4,5},{5,4},{6,7},{7,6},{8,9},{9,8},{10,11... | collective-permute-start | bytes 835592 | tf_op jit(solution)/shard_map/ppermute | solution.py:508
  35.4 0.0 collective-permute-done.4.refs_5_.refs_4_
  35.4 0.3 collective-permute-done.5.refs_6_
  35.7 1.7 %decode0.1._.refs_5_ = bf16[2,2,2,128,256]{4,3,2,1,0:T(8,128)(2,1)S(1)} custom-call(f32[2,2,128,256]{3,2,1,0:T(8,128)S(1)} %get-tuple-element.32._.refs_3_, s32[3]{0:T(128)S(1)} %pad_add_fusion.pos_ref.refs_0_, f32[8,512]{1,0:T(8,128)S(1)} %get-tuple-element.25.refs_5_.refs_1_.refs_3_, f32[8,512]{1,0:T(8,128)S(1)} %get-tuple-element.31.refs_6_.refs_2_, ...), custom_call_target="tpu_custom_call" | custom-call | bytes 2097152 | tf_op jit(solution)/shard_map/decode0/pallas_call | solution.py:426
  37.4 2.2 %pair11.1 = (f32[2,2,128,256]{3,2,1,0:T(8,128)S(1)}, bf16[544,256]{1,0:T(8,128)(2,1)S(1)}, f32[8,512]{1,0:T(8,128)S(1)}) custom-call(bf16[2,2,2,128,256]{4,3,2,1,0:T(8,128)(2,1)S(1)} %decode0.1._.refs_5_, s32[3]{0:T(128)S(1)} %pad_add_fusion.pos_ref.refs_0_, s32[1,4]{1,0:T(1,128)S(1)} %copy-done.2, bf16[2,4,512,256]{3,2,1,0:T(8,128)(2,1)S(1)} %bitcast.10, ...), custom_call_target="tpu_custom_call" | custom-call | bytes 2097152 | tf_op jit(solution)/shard_map/pair11/pallas_call | solution.py:426
  39.7 4.1 %collective-permute-start.7 = (bf16[544,256]{1,0:T(8,128)(2,1)S(1)}, bf16[544,256]{1,0:T(8,128)(2,1)S(1)}, u32[]{:S(2)}, u32[]{:S(2)}) collective-permute-start(bf16[544,256]{1,0:T(8,128)(2,1)S(1)} %get-tuple-element.39), channel_id=1, source_target_pairs={{0,1},{1,0},{2,3},{3,2},{4,5},{5,4},{6,7},{7,6},{8,9},{9,8},{10,11... | collective-permute-start | bytes 835592 | tf_op jit(solution)/shard_map/ppermute | solution.py:508
  43.7 5.9 %collective-permute-start.8 = (bf16[2,2,2,128,256]{4,3,2,1,0:T(8,128)(2,1)S(1)}, bf16[2,2,2,128,256]{4,3,2,1,0:T(8,128)(2,1)S(1)}, u32[]{:S(2)}, u32[]{:S(2)}) collective-permute-start(bf16[2,2,2,128,256]{4,3,2,1,0:T(8,128)(2,1)S(1)} %decode0.1._.refs_5_), channel_id=1, source_target_pairs={{12,4},{20,12},{28,20},{36,28},{44,36},{52,44},{60,52},{68,60},{76... | collective-permute-start | bytes 1572872 | tf_op jit(solution)/shard_map/ppermute | solution.py:491
  49.7 0.0 collective-permute-done.6.refs_4_
  49.7 1.1 %decode1.1._.refs_6_ = bf16[1,2,2,128,256]{4,3,2,1,0:T(8,128)(2,1)S(1)} custom-call(f32[2,2,128,256]{3,2,1,0:T(8,128)S(1)} %get-tuple-element.36._.refs_3_, s32[3]{0:T(128)S(1)} %pad_add_fusion.pos_ref.refs_0_, f32[8,512]{1,0:T(8,128)S(1)} %get-tuple-element.25.refs_5_.refs_1_.refs_3_, f32[8,512]{1,0:T(8,128)S(1)} %get-tuple-element.35.refs_6_.refs_2_, ...), custom_call_target="tpu_custom_call" | custom-call | bytes 2097152 | tf_op jit(solution)/shard_map/decode1/pallas_call | solution.py:426
  50.8 1.9 %collective-permute-start.9 = (bf16[1,2,2,128,256]{4,3,2,1,0:T(8,128)(2,1)S(1)}, bf16[1,2,2,128,256]{4,3,2,1,0:T(8,128)(2,1)S(1)}, u32[]{:S(2)}, u32[]{:S(2)}) collective-permute-start(bf16[1,2,2,128,256]{4,3,2,1,0:T(8,128)(2,1)S(1)} %decode1.1._.refs_6_), channel_id=1, source_target_pairs={{12,4},{20,12},{28,20},{36,28},{44,36},{52,44},{60,52},{68,60},{76... | collective-permute-start | bytes 786440 | tf_op jit(solution)/shard_map/ppermute | solution.py:491
  52.8 0.0 collective-permute-done.7.refs_4_
  52.8 1.1 %decode2.1._.fin_ref = bf16[1,2,2,128,256]{4,3,2,1,0:T(8,128)(2,1)S(1)} custom-call(bf16[1,2,2,128,256]{4,3,2,1,0:T(8,128)(2,1)S(1)} %decode1.1._.refs_6_, s32[3]{0:T(128)S(1)} %pad_add_fusion.pos_ref.refs_0_, f32[8,512]{1,0:T(8,128)S(1)} %get-tuple-element.25.refs_5_.refs_1_.refs_3_, f32[8,512]{1,0:T(8,128)S(1)} %get-tuple-element.38.refs_2_, ...), custom_call_target="tpu_custom_call" | custom-call | bytes 2097152 | tf_op jit(solution)/shard_map/decode2/pallas_call | solution.py:426
  53.9 2.6 %collective-permute-start.10 = (bf16[1,2,2,128,256]{4,3,2,1,0:T(8,128)(2,1)S(1)}, bf16[1,2,2,128,256]{4,3,2,1,0:T(8,128)(2,1)S(1)}, u32[]{:S(2)}, u32[]{:S(2)}) collective-permute-start(bf16[1,2,2,128,256]{4,3,2,1,0:T(8,128)(2,1)S(1)} %decode2.1._.fin_ref), channel_id=1, source_target_pairs={{12,4},{20,12},{28,20},{36,28},{44,36},{52,44},{60,52},{68,60},{76... | collective-permute-start | bytes 786440 | tf_op jit(solution)/shard_map/ppermute | solution.py:491
  56.5 3.6 %collective-permute-done.9.refs_8_ = bf16[1,2,2,128,256]{4,3,2,1,0:T(8,128)(2,1)S(1)} collective-permute-done((bf16[1,2,2,128,256]{4,3,2,1,0:T(8,128)(2,1)S(1)}, bf16[1,2,2,128,256]{4,3,2,1,0:T(8,128)(2,1)S(1)}, u32[]{:S(2)}, u32[]{:S(2)}) %collective-permute-start.9) | collective-permute-done | bytes 262176 | tf_op jit(solution)/shard_map/ppermute | solution.py:491
  60.1 0.0 collective-permute-done.8.refs_7_
  60.1 2.5 %finish.1.out_in_ref = bf16[2,1,3,256,512]{4,3,2,1,0:T(8,128)(2,1)} custom-call(bf16[1,2,2,128,256]{4,3,2,1,0:T(8,128)(2,1)S(1)} %decode2.1._.fin_ref, s32[3]{0:T(128)S(1)} %pad_add_fusion.pos_ref.refs_0_, f32[2,256,512]{2,1,0:T(8,128)S(1)} %get-tuple-element.40.refs_1_, bf16[2,256,512]{2,1,0:T(8,128)(2,1)S(1)} %collective-permute-done.1.refs_0_.refs_2_, ...), custom_call_target="tpu_custom_call" | custom-call | bytes 2097152 | tf_op jit(solution)/shard_map/finish/pallas_call | solution.py:426
  62.5 0.6 collective-permute-done.10.back_ref
  63.1 1.3 %place.1 = bf16[2,1,3,256,512]{4,3,2,1,0:T(8,128)(2,1)} custom-call(s32[3]{0:T(128)S(1)} %pad_add_fusion.pos_ref.refs_0_, bf16[2,1,3,256,512]{4,3,2,1,0:T(8,128)(2,1)} %finish.1.out_in_ref, bf16[1,2,2,128,256]{4,3,2,1,0:T(8,128)(2,1)S(1)} %decode2.1._.fin_ref, ...), custom_call_target="tpu_custom_call", output_to_operand_aliasing={{}: (1, {})} | custom-call | bytes 2097152 | tf_op jit(solution)/shard_map/place/pallas_call | solution.py:530
  (2 shorter events, 0.0 us)
Async XLA Ops:
  0.0 6.0 %copy-start = (bf16[2,1,4,512,256]{4,3,2,1,0:T(8,128)(2,1)S(1)}, bf16[2,1,4,512,256]{4,3,2,1,0:T(8,128)(2,1)}, u32[]{:S(2)}) copy-start(bf16[2,1,4,512,256]{4,3,2,1,0:T(8,128)(2,1)} %param.2) | copy-start | bytes 6291460
  0.1 0.8 %copy-start.1 = (s32[1,4]{1,0:T(1,128)S(1)}, s32[1,4]{1,0:T(1,128)}, u32[]{:S(2)}) copy-start(s32[1,4]{1,0:T(1,128)} %refs_1_.7) | copy-start | bytes 52
  2.8 15.9 %collective-permute-start = (bf16[2064,256]{1,0:T(8,128)(2,1)S(1)}, bf16[2064,256]{1,0:T(8,128)(2,1)S(1)}, u32[]{:S(2)}, u32[]{:S(2)}) collective-permute-start(bf16[2064,256]{1,0:T(8,128)(2,1)S(1)} %get-tuple-element.23), channel_id=1, source_target_pairs={{8,0},{16,8},{24,16},{32,24},{40,32},{48,40},{56,48},{64,56},{72,6... | collective-permute-start | bytes 3170312 | tf_op jit(solution)/shard_map/ppermute | solution.py:451
  9.6 15.3 %collective-permute-start.1 = (bf16[2,256,512]{2,1,0:T(8,128)(2,1)S(1)}, bf16[2,256,512]{2,1,0:T(8,128)(2,1)S(1)}, u32[]{:S(2)}, u32[]{:S(2)}) collective-permute-start(bf16[2,256,512]{2,1,0:T(8,128)(2,1)S(1)} %get-tuple-element.27._), channel_id=1, source_target_pairs={{0,1},{1,0},{2,3},{3,2},{4,5},{5,4},{6,7},{7,6},{8,9},{9,8},{10,11... | collective-permute-start | bytes 1572872 | tf_op jit(solution)/shard_map/ppermute | solution.py:464
  12.8 17.7 %collective-permute-start.3 = (bf16[2048,256]{1,0:T(8,128)(2,1)S(1)}, bf16[2048,256]{1,0:T(8,128)(2,1)S(1)}, u32[]{:S(2)}, u32[]{:S(2)}) collective-permute-start(bf16[2048,256]{1,0:T(8,128)(2,1)S(1)} %second.1), channel_id=1, source_target_pairs={{8,0},{16,8},{24,16},{32,24},{40,32},{48,40},{56,48},{64,56},{72,6... | collective-permute-start | bytes 3145736 | tf_op jit(solution)/shard_map/ppermute | solution.py:472
  16.0 2.7 %copy-start.2 = (s32[1,4]{1,0:T(1,128)S(1)}, s32[1,4]{1,0:T(1,128)}, u32[]{:S(2)}) copy-start(s32[1,4]{1,0:T(1,128)} %refs_1_.7) | copy-start | bytes 52
  16.0 8.9 %collective-permute-start.2 = (bf16[2,4,512,256]{3,2,1,0:T(8,128)(2,1)S(1)}, bf16[2,4,512,256]{3,2,1,0:T(8,128)(2,1)S(1)}, u32[]{:S(2)}, u32[]{:S(2)}) collective-permute-start(bf16[2,4,512,256]{3,2,1,0:T(8,128)(2,1)S(1)} %get-tuple-element.29), channel_id=1, source_target_pairs={{0,4},{4,0},{8,12},{12,8},{16,20},{20,16},{24,28},{28,24},{32,36},... | collective-permute-start | bytes 6291464 | tf_op jit(solution)/shard_map/ppermute | solution.py:473
  21.0 14.4 %collective-permute-start.4 = (bf16[544,256]{1,0:T(8,128)(2,1)S(1)}, bf16[544,256]{1,0:T(8,128)(2,1)S(1)}, u32[]{:S(2)}, u32[]{:S(2)}) collective-permute-start(bf16[544,256]{1,0:T(8,128)(2,1)S(1)} %get-tuple-element.33), channel_id=1, source_target_pairs={{0,1},{1,0},{2,3},{3,2},{4,5},{5,4},{6,7},{7,6},{8,9},{9,8},{10,11... | collective-permute-start | bytes 835592 | tf_op jit(solution)/shard_map/ppermute | solution.py:508
  27.3 8.4 %collective-permute-start.5 = (bf16[544,256]{1,0:T(8,128)(2,1)S(1)}, bf16[544,256]{1,0:T(8,128)(2,1)S(1)}, u32[]{:S(2)}, u32[]{:S(2)}) collective-permute-start(bf16[544,256]{1,0:T(8,128)(2,1)S(1)} %get-tuple-element.34), channel_id=1, source_target_pairs={{0,1},{1,0},{2,3},{3,2},{4,5},{5,4},{6,7},{7,6},{8,9},{9,8},{10,11... | collective-permute-start | bytes 835592 | tf_op jit(solution)/shard_map/ppermute | solution.py:508
  32.8 16.9 %collective-permute-start.6 = (bf16[544,256]{1,0:T(8,128)(2,1)S(1)}, bf16[544,256]{1,0:T(8,128)(2,1)S(1)}, u32[]{:S(2)}, u32[]{:S(2)}) collective-permute-start(bf16[544,256]{1,0:T(8,128)(2,1)S(1)} %get-tuple-element.37), channel_id=1, source_target_pairs={{0,1},{1,0},{2,3},{3,2},{4,5},{5,4},{6,7},{7,6},{8,9},{9,8},{10,11... | collective-permute-start | bytes 835592 | tf_op jit(solution)/shard_map/ppermute | solution.py:508
  39.7 13.1 %collective-permute-start.7 = (bf16[544,256]{1,0:T(8,128)(2,1)S(1)}, bf16[544,256]{1,0:T(8,128)(2,1)S(1)}, u32[]{:S(2)}, u32[]{:S(2)}) collective-permute-start(bf16[544,256]{1,0:T(8,128)(2,1)S(1)} %get-tuple-element.39), channel_id=1, source_target_pairs={{0,1},{1,0},{2,3},{3,2},{4,5},{5,4},{6,7},{7,6},{8,9},{9,8},{10,11... | collective-permute-start | bytes 835592 | tf_op jit(solution)/shard_map/ppermute | solution.py:508
  43.7 16.3 %collective-permute-start.8 = (bf16[2,2,2,128,256]{4,3,2,1,0:T(8,128)(2,1)S(1)}, bf16[2,2,2,128,256]{4,3,2,1,0:T(8,128)(2,1)S(1)}, u32[]{:S(2)}, u32[]{:S(2)}) collective-permute-start(bf16[2,2,2,128,256]{4,3,2,1,0:T(8,128)(2,1)S(1)} %decode0.1._.refs_5_), channel_id=1, source_target_pairs={{12,4},{20,12},{28,20},{36,28},{44,36},{52,44},{60,52},{68,60},{76... | collective-permute-start | bytes 1572872 | tf_op jit(solution)/shard_map/ppermute | solution.py:491
  50.8 9.2 %collective-permute-start.9 = (bf16[1,2,2,128,256]{4,3,2,1,0:T(8,128)(2,1)S(1)}, bf16[1,2,2,128,256]{4,3,2,1,0:T(8,128)(2,1)S(1)}, u32[]{:S(2)}, u32[]{:S(2)}) collective-permute-start(bf16[1,2,2,128,256]{4,3,2,1,0:T(8,128)(2,1)S(1)} %decode1.1._.refs_6_), channel_id=1, source_target_pairs={{12,4},{20,12},{28,20},{36,28},{44,36},{52,44},{60,52},{68,60},{76... | collective-permute-start | bytes 786440 | tf_op jit(solution)/shard_map/ppermute | solution.py:491
  53.9 9.2 %collective-permute-start.10 = (bf16[1,2,2,128,256]{4,3,2,1,0:T(8,128)(2,1)S(1)}, bf16[1,2,2,128,256]{4,3,2,1,0:T(8,128)(2,1)S(1)}, u32[]{:S(2)}, u32[]{:S(2)}) collective-permute-start(bf16[1,2,2,128,256]{4,3,2,1,0:T(8,128)(2,1)S(1)} %decode2.1._.fin_ref), channel_id=1, source_target_pairs={{12,4},{20,12},{28,20},{36,28},{44,36},{52,44},{60,52},{68,60},{76... | collective-permute-start | bytes 786440 | tf_op jit(solution)/shard_map/ppermute | solution.py:491
